TPU v7x, 32 devices: a whole 2x2x4 slice. The times are simulated.
32 devices in a mesh: dp: 8 (over z, y), mp: 4 (over x, core).
Axes of the slice: x: 2, y: 2, z: 4, core: 2. Of those that a mesh axis runs over, the one named last changes fastest.
Arguments:
- public_input_activations: bfloat16 [8, 112, 8192], P('dp', None, 'mp')
- public_output_cotangents: bfloat16 [8, 112, 8192], P('dp', None, 'mp')
- public_token_lengths: int32 [8], P('dp'), may hold values from 28 to 112, as said below
- private_input_activations: bfloat16 [32, 112, 8192], P('dp', None, 'mp')
- private_output_cotangents: bfloat16 [32, 112, 8192], P('dp', None, 'mp')
- private_token_lengths: int32 [32], P('dp'), may hold values from 28 to 112, as said below
- adapter_down_matrix: bfloat16 [8192, 16], P('mp'), may hold values from -0.0625 to 0.0625
- adapter_up_matrix: bfloat16 [16, 8192], P(None, 'mp'), may hold values from -0.0625 to 0.0625
- embedding_coefficient_noise: float32 [8], replicated, may hold values from -6 to 6
- residual_down_noise: float32 [4, 32768], P('mp', 'dp'), may hold values from -6 to 6
- residual_up_noise: float32 [4, 32768], P('mp', 'dp'), may hold values from -6 to 6
Outputs:
- update_down: float32 [4, 32768], P('mp', 'dp')
- update_up: float32 [4, 32768], P('mp', 'dp')
Inputs may be any that keep to these rules, and one draw needn't show every extreme that they name: `public_token_lengths`: each example has between 28 and 112 live tokens at the start of its slots. `private_token_lengths`: each example has between 28 and 112 live tokens at the start of its slots.
All inputs are finite; a program needn't handle non-finite values.
Results may differ from a plain program's by a relative error of at most 0.0028.
Values may be sent and summed in bfloat16 or wider, within the bound.
No kernel may reach another device: no remote copies, remote signals or barrier semaphores. Data moves between devices by JAX's collectives and lax.ppermute only.
A program may use at most 64 MiB of HBM per device.

v0:
```python
import math

import jax
import jax.numpy as jnp
from jax import lax
from jax.sharding import PartitionSpec as P

CLIP_COEF = 0.5
CLIP_RESIDUAL = 0.7
SIGMA_COEF = 1.0
SIGMA_RESIDUAL = 0.04
PRECISE = lax.Precision.HIGHEST


def partial_gram_terms(
    input_activations, output_cotangents, adapter_down_matrix, adapter_up_matrix
):
    projected_gradients = jnp.einsum(
        "umo,ov->umv", input_activations, adapter_down_matrix, preferred_element_type=jnp.float32
    )
    reconstructed_gradients = jnp.einsum(
        "fpb,ab->fpa", output_cotangents, adapter_up_matrix, preferred_element_type=jnp.float32
    )
    return (projected_gradients, reconstructed_gradients)


def shard_grads(
    input_activations,
    output_cotangents,
    token_lengths,
    projected_gradients,
    reconstructed_gradients,
):
    example_total_count = input_activations.shape[0]
    token_steps = input_activations.shape[1]
    positions = lax.broadcasted_iota(jnp.int32, (example_total_count, token_steps), 1)
    live_mask = (positions < token_lengths[:, None]).astype(jnp.float32)[:, :, None]
    projected_live = (projected_gradients * live_mask).astype(jnp.bfloat16)
    returned_live = (reconstructed_gradients * live_mask).astype(jnp.bfloat16)
    grad_down = jnp.einsum(
        "etd,etr->edr", input_activations, returned_live, preferred_element_type=jnp.float32
    ).astype(jnp.bfloat16)
    grad_up = jnp.einsum(
        "etr,eto->ero", projected_live, output_cotangents, preferred_element_type=jnp.float32
    ).astype(jnp.bfloat16)
    return (grad_down.reshape(example_total_count, -1), grad_up.reshape(example_total_count, -1))


def lower_solve(factor, right_side, backward):
    return lax.linalg.triangular_solve(
        factor, right_side, left_side=True, lower=True, transpose_a=backward
    )


def limits(gram_matrix):
    factor = jnp.linalg.cholesky(gram_matrix)
    norm_scale = jnp.mean(jnp.sqrt(jnp.diagonal(gram_matrix)))
    return (factor, CLIP_COEF * norm_scale, CLIP_RESIDUAL * norm_scale)


def keep_factors(coeffs, residual_squares, coefficient_limit, residual_limit):
    coefficient_norm = jnp.sqrt(jnp.sum(coeffs * coeffs, axis=0))
    keep_coefficient = coefficient_limit / jnp.maximum(coefficient_norm, coefficient_limit)
    keep_residual = residual_limit / jnp.maximum(jnp.sqrt(residual_squares), residual_limit)
    return (keep_coefficient, keep_residual)


def body(
    public_input_activations,
    public_output_cotangents,
    public_token_lengths,
    private_input_activations,
    private_output_cotangents,
    private_token_lengths,
    adapter_down_matrix,
    adapter_up_matrix,
    embedding_coefficient_noise,
    residual_down_noise,
    residual_up_noise,
):
    public_projected, public_returned = partial_gram_terms(
        public_input_activations, public_output_cotangents, adapter_down_matrix, adapter_up_matrix
    )
    private_projected, private_returned = partial_gram_terms(
        private_input_activations, private_output_cotangents, adapter_down_matrix, adapter_up_matrix
    )
    public_projected, public_returned, private_projected, private_returned = lax.psum(
        (public_projected, public_returned, private_projected, private_returned), "mp"
    )
    public_down, public_up = shard_grads(
        public_input_activations,
        public_output_cotangents,
        public_token_lengths,
        public_projected,
        public_returned,
    )
    private_down, private_up = shard_grads(
        private_input_activations,
        private_output_cotangents,
        private_token_lengths,
        private_projected,
        private_returned,
    )
    public_down, public_up, private_down, private_up = (
        lax.all_to_all(public_down, "dp", split_axis=1, concat_axis=0, tiled=True),
        lax.all_to_all(public_up, "dp", split_axis=1, concat_axis=0, tiled=True),
        lax.all_to_all(private_down, "dp", split_axis=1, concat_axis=0, tiled=True),
        lax.all_to_all(private_up, "dp", split_axis=1, concat_axis=0, tiled=True),
    )
    public_group = jnp.concatenate([public_down, public_up], axis=1)
    private_group = jnp.concatenate([private_down, private_up], axis=1)
    public_wide = public_group.astype(jnp.float32)
    private_wide = private_group.astype(jnp.float32)
    gram_partial = jnp.einsum(
        "pk,qk->pq", public_group, public_group, preferred_element_type=jnp.float32
    )
    cross_partial = jnp.einsum(
        "pk,qk->pq", public_group, private_group, preferred_element_type=jnp.float32
    )
    square_partial = jnp.sum(private_wide * private_wide, axis=1)
    gram_matrix, cross_terms, square_totals = lax.psum(
        (gram_partial, cross_partial, square_partial), ("dp", "mp")
    )
    factor, coefficient_limit, residual_limit = limits(gram_matrix)
    coeffs = lower_solve(factor, cross_terms, False)
    residual_squares = square_totals - jnp.sum(coeffs * coeffs, axis=0)
    keep_coefficient, keep_residual = keep_factors(
        coeffs, residual_squares, coefficient_limit, residual_limit
    )
    correction = jnp.dot(coeffs, keep_coefficient - keep_residual, precision=PRECISE)
    target = correction + SIGMA_COEF * coefficient_limit * embedding_coefficient_noise
    anchor = lower_solve(factor, target[:, None], True)[:, 0]
    update = jnp.dot(anchor, public_wide, precision=PRECISE) + jnp.dot(
        keep_residual, private_wide, precision=PRECISE
    )
    noise_shard = jnp.concatenate([residual_down_noise[0], residual_up_noise[0]], axis=0)
    private_total = private_input_activations.shape[0] * lax.axis_size("dp")
    update_gain = 1.0 / math.sqrt(private_total * private_input_activations.shape[1])
    result = (update + SIGMA_RESIDUAL * residual_limit * noise_shard) * update_gain
    split_point = public_down.shape[1]
    return (result[None, :split_point], result[None, split_point:])


def solution(mesh):
    placed = (
        P("dp", None, "mp"),
        P("dp", None, "mp"),
        P("dp"),
        P("dp", None, "mp"),
        P("dp", None, "mp"),
        P("dp"),
        P("mp", None),
        P(None, "mp"),
        P(),
        P("mp", "dp"),
        P("mp", "dp"),
    )
    return jax.shard_map(
        body, mesh=mesh, in_specs=placed, out_specs=(P("mp", "dp"), P("mp", "dp")), check_vma=False
    )
```

profile of v0, /device:TPU:0, one launch (start us, length us, event | category | flops | bytes accessed | tf_op | source)
XLA Modules:
  0.0 157.3 jit_solution(1515079057697181243)
XLA Ops:
  7.3 1.4 copy-done
  8.7 2.2 %fusion.8 = f32[4,112,16]{1,2,0:T(8,128)} fusion(bf16[4,112,2048]{2,1,0:T(8,128)(2,1)S(1)} %copy-done, bf16[2048,16]{0,1:T(8,128)(2,1)} %param.17), kind=kOutput, calls=%fused_computation.21 | convolution fusion | flops 29360128 | bytes 1929216 | tf_op jit(solution)/shard_map/umo,ov->umv/dot_general | solution.py:18
  10.9 1.9 %convolution_bitcast_fusion = f32[1,112,16]{1,2,0:T(8,128)} fusion(bf16[2048,16]{0,1:T(8,128)(2,1)S(1)} %copy-done.4, bf16[1,112,2048]{2,1,0:T(8,128)(2,1)} %param.11), kind=kOutput, calls=%fused_computation.7 | convolution fusion | flops 7340032 | bytes 531456 | tf_op jit(solution)/shard_map/umo,ov->umv/dot_general | solution.py:18
  12.8 1.2 fusion.10
  14.0 0.8 convolution_bitcast_fusion.1
  15.6 32.0 %all-reduce.4.cloned.1.call-done = (f32[4,112,16]{1,2,0:T(8,128)}, f32[4,112,16]{1,2,0:T(8,128)}, f32[1,112,16]{1,2,0:T(8,128)}, f32[1,112,16]{1,2,0:T(8,128)}) async-done(((f32[4,112,16]{1,2,0:T(8,128)}, f32[4,112,16]{1,2,0:T(8,128)}, f32[1,112,16]{1,2,0:T(8,128)}, f32[1,112,16]{1,2,0:T(8,128)}), (f32[4,112,16]{1,2,0:T(8,128)}, f32[4,112,16]{1,2,0:T(8,128)}, f32[1,112,16]{1,2,0:T(8,128)}, ...) | async-done | bytes 71696 | tf_op jit(solution)/shard_map/psum | solution.py:87
  47.7 0.9 convolution_convert_fusion.2
  48.5 0.1 all_to_all.67
  48.6 0.5 broadcast.100
  49.2 1.0 reduce.6
  50.2 0.6 reshape.120
  50.8 5.6 %all-to-all-start.1 = ((bf16[8,2,2048]{2,1,0:T(2,128)(2,1)}), bf16[8,2,2048]{2,1,0:T(2,128)(2,1)S(1)}, u32[]{:S(2)}, u32[]{:S(2)}) async-start(bf16[8,2,2048]{2,1,0:T(2,128)(2,1)} %reshape.120), calls=%async_computation.1 | async-start | bytes 131072 | tf_op jit(solution)/shard_map/all_to_all | solution.py:106
  56.5 1.1 fusion
  57.6 0.2 fusion.1
  57.8 0.3 copy.32
  58.0 0.4 all_to_all.66
  58.4 1.0 reduce.7
  59.4 0.7 reshape.122
  60.1 3.3 %all-to-all-done.1 = bf16[8,2,2048]{2,1,0:T(2,128)(2,1)S(1)} async-done(((bf16[8,2,2048]{2,1,0:T(2,128)(2,1)}), bf16[8,2,2048]{2,1,0:T(2,128)(2,1)S(1)}, u32[]{:S(2)}, u32[]{:S(2)}) %all-to-all-start.1) | async-done | bytes 65568 | tf_op jit(solution)/shard_map/all_to_all | solution.py:106
  63.4 3.3 %all-to-all-start = ((bf16[8,2,2048]{2,1,0:T(2,128)(2,1)}), bf16[8,2,2048]{2,1,0:T(2,128)(2,1)S(1)}, u32[]{:S(2)}, u32[]{:S(2)}) async-start(bf16[8,2,2048]{2,1,0:T(2,128)(2,1)} %reshape.122), calls=%async_computation | async-start | bytes 131072 | tf_op jit(solution)/shard_map/all_to_all | solution.py:105
  66.7 1.8 %convolution_convert_fusion = bf16[4,16,2048]{2,1,0:T(8,128)(2,1)S(1)} fusion(bf16[4,112,2048]{2,1,0:T(8,128)(2,1)} %param.15, f32[4,112,16]{1,2,0:T(8,128)S(1)} %copy-done.6, f32[4,112]{1,0:T(4,128)S(1)} %fusion.30), kind=kOutput, calls=%fused_computation.1 | convolution fusion | flops 29505536 | bytes 2127616 | tf_op jit(solution)/shard_map/etr,eto->ero/dot_general | solution.py:43
  68.6 1.8 %copy.38 = bf16[4,2048,16]{2,1,0:T(8,128)(2,1)} copy(bf16[4,2048,16]{1,2,0:T(8,128)(2,1)S(1)} %fusion) | data formatting | bytes 524288 | tf_op jit(solution)/shard_map/convert_element_type | solution.py:42
  70.3 4.7 %all_to_all.58 = bf16[4,8,4096]{2,1,0:T(8,128)(2,1)S(1)} reshape(bf16[4,2048,16]{2,1,0:T(8,128)(2,1)} %copy.38) | data formatting | bytes 524288 | tf_op jit(solution)/shard_map/all_to_all | solution.py:107
  75.0 0.9 copy.39
  75.9 0.1 all_to_all.62
  76.0 0.9 copy.40
  77.0 5.9 %all-to-all-start.2 = ((bf16[4,8,4096]{2,0,1:T(4,128)(2,1)}), bf16[4,8,4096]{2,0,1:T(4,128)(2,1)S(1)}, u32[]{:S(2)}, u32[]{:S(2)}) async-start(bf16[4,8,4096]{2,0,1:T(4,128)(2,1)} %copy.39), calls=%async_computation.2 | async-start | bytes 524288 | tf_op jit(solution)/shard_map/all_to_all | solution.py:107
  83.0 0.2 copy_bitcast_fusion
  83.2 8.0 %all-to-all-done.2 = bf16[4,8,4096]{2,0,1:T(4,128)(2,1)S(1)} async-done(((bf16[4,8,4096]{2,0,1:T(4,128)(2,1)}), bf16[4,8,4096]{2,0,1:T(4,128)(2,1)S(1)}, u32[]{:S(2)}, u32[]{:S(2)}) %all-to-all-start.2) | async-done | bytes 262176 | tf_op jit(solution)/shard_map/all_to_all | solution.py:107
  91.2 3.4 %all-to-all-start.3 = ((bf16[4,8,4096]{2,0,1:T(4,128)(2,1)}), bf16[4,8,4096]{2,0,1:T(4,128)(2,1)S(1)}, u32[]{:S(2)}, u32[]{:S(2)}) async-start(bf16[4,8,4096]{2,0,1:T(4,128)(2,1)} %copy.40), calls=%async_computation.3 | async-start | bytes 524288 | tf_op jit(solution)/shard_map/all_to_all | solution.py:108
  94.6 0.2 fusion.14
  94.8 0.1 all_to_all.61
  94.9 7.8 %all-to-all-done.3 = bf16[4,8,4096]{2,0,1:T(4,128)(2,1)S(1)} async-done(((bf16[4,8,4096]{2,0,1:T(4,128)(2,1)}), bf16[4,8,4096]{2,0,1:T(4,128)(2,1)S(1)}, u32[]{:S(2)}, u32[]{:S(2)}) %all-to-all-start.3) | async-done | bytes 262176 | tf_op jit(solution)/shard_map/all_to_all | solution.py:108
  102.8 0.2 fusion.13
  103.1 0.2 multiply_reduce_fusion
  103.3 39.4 %all-reduce = (f32[8,32]{1,0:T(8,128)S(1)}, f32[8,8]{0,1:T(8,128)S(1)}, f32[32]{0:T(128)S(1)}) all-reduce(f32[8,32]{1,0:T(8,128)S(1)} %fusion.13, f32[8,8]{0,1:T(8,128)S(1)} %fusion.14, f32[32]{0:T(128)S(1)} %multiply_reduce_fusion), channel_id=1, replica_groups=mesh['dp'=8,'mp'=4] {'dp','mp'}, use_global_device_ids=true, to_apply=%region_7.0 | all-reduce | flops 352 | bytes 2816 | tf_op jit(solution)/shard_map/psum | solution.py:121
  142.8 0.7 cholesky.16
  143.6 0.6 compare_reduce_fusion
  144.2 0.6 fusion.19
  144.9 0.6 custom-call.8
  145.5 0.6 gather_fusion
  146.1 0.6 sqrt_reduce_fusion
  148.0 0.2 multiply_reduce_fusion.1
  148.2 0.3 fusion.31
  148.6 0.1 fusion.3
  148.7 0.1 convolution_bitcast_fusion.2
  148.9 0.3 fusion.12
  149.9 0.6 fusion.39
  (38 shorter events, 0.6 us)
Async XLA Ops:
  7.2 1.5 copy-start
  7.2 3.7 %copy-start.4 = (bf16[2048,16]{0,1:T(8,128)(2,1)S(1)}, bf16[2048,16]{0,1:T(8,128)(2,1)}, u32[]{:S(2)}) copy-start(bf16[2048,16]{0,1:T(8,128)(2,1)} %param.17) | copy-start | bytes 196612
  7.2 5.6 %copy-start.5 = (bf16[16,2048]{1,0:T(8,128)(2,1)S(1)}, bf16[16,2048]{1,0:T(8,128)(2,1)}, u32[]{:S(2)}) copy-start(bf16[16,2048]{1,0:T(8,128)(2,1)} %param.18) | copy-start | bytes 196612
  7.2 6.8 %copy-start.2 = (bf16[1,112,2048]{2,1,0:T(8,128)(2,1)S(1)}, bf16[1,112,2048]{2,1,0:T(8,128)(2,1)}, u32[]{:S(2)}) copy-start(bf16[1,112,2048]{2,1,0:T(8,128)(2,1)} %param.12) | copy-start | bytes 1376260
  7.2 40.4 %all-reduce.4.cloned.1.call-start = ((), (), s32[]{:S(2)}) async-start(), calls=%async_computation.4 | async-start | bytes 163840 | tf_op jit(solution)/shard_map/psum | solution.py:87
  8.7 4.1 %copy-start.1 = (bf16[4,112,2048]{2,1,0:T(8,128)(2,1)S(1)}, bf16[4,112,2048]{2,1,0:T(8,128)(2,1)}, u32[]{:S(2)}) copy-start(bf16[4,112,2048]{2,1,0:T(8,128)(2,1)} %param.15) | copy-start | bytes 5505028
  10.9 4.0 %copy-start.10 = (s32[4]{0:T(128)S(1)}, s32[4]{0:T(128)}, u32[]{:S(2)}) copy-start(s32[4]{0:T(128)} %param.16) | copy-start | bytes 52
  14.8 42.7 %copy-start.3 = (bf16[1,112,2048]{2,1,0:T(8,128)(2,1)S(1)}, bf16[1,112,2048]{2,1,0:T(8,128)(2,1)}, u32[]{:S(2)}) copy-start(bf16[1,112,2048]{2,1,0:T(8,128)(2,1)} %param.11) | copy-start | bytes 1376260
  47.6 9.9 %copy-start.9 = (f32[1,112,16]{1,2,0:T(8,128)S(1)}, f32[1,112,16]{1,2,0:T(8,128)}, u32[]{:S(2)}) copy-start(f32[1,112,16]{1,2,0:T(8,128)} %get-tuple-element.8) | copy-start | bytes 21508
  50.8 12.5 %all-to-all-start.1 = ((bf16[8,2,2048]{2,1,0:T(2,128)(2,1)}), bf16[8,2,2048]{2,1,0:T(2,128)(2,1)S(1)}, u32[]{:S(2)}, u32[]{:S(2)}) async-start(bf16[8,2,2048]{2,1,0:T(2,128)(2,1)} %reshape.120), calls=%async_computation.1 | async-start | bytes 131072 | tf_op jit(solution)/shard_map/all_to_all | solution.py:106
  56.4 10.3 %copy-start.6 = (f32[4,112,16]{1,2,0:T(8,128)S(1)}, f32[4,112,16]{1,2,0:T(8,128)}, u32[]{:S(2)}) copy-start(f32[4,112,16]{1,2,0:T(8,128)} %get-tuple-element.6) | copy-start | bytes 86020
  63.4 13.6 %all-to-all-start = ((bf16[8,2,2048]{2,1,0:T(2,128)(2,1)}), bf16[8,2,2048]{2,1,0:T(2,128)(2,1)S(1)}, u32[]{:S(2)}, u32[]{:S(2)}) async-start(bf16[8,2,2048]{2,1,0:T(2,128)(2,1)} %reshape.122), calls=%async_computation | async-start | bytes 131072 | tf_op jit(solution)/shard_map/all_to_all | solution.py:105
  77.0 14.2 %all-to-all-start.2 = ((bf16[4,8,4096]{2,0,1:T(4,128)(2,1)}), bf16[4,8,4096]{2,0,1:T(4,128)(2,1)S(1)}, u32[]{:S(2)}, u32[]{:S(2)}) async-start(bf16[4,8,4096]{2,0,1:T(4,128)(2,1)} %copy.39), calls=%async_computation.2 | async-start | bytes 524288 | tf_op jit(solution)/shard_map/all_to_all | solution.py:107
  91.2 11.6 %all-to-all-start.3 = ((bf16[4,8,4096]{2,0,1:T(4,128)(2,1)}), bf16[4,8,4096]{2,0,1:T(4,128)(2,1)S(1)}, u32[]{:S(2)}, u32[]{:S(2)}) async-start(bf16[4,8,4096]{2,0,1:T(4,128)(2,1)} %copy.40), calls=%async_computation.3 | async-start | bytes 524288 | tf_op jit(solution)/shard_map/all_to_all | solution.py:108
  94.9 53.7 %copy-start.11 = (f32[8]{0:T(128)S(1)}, f32[8]{0:T(128)}, u32[]{:S(2)}) copy-start(f32[8]{0:T(128)} %param.19) | copy-start | bytes 100
  94.9 54.9 %copy-start.7 = (f32[1,4096]{1,0:T(1,128)S(1)}, f32[1,4096]{1,0:T(1,128)}, u32[]{:S(2)}) copy-start(f32[1,4096]{1,0:T(1,128)} %param.21) | copy-start | bytes 49156
  94.9 54.9 %copy-start.8 = (f32[1,4096]{1,0:T(1,128)S(1)}, f32[1,4096]{1,0:T(1,128)}, u32[]{:S(2)}) copy-start(f32[1,4096]{1,0:T(1,128)} %param.20) | copy-start | bytes 49156
Sparse Core Ops, SparseCore 0:
  15.0 32.6 all-reduce.3
where the time goes:
time: 158 us; the launch traced here: 157 us
  waiting for transfers between devices  51.1 us (32%)
  blocking collectives  39.4 us (25%)
  starting transfers between devices  18.4 us (12%)
  between operations  16.9 us (11%)
  local copies, waits for them, and re-layouts  14.2 us (9%)
  matrix products  11.7 us (7%)
  other arithmetic  5.66 us (4%)
    psum x1, blocking collectives, body(): lax.psum((gram_partial, cross_partial, square_partial), ('dp', 'mp'))  39.4 us
    psum x1, waiting for transfers between devices, body(): lax.psum((public_projected, public_returned, private_projected, private_r...  32 us
    all_to_all x1, waiting for transfers between devices, body(): lax.all_to_all(private_down, 'dp', split_axis=1, concat_axis=0, tiled=True)  8.01 us
    all_to_all x1, waiting for transfers between devices, body(): lax.all_to_all(private_up, 'dp', split_axis=1, concat_axis=0, tiled=True)  7.83 us
    all_to_all x1, starting transfers between devices, body(): lax.all_to_all(private_down, 'dp', split_axis=1, concat_axis=0, tiled=True)  5.94 us
    all_to_all x3, local copies, waits for them, and re-layouts, body(): lax.all_to_all(private_down, 'dp', split_axis=1, concat_axis=0, tiled=True)  5.66 us
    all_to_all x1, starting transfers between devices, body(): lax.all_to_all(public_up, 'dp', split_axis=1, concat_axis=0, tiled=True)  5.62 us
    dot_general x2, matrix products, partial_gram_terms(): jnp.einsum('umo,ov->umv', input_activations, adapter_down_matrix, preferr...  4.07 us
  transfers between devices with their start and end apart: 5, of which 4 were waited for; matrix products, arithmetic and copies ran while one was open for 6% of the time, Pallas kernels for 0%

commit v1 on v0

--- a/solution.py
+++ b/solution.py
@@ -1,8 +1,11 @@
+import functools
 import math
 
 import jax
 import jax.numpy as jnp
 from jax import lax
+from jax.experimental import pallas as pl
+from jax.experimental.pallas import tpu as pltpu
 from jax.sharding import PartitionSpec as P
 
 CLIP_COEF = 0.5
@@ -10,6 +13,265 @@
 SIGMA_COEF = 1.0
 SIGMA_RESIDUAL = 0.04
 PRECISE = lax.Precision.HIGHEST
+LANES = 128
+VMEM = pl.BlockSpec(memory_space=pltpu.VMEM)
+SMEM = pl.BlockSpec(memory_space=pltpu.SMEM)
+BOTH_LAST = (((1,), (1,)), ((), ()))
+FIRST_LAST = (((1,), (0,)), ((), ()))
+PARAMS = pltpu.CompilerParams(vmem_limit_bytes=40 * 1024 * 1024)
+
+
+def dot(a, b, dims, precision=None):
+    return lax.dot_general(a, b, dims, precision=precision, preferred_element_type=jnp.float32)
+
+
+def iota(shape, axis):
+    return lax.broadcasted_iota(jnp.int32, shape, axis)
+
+
+def project_kernel(pub_in, pub_out, priv_in, priv_out, down_t, up, out):
+    rank = up.shape[0]
+    tokens = pub_in.shape[1]
+    out[...] = jnp.zeros_like(out)
+    slot = 0
+    for inputs, cotangents in ((pub_in, pub_out), (priv_in, priv_out)):
+        for e in range(inputs.shape[0]):
+            at = slice(slot * LANES, slot * LANES + tokens)
+            out[0:rank, at] = dot(down_t[...], inputs[e], BOTH_LAST)
+            out[rank : 2 * rank, at] = dot(up[...], cotangents[e], BOTH_LAST)
+            slot += 1
+
+
+def gradient_kernel(dp, pub_len, priv_len, own, other, pub_in, pub_out, priv_in, priv_out, *rest):
+    blocks, down_rows, up_rows = rest[:dp], rest[dp], rest[dp + 1]
+    me = lax.axis_index("dp")
+    rank = own.shape[0] // 2
+    tokens, width = pub_in.shape[1:]
+    lanes = width // dp
+    per = rank // dp
+    slot = 0
+    for inputs, cotangents, lengths in (
+        (pub_in, pub_out, pub_len),
+        (priv_in, priv_out, priv_len),
+    ):
+        for e in range(inputs.shape[0]):
+            at = slice(slot * LANES, slot * LANES + tokens)
+            both = own[:, at] + other[:, at]
+            live = iota(both.shape, 1) < lengths[e]
+            both = jnp.where(live, both, 0.0).astype(jnp.bfloat16)
+            for c in range(dp):
+                features = slice(c * lanes, (c + 1) * lanes)
+                at = slice(c * rank, (c + 1) * rank)
+                down_part = dot(both[rank:], inputs[e, :, features], FIRST_LAST)
+                up_part = dot(both[:rank], cotangents[e, :, features], FIRST_LAST)
+                down_rows[at, :] = down_part.astype(jnp.bfloat16)
+                for h in range(lanes // LANES):
+                    up_rows[h, at, :] = up_part[:, h * LANES : (h + 1) * LANES]
+            for k in range(dp):
+                to = me ^ k
+                row = slot * 2 * rank
+                blocks[k][row : row + rank, :] = down_rows[
+                    pl.ds(pl.multiple_of(to * rank, rank), rank), :
+                ]
+                for h in range(lanes // LANES):
+                    pieces = [
+                        up_rows[h, pl.ds(to * per + r, dp, stride=rank), :] for r in range(per)
+                    ]
+                    blocks[k][row + rank : row + 2 * rank, h * LANES : (h + 1) * LANES] = (
+                        jnp.concatenate(pieces, axis=0).astype(jnp.bfloat16)
+                    )
+            slot += 1
+
+
+def gram_kernel(dp, n_pub, n_priv, *refs):
+    blocks, group, out = refs[:dp], refs[dp], refs[dp + 1]
+    me = lax.axis_index("dp")
+    rows = blocks[0].shape[0] // (n_pub + n_priv)
+    pub_rows, priv_rows = n_pub * rows, n_priv * rows
+    for k in range(dp):
+        source = me ^ k
+        group[pl.ds(pl.multiple_of(source * pub_rows, pub_rows), pub_rows), :] = blocks[k][:pub_rows]
+        group[
+            pl.ds(pl.multiple_of(dp * pub_rows + source * priv_rows, priv_rows), priv_rows), :
+        ] = blocks[k][pub_rows:]
+    publics = dp * n_pub
+    span = publics * rows
+    lanes = group.shape[1]
+    public = group[:span, :]
+    total = jnp.zeros((publics, LANES), jnp.float32)
+    same = iota((span, span), 0) % rows == iota((span, span), 1) % rows
+    squares = []
+    for c in range(group.shape[0] // span):
+        part = group[c * span : (c + 1) * span, :]
+        products = jnp.where(same, dot(public, part, BOTH_LAST), 0.0)
+        products = jnp.sum(products.reshape(publics, rows, span), axis=1)
+        pick = (iota((span, LANES), 0) // rows + c * publics == iota((span, LANES), 1)).astype(
+            jnp.float32
+        )
+        total += dot(products, pick, FIRST_LAST, PRECISE)
+        if c > 0:
+            wide = part.astype(jnp.float32)
+            squares.append(jnp.sum((wide * wide).reshape(publics, rows, lanes), axis=1))
+    examples = group.shape[0] // rows
+    before = LANES // 2 + publics
+    after = LANES // 2 - examples
+    stacked = jnp.concatenate(
+        [jnp.zeros((before, lanes), jnp.float32)]
+        + squares
+        + ([jnp.zeros((after, lanes), jnp.float32)] if after else []),
+        axis=0,
+    )
+    total_squares = dot(jnp.ones((publics, lanes), jnp.float32), stacked, BOTH_LAST, PRECISE)
+    total += jnp.where(iota(total.shape, 0) == 0, total_squares, 0.0)
+    for d in range(out.shape[0]):
+        out[d] = total
+
+
+def update_kernel(gain, shares, group, noise, down_noise, up_noise, down, up):
+    total = shares[0]
+    for d in range(1, shares.shape[0]):
+        total = total + shares[d]
+    publics = total.shape[0]
+    shape = total.shape
+    row, lane = iota(shape, 0), iota(shape, 1)
+    half = LANES // 2
+    squares = pltpu.roll(total, half, 1)[0:1]
+    gram_diagonal = jnp.sum(jnp.where(row == lane, total, 0.0), axis=1, keepdims=True)
+    norm_scale = jnp.mean(jnp.sqrt(gram_diagonal), axis=0, keepdims=True)
+    coefficient_limit = CLIP_COEF * norm_scale
+    residual_limit = CLIP_RESIDUAL * norm_scale
+    work = jnp.where(lane < half, total, jnp.where(lane == row + half, 1.0, 0.0))
+    for j in range(publics):
+        inverse = lax.rsqrt(work[j : j + 1, j : j + 1])
+        pivot = work[j : j + 1, :] * inverse
+        column = work[:, j : j + 1] * inverse
+        work = jnp.where(row > j, work - column * pivot, jnp.where(row == j, pivot, work))
+    examples = group.shape[0] * publics // (publics * (2 * up.shape[1] // group.shape[1]))
+    private = jnp.logical_and(lane >= publics, lane < examples)
+    coeffs = jnp.where(private, work, 0.0)
+    coefficient_squares = jnp.sum(coeffs * coeffs, axis=0, keepdims=True)
+    residual_squares = jnp.maximum(squares - coefficient_squares, 0.0)
+    keep_coefficient = coefficient_limit / jnp.maximum(
+        jnp.sqrt(coefficient_squares), coefficient_limit
+    )
+    keep_residual = residual_limit / jnp.maximum(jnp.sqrt(residual_squares), residual_limit)
+    correction = jnp.sum(
+        coeffs * (keep_coefficient - keep_residual), axis=1, keepdims=True
+    )
+    noise_column = jnp.zeros((publics, 1), jnp.float32)
+    for j in range(publics):
+        noise_column = jnp.where(iota((publics, 1), 0) == j, noise[j], noise_column)
+    target = correction + SIGMA_COEF * coefficient_limit * noise_column
+    inverse_factor = jnp.where(lane >= half, work, 0.0)
+    anchor = pltpu.roll(jnp.sum(inverse_factor * target, axis=0, keepdims=True), half, 1)
+    weights = jnp.where(lane[0:1] < publics, anchor, keep_residual)
+
+    lanes = group.shape[1]
+    rows = group.shape[0] // examples
+    rank = rows // 2
+    acc = jnp.zeros((rows, lanes), jnp.float32)
+    for i in range(examples):
+        acc = acc + weights[:, i : i + 1] * group[i * rows : (i + 1) * rows, :].astype(jnp.float32)
+    scale = SIGMA_RESIDUAL * residual_limit
+    per = LANES // rank
+    flat = lanes * rank // LANES
+    wide = jnp.concatenate([acc[:rank]] * per, axis=0)
+    wide = jnp.where(iota((LANES, lanes), 0) // rank == iota((LANES, lanes), 1) % per, wide, 0.0)
+    pick = (iota((flat, lanes), 0) == iota((flat, lanes), 1) // per).astype(jnp.float32)
+    turned = dot(pick, wide, BOTH_LAST, PRECISE)
+    for a in range(flat):
+        at = slice(a * LANES, (a + 1) * LANES)
+        down[0:1, at] = (turned[a : a + 1] + scale * down_noise[0:1, at]) * gain
+    for a in range(rank):
+        at = slice(a * lanes, (a + 1) * lanes)
+        up[0:1, at] = (acc[rank + a : rank + a + 1] + scale * up_noise[0:1, at]) * gain
+
+
+def exchange(x, axis, step):
+    return lax.ppermute(x, axis, [(s, s ^ step) for s in range(lax.axis_size(axis))])
+
+
+def small_group(
+    pub_in, pub_out, pub_len, priv_in, priv_out, priv_len, down, up, noise, down_noise, up_noise
+):
+    dp, mp = lax.axis_size("dp"), lax.axis_size("mp")
+    n_pub, tokens, width = pub_in.shape
+    n_priv = priv_in.shape[0]
+    examples = n_pub + n_priv
+    rank = up.shape[0]
+    lanes = width // dp
+    f32, bf16 = jnp.float32, jnp.bfloat16
+
+    own = pl.pallas_call(
+        project_kernel,
+        out_shape=jax.ShapeDtypeStruct((2 * rank, examples * LANES), f32),
+        in_specs=[VMEM] * 6,
+        out_specs=VMEM,
+        compiler_params=PARAMS,
+        name="project",
+    )(pub_in, pub_out, priv_in, priv_out, down.T, up)
+    step = 1
+    while step < mp:
+        other = exchange(own, "mp", step)
+        step *= 2
+        if step < mp:
+            own = own + other
+
+    block = jax.ShapeDtypeStruct((examples * 2 * rank, lanes), bf16)
+    blocks = pl.pallas_call(
+        functools.partial(gradient_kernel, dp),
+        out_shape=[block] * dp,
+        in_specs=[SMEM] * 2 + [VMEM] * 6,
+        out_specs=[VMEM] * dp,
+        scratch_shapes=[
+            pltpu.VMEM((dp * rank, lanes), bf16),
+            pltpu.VMEM((lanes // LANES, dp * rank, LANES), f32),
+        ],
+        compiler_params=PARAMS,
+        name="gradients",
+    )(pub_len, priv_len, own, other, pub_in, pub_out, priv_in, priv_out)
+    blocks = [blocks[0]] + [exchange(blocks[k], "dp", k) for k in range(1, dp)]
+
+    group, shares = pl.pallas_call(
+        functools.partial(gram_kernel, dp, n_pub, n_priv),
+        out_shape=[
+            jax.ShapeDtypeStruct((dp * examples * 2 * rank, lanes), bf16),
+            jax.ShapeDtypeStruct((dp * mp, dp * n_pub, LANES), f32),
+        ],
+        in_specs=[VMEM] * dp,
+        out_specs=[VMEM] * 2,
+        compiler_params=PARAMS,
+        name="inner_products",
+    )(*blocks)
+    shares = lax.all_to_all(shares, ("dp", "mp"), 0, 0, tiled=True)
+
+    gain = 1.0 / math.sqrt(n_priv * dp * tokens)
+    return pl.pallas_call(
+        functools.partial(update_kernel, gain),
+        out_shape=[
+            jax.ShapeDtypeStruct(down_noise.shape, f32),
+            jax.ShapeDtypeStruct(up_noise.shape, f32),
+        ],
+        in_specs=[VMEM, VMEM, SMEM, VMEM, VMEM],
+        out_specs=[VMEM] * 2,
+        compiler_params=PARAMS,
+        name="update",
+    )(shares, group, noise, down_noise, up_noise)
+
+
+def fits(mesh, pub_in, priv_in, up):
+    dp = mesh.shape["dp"]
+    width = pub_in.shape[2] // mesh.shape["mp"]
+    publics = pub_in.shape[0]
+    return (
+        up.shape[0] == 16
+        and dp in (2, 4, 8)
+        and width % (dp * LANES) == 0
+        and publics == 8
+        and priv_in.shape[0] % 8 == 0
+        and publics + priv_in.shape[0] <= LANES // 2
+        and pub_in.shape[1] <= LANES
+    )
 
 
 def partial_gram_terms(
@@ -65,7 +327,7 @@
     return (keep_coefficient, keep_residual)
 
 
-def body(
+def large_group(
     public_input_activations,
     public_output_cotangents,
     public_token_lengths,
@@ -155,6 +417,15 @@
         P("mp", "dp"),
         P("mp", "dp"),
     )
-    return jax.shard_map(
-        body, mesh=mesh, in_specs=placed, out_specs=(P("mp", "dp"), P("mp", "dp")), check_vma=False
-    )
+
+    def run(*arrays):
+        body = small_group if fits(mesh, arrays[0], arrays[3], arrays[7]) else large_group
+        return jax.shard_map(
+            body,
+            mesh=mesh,
+            in_specs=placed,
+            out_specs=(P("mp", "dp"), P("mp", "dp")),
+            check_vma=False,
+        )(*arrays)
+
+    return run

time: 158 us -> 54.2 us (0.34)
  waiting for transfers between devices: 51.1 us -> 11.4 us
  blocking collectives: 39.4 us -> 13 us
  between operations: 16.9 us -> 1.36 us
  matrix products: 11.7 us -> 0 us
  local copies, waits for them, and re-layouts: 14.2 us -> 6.73 us
  Pallas kernels: 0 us -> 6.57 us
  other arithmetic: 5.66 us -> 0.01 us
  starting transfers between devices: 18.4 us -> 14.7 us
    psum x1 -> x0, blocking collectives: 39.4 us -> none  [body(): lax.psum((gram_partial, cross_partial, square_partial), ('dp', 'mp'))]
    psum x1 -> x0, waiting for transfers between devices: 32 us -> none  [body(): lax.psum((public_projected, public_returned, private_projected, private_r...]
    all_to_all x4 -> x0, waiting for transfers between devices: 19.1 us -> none  [the longest x1 8.01 us: body(): lax.all_to_all(private_down, 'dp', split_axis=1, concat_axis=0, tiled=True)]
    all_to_all x4 -> x0, starting transfers between devices: 18.3 us -> none  [the longest x1 5.94 us: body(): lax.all_to_all(private_down, 'dp', split_axis=1, concat_axis=0, tiled=True)]
    ppermute x0 -> x9, starting transfers between devices: none -> 14.7 us  [exchange(): lax.ppermute(x, axis, [(s, s ^ step) for s in range(lax.axis_size(axis))])]
    all_to_all x0 -> x1, blocking collectives: none -> 13 us  [small_group(): shares = lax.all_to_all(shares, ('dp', 'mp'), 0, 0, tiled=True)]
    ppermute x0 -> x9, waiting for transfers between devices: none -> 11.4 us  [exchange(): lax.ppermute(x, axis, [(s, s ^ step) for s in range(lax.axis_size(axis))])]
    dot_general x13 -> x0, matrix products: 11.3 us -> none  [the longest x2 4.07 us: partial_gram_terms(): jnp.einsum('umo,ov->umv', input_activations, adapter_down_matrix, preferr...]
  transfers between devices with their start and end apart: 5 -> 9, of which waited for: 4 -> 3; matrix products, arithmetic and copies ran while one was open for 6% -> 0% of each run, Pallas kernels for 0% -> 0%
where the time goes in v1:
time: 54.2 us; the launch traced here: 53.8 us
  starting transfers between devices  14.7 us (27%)
  blocking collectives  13 us (24%)
  waiting for transfers between devices  11.4 us (21%)
  local copies, waits for them, and re-layouts  6.73 us (12%)
  Pallas kernels  6.57 us (12%)
  between operations  1.36 us (3%)
    ppermute x9, starting transfers between devices, exchange(): lax.ppermute(x, axis, [(s, s ^ step) for s in range(lax.axis_size(axis))])  14.7 us
    all_to_all x1, blocking collectives, small_group(): shares = lax.all_to_all(shares, ('dp', 'mp'), 0, 0, tiled=True)  13 us
    ppermute x9, waiting for transfers between devices, exchange(): lax.ppermute(x, axis, [(s, s ^ step) for s in range(lax.axis_size(axis))])  11.4 us
    unnamed x20, local copies, waits for them, and re-layouts  6.73 us
    pallas_call x1, Pallas kernels, small_group(): pl.pallas_call(functools.partial(update_kernel, gain), out_shape=[jax.Sha...  2.52 us
    pallas_call x1, Pallas kernels, small_group(): pl.pallas_call(functools.partial(gram_kernel, dp, n_pub, n_priv), out_sha...  1.4 us
    pallas_call x1, Pallas kernels, small_group(): pl.pallas_call(functools.partial(gradient_kernel, dp), out_shape=[block]...  1.37 us
    pallas_call x1, Pallas kernels, small_group(): pl.pallas_call(project_kernel, out_shape=jax.ShapeDtypeStruct((2 * rank,...  1.29 us
  transfers between devices with their start and end apart: 9, of which 3 were waited for; matrix products, arithmetic and copies ran while one was open for 0% of the time, Pallas kernels for 0%

profile of v1, /device:TPU:0, one launch (start us, length us, event | category | flops | bytes accessed | tf_op | source)
XLA Modules:
  0.0 53.8 jit_solution(14955093484357180267)
XLA Ops:
  0.6 0.0 copy-start
  0.6 1.5 %copy-done = bf16[4,112,2048]{2,1,0:T(8,128)(2,1)S(1)} copy-done((bf16[4,112,2048]{2,1,0:T(8,128)(2,1)S(1)}, bf16[4,112,2048]{2,1,0:T(8,128)(2,1)}, u32[]{:S(2)}) %copy-start) | copy-done | bytes 1835032
  2.1 0.0 copy-start.1
  2.1 1.5 %copy-done.1 = bf16[4,112,2048]{2,1,0:T(8,128)(2,1)S(1)} copy-done((bf16[4,112,2048]{2,1,0:T(8,128)(2,1)S(1)}, bf16[4,112,2048]{2,1,0:T(8,128)(2,1)}, u32[]{:S(2)}) %copy-start.1) | copy-done | bytes 1835032
  3.6 0.0 copy-start.2
  3.6 1.0 %copy-done.2 = bf16[1,112,2048]{2,1,0:T(8,128)(2,1)S(1)} copy-done((bf16[1,112,2048]{2,1,0:T(8,128)(2,1)S(1)}, bf16[1,112,2048]{2,1,0:T(8,128)(2,1)}, u32[]{:S(2)}) %copy-start.2) | copy-done | bytes 458776
  4.7 0.0 copy-start.3
  4.7 1.0 %copy-done.3 = bf16[1,112,2048]{2,1,0:T(8,128)(2,1)S(1)} copy-done((bf16[1,112,2048]{2,1,0:T(8,128)(2,1)S(1)}, bf16[1,112,2048]{2,1,0:T(8,128)(2,1)}, u32[]{:S(2)}) %copy-start.3) | copy-done | bytes 458776
  5.7 0.0 copy-start.4
  5.7 0.8 %copy-done.4 = bf16[2048,16]{0,1:T(8,128)(2,1)S(1)} copy-done((bf16[2048,16]{0,1:T(8,128)(2,1)S(1)}, bf16[2048,16]{0,1:T(8,128)(2,1)}, u32[]{:S(2)}) %copy-start.4) | copy-done | bytes 65560
  6.5 0.0 copy-start.5
  6.5 0.8 %copy-done.5 = bf16[16,2048]{1,0:T(8,128)(2,1)S(1)} copy-done((bf16[16,2048]{1,0:T(8,128)(2,1)S(1)}, bf16[16,2048]{1,0:T(8,128)(2,1)}, u32[]{:S(2)}) %copy-start.5) | copy-done | bytes 65560
  7.4 0.0 copy-start.9
  7.4 1.3 %project.1 = f32[32,640]{1,0:T(8,128)S(1)} custom-call(bf16[1,112,2048]{2,1,0:T(8,128)(2,1)S(1)} %copy-done.2, bf16[1,112,2048]{2,1,0:T(8,128)(2,1)S(1)} %copy-done.3, bf16[4,112,2048]{2,1,0:T(8,128)(2,1)S(1)} %copy-done, bf16[4,112,2048]{2,1,0:T(8,128)(2,1)S(1)} %copy-done.1, bf16[16,2048]{1,0:T(8,128)(2,1)S(1)} %bitcast.1, bf16[16,2048]{1,0:T(8,128)(2,1)S(1)} %copy-done.5), custom_call_target="tpu_custom_call" | custom-call | tf_op jit(solution)/shard_map/project/pallas_call | solution.py:205
  8.6 0.5 collective-permute-start
  9.1 0.9 %collective-permute-done = f32[32,640]{1,0:T(8,128)S(1)} collective-permute-done((f32[32,640]{1,0:T(8,128)S(1)}, f32[32,640]{1,0:T(8,128)S(1)}, u32[]{:S(2)}, u32[]{:S(2)}) %collective-permute-start) | collective-permute-done | bytes 81952 | tf_op jit(solution)/shard_map/ppermute | solution.py:191
  10.0 2.9 %collective-permute-start.1 = (f32[32,640]{1,0:T(8,128)S(1)}, f32[32,640]{1,0:T(8,128)S(1)}, u32[]{:S(2)}, u32[]{:S(2)}) collective-permute-start(f32[32,640]{1,0:T(8,128)S(1)} %add.3.own), channel_id=1, source_target_pairs={{0,2},{1,3},{2,0},{3,1},{4,6},{5,7},{6,4},{7,5},{8,10},{9,11},{10,... | collective-permute-start | bytes 245768 | tf_op jit(solution)/shard_map/ppermute | solution.py:191
  13.6 0.0 copy-start.6
  13.6 0.0 copy-start.7
  13.6 0.0 copy-start.8
  13.6 2.1 %collective-permute-done.1.other = f32[32,640]{1,0:T(8,128)S(1)} collective-permute-done((f32[32,640]{1,0:T(8,128)S(1)}, f32[32,640]{1,0:T(8,128)S(1)}, u32[]{:S(2)}, u32[]{:S(2)}) %collective-permute-start.1) | collective-permute-done | bytes 81952 | tf_op jit(solution)/shard_map/ppermute | solution.py:191
  15.7 0.0 copy-done.9
  15.7 1.4 %gradients.1 = (bf16[160,256]{1,0:T(8,128)(2,1)S(1)}, bf16[160,256]{1,0:T(8,128)(2,1)S(1)}, bf16[160,256]{1,0:T(8,128)(2,1)S(1)}, bf16[160,256]{1,0:T(8,128)(2,1...) custom-call(s32[1]{0:T(128)S(6)} %copy.13.pub_len, ...), custom_call_target="tpu_custom_call" | custom-call | tf_op jit(solution)/shard_map/gradients/pallas_call | solution.py:221
  17.1 1.8 %collective-permute-start.2 = (bf16[160,256]{1,0:T(8,128)(2,1)S(1)}, bf16[160,256]{1,0:T(8,128)(2,1)S(1)}, u32[]{:S(2)}, u32[]{:S(2)}) collective-permute-start(bf16[160,256]{1,0:T(8,128)(2,1)S(1)} %get-tuple-element.13), channel_id=1, source_target_pairs={{0,4},{4,0},{8,12},{12,8},{16,20},{20,16},{24,28},{28,24},{1,5},{5... | collective-permute-start | bytes 245768 | tf_op jit(solution)/shard_map/ppermute | solution.py:191
  18.9 1.6 %collective-permute-start.3 = (bf16[160,256]{1,0:T(8,128)(2,1)S(1)}, bf16[160,256]{1,0:T(8,128)(2,1)S(1)}, u32[]{:S(2)}, u32[]{:S(2)}) collective-permute-start(bf16[160,256]{1,0:T(8,128)(2,1)S(1)} %get-tuple-element.14), channel_id=1, source_target_pairs={{0,8},{4,12},{8,0},{12,4},{16,24},{20,28},{24,16},{28,20},{1,9},{5... | collective-permute-start | bytes 245768 | tf_op jit(solution)/shard_map/ppermute | solution.py:191
  20.5 0.1 collective-permute-start.4
  20.7 2.9 %collective-permute-start.5 = (bf16[160,256]{1,0:T(8,128)(2,1)S(1)}, bf16[160,256]{1,0:T(8,128)(2,1)S(1)}, u32[]{:S(2)}, u32[]{:S(2)}) collective-permute-start(bf16[160,256]{1,0:T(8,128)(2,1)S(1)} %get-tuple-element.16), channel_id=1, source_target_pairs={{0,16},{4,20},{8,24},{12,28},{16,0},{20,4},{24,8},{28,12},{1,17},{... | collective-permute-start | bytes 245768 | tf_op jit(solution)/shard_map/ppermute | solution.py:191
  23.5 1.3 %collective-permute-start.6 = (bf16[160,256]{1,0:T(8,128)(2,1)S(1)}, bf16[160,256]{1,0:T(8,128)(2,1)S(1)}, u32[]{:S(2)}, u32[]{:S(2)}) collective-permute-start(bf16[160,256]{1,0:T(8,128)(2,1)S(1)} %get-tuple-element.17), channel_id=1, source_target_pairs={{0,20},{4,16},{8,28},{12,24},{16,4},{20,0},{24,12},{28,8},{1,21},{... | collective-permute-start | bytes 245768 | tf_op jit(solution)/shard_map/ppermute | solution.py:191
  24.8 0.0 collective-permute-done.2.refs_1_
  24.8 3.6 %collective-permute-start.7 = (bf16[160,256]{1,0:T(8,128)(2,1)S(1)}, bf16[160,256]{1,0:T(8,128)(2,1)S(1)}, u32[]{:S(2)}, u32[]{:S(2)}) collective-permute-start(bf16[160,256]{1,0:T(8,128)(2,1)S(1)} %get-tuple-element.18), channel_id=1, source_target_pairs={{0,24},{4,28},{8,16},{12,20},{16,8},{20,12},{24,0},{28,4},{1,25},{... | collective-permute-start | bytes 245768 | tf_op jit(solution)/shard_map/ppermute | solution.py:191
  28.4 0.0 collective-permute-done.3.refs_2_
  28.4 0.0 collective-permute-start.8
  28.4 0.0 collective-permute-done.4.refs_3_
  28.4 0.0 collective-permute-done.5.refs_4_
  28.4 8.4 %collective-permute-done.6.refs_5_ = bf16[160,256]{1,0:T(8,128)(2,1)S(1)} collective-permute-done((bf16[160,256]{1,0:T(8,128)(2,1)S(1)}, bf16[160,256]{1,0:T(8,128)(2,1)S(1)}, u32[]{:S(2)}, u32[]{:S(2)}) %collective-permute-start.6) | collective-permute-done | bytes 81952 | tf_op jit(solution)/shard_map/ppermute | solution.py:191
  36.8 0.0 collective-permute-done.7.refs_6_
  36.8 0.0 collective-permute-done.8.refs_7_
  36.8 1.4 %inner_products.1 = (bf16[1280,256]{1,0:T(8,128)(2,1)S(1)}, f32[32,8,128]{2,1,0:T(8,128)S(1)}) custom-call(bf16[160,256]{1,0:T(8,128)(2,1)S(1)} %get-tuple-element.12.refs_0_, bf16[160,256]{1,0:T(8,128)(2,1)S(1)} %collective-permute-done.2.refs_1_, bf16[160,256]{1,0:T(8,128)(2,1)S(1)} %collective-permute-done.3.refs_2_, ...), custom_call_target="tpu_custom_call" | custom-call | tf_op jit(solution)/shard_map/inner_products/pallas_call | solution.py:235
  38.3 13.0 %all_to_all.5.shares = f32[32,8,128]{2,1,0:T(8,128)S(1)} all-to-all(f32[32,8,128]{2,1,0:T(8,128)S(1)} %get-tuple-element.20), channel_id=1, replica_groups=mesh['dp'=8,'mp'=4] {'dp','mp'}, dimensions={0} | all-to-all | bytes 262144 | tf_op jit(solution)/shard_map/all_to_all | solution.py:246
  51.3 0.0 copy-done.6
  51.3 0.0 copy-done.7
  51.3 0.0 copy-done.8
  51.3 2.5 %update.1 = (f32[1,4096]{1,0:T(1,128)}, f32[1,4096]{1,0:T(1,128)}) custom-call(f32[32,8,128]{2,1,0:T(8,128)S(1)} %all_to_all.5.shares, bf16[1280,256]{1,0:T(8,128)(2,1)S(1)} %get-tuple-element.21.group, f32[8]{0:T(128)S(1)} %copy-done.8, f32[1,4096]{1,0:T(1,128)S(1)} %copy-done.6, f32[1,4096]{1,0:T(1,128)S(1)} %copy-done.7), custom_call_target="tpu_custom_call" | custom-call | tf_op jit(solution)/shard_map/update/pallas_call | solution.py:249
  (1 shorter events, 0.0 us)
Async XLA Ops:
  0.6 1.5 %copy-start = (bf16[4,112,2048]{2,1,0:T(8,128)(2,1)S(1)}, bf16[4,112,2048]{2,1,0:T(8,128)(2,1)}, u32[]{:S(2)}) copy-start(bf16[4,112,2048]{2,1,0:T(8,128)(2,1)} %priv_in.3) | copy-start | bytes 5505028
  2.1 1.5 %copy-start.1 = (bf16[4,112,2048]{2,1,0:T(8,128)(2,1)S(1)}, bf16[4,112,2048]{2,1,0:T(8,128)(2,1)}, u32[]{:S(2)}) copy-start(bf16[4,112,2048]{2,1,0:T(8,128)(2,1)} %priv_out.3) | copy-start | bytes 5505028
  3.6 1.0 %copy-start.2 = (bf16[1,112,2048]{2,1,0:T(8,128)(2,1)S(1)}, bf16[1,112,2048]{2,1,0:T(8,128)(2,1)}, u32[]{:S(2)}) copy-start(bf16[1,112,2048]{2,1,0:T(8,128)(2,1)} %pub_in.3) | copy-start | bytes 1376260
  4.7 1.0 %copy-start.3 = (bf16[1,112,2048]{2,1,0:T(8,128)(2,1)S(1)}, bf16[1,112,2048]{2,1,0:T(8,128)(2,1)}, u32[]{:S(2)}) copy-start(bf16[1,112,2048]{2,1,0:T(8,128)(2,1)} %pub_out.3) | copy-start | bytes 1376260
  5.7 0.8 %copy-start.4 = (bf16[2048,16]{0,1:T(8,128)(2,1)S(1)}, bf16[2048,16]{0,1:T(8,128)(2,1)}, u32[]{:S(2)}) copy-start(bf16[2048,16]{0,1:T(8,128)(2,1)} %param.17) | copy-start | bytes 196612
  6.5 0.8 %copy-start.5 = (bf16[16,2048]{1,0:T(8,128)(2,1)S(1)}, bf16[16,2048]{1,0:T(8,128)(2,1)}, u32[]{:S(2)}) copy-start(bf16[16,2048]{1,0:T(8,128)(2,1)} %up.1) | copy-start | bytes 196612
  7.4 8.4 %copy-start.9 = (s32[4]{0:T(128)S(1)}, s32[4]{0:T(128)}, u32[]{:S(2)}) copy-start(s32[4]{0:T(128)} %priv_len.1) | copy-start | bytes 52
  8.6 1.4 %collective-permute-start = (f32[32,640]{1,0:T(8,128)S(1)}, f32[32,640]{1,0:T(8,128)S(1)}, u32[]{:S(2)}, u32[]{:S(2)}) collective-permute-start(f32[32,640]{1,0:T(8,128)S(1)} %project.1), channel_id=1, source_target_pairs={{0,1},{1,0},{2,3},{3,2},{4,5},{5,4},{6,7},{7,6},{8,9},{9,8},{10,11... | collective-permute-start | bytes 245768 | tf_op jit(solution)/shard_map/ppermute | solution.py:191
  10.0 5.7 %collective-permute-start.1 = (f32[32,640]{1,0:T(8,128)S(1)}, f32[32,640]{1,0:T(8,128)S(1)}, u32[]{:S(2)}, u32[]{:S(2)}) collective-permute-start(f32[32,640]{1,0:T(8,128)S(1)} %add.3.own), channel_id=1, source_target_pairs={{0,2},{1,3},{2,0},{3,1},{4,6},{5,7},{6,4},{7,5},{8,10},{9,11},{10,... | collective-permute-start | bytes 245768 | tf_op jit(solution)/shard_map/ppermute | solution.py:191
  13.6 37.7 %copy-start.6 = (f32[1,4096]{1,0:T(1,128)S(1)}, f32[1,4096]{1,0:T(1,128)}, u32[]{:S(2)}) copy-start(f32[1,4096]{1,0:T(1,128)} %down_noise.1) | copy-start | bytes 49156
  13.6 37.7 %copy-start.7 = (f32[1,4096]{1,0:T(1,128)S(1)}, f32[1,4096]{1,0:T(1,128)}, u32[]{:S(2)}) copy-start(f32[1,4096]{1,0:T(1,128)} %up_noise.1) | copy-start | bytes 49156
  13.6 37.7 %copy-start.8 = (f32[8]{0:T(128)S(1)}, f32[8]{0:T(128)}, u32[]{:S(2)}) copy-start(f32[8]{0:T(128)} %noise.1) | copy-start | bytes 100
  17.1 7.7 %collective-permute-start.2 = (bf16[160,256]{1,0:T(8,128)(2,1)S(1)}, bf16[160,256]{1,0:T(8,128)(2,1)S(1)}, u32[]{:S(2)}, u32[]{:S(2)}) collective-permute-start(bf16[160,256]{1,0:T(8,128)(2,1)S(1)} %get-tuple-element.13), channel_id=1, source_target_pairs={{0,4},{4,0},{8,12},{12,8},{16,20},{20,16},{24,28},{28,24},{1,5},{5... | collective-permute-start | bytes 245768 | tf_op jit(solution)/shard_map/ppermute | solution.py:191
  18.9 9.5 %collective-permute-start.3 = (bf16[160,256]{1,0:T(8,128)(2,1)S(1)}, bf16[160,256]{1,0:T(8,128)(2,1)S(1)}, u32[]{:S(2)}, u32[]{:S(2)}) collective-permute-start(bf16[160,256]{1,0:T(8,128)(2,1)S(1)} %get-tuple-element.14), channel_id=1, source_target_pairs={{0,8},{4,12},{8,0},{12,4},{16,24},{20,28},{24,16},{28,20},{1,9},{5... | collective-permute-start | bytes 245768 | tf_op jit(solution)/shard_map/ppermute | solution.py:191
  20.5 7.9 %collective-permute-start.4 = (bf16[160,256]{1,0:T(8,128)(2,1)S(1)}, bf16[160,256]{1,0:T(8,128)(2,1)S(1)}, u32[]{:S(2)}, u32[]{:S(2)}) collective-permute-start(bf16[160,256]{1,0:T(8,128)(2,1)S(1)} %get-tuple-element.15), channel_id=1, source_target_pairs={{0,12},{4,8},{8,4},{12,0},{16,28},{20,24},{24,20},{28,16},{1,13},{... | collective-permute-start | bytes 245768 | tf_op jit(solution)/shard_map/ppermute | solution.py:191
  20.7 7.8 %collective-permute-start.5 = (bf16[160,256]{1,0:T(8,128)(2,1)S(1)}, bf16[160,256]{1,0:T(8,128)(2,1)S(1)}, u32[]{:S(2)}, u32[]{:S(2)}) collective-permute-start(bf16[160,256]{1,0:T(8,128)(2,1)S(1)} %get-tuple-element.16), channel_id=1, source_target_pairs={{0,16},{4,20},{8,24},{12,28},{16,0},{20,4},{24,8},{28,12},{1,17},{... | collective-permute-start | bytes 245768 | tf_op jit(solution)/shard_map/ppermute | solution.py:191
  23.5 13.3 %collective-permute-start.6 = (bf16[160,256]{1,0:T(8,128)(2,1)S(1)}, bf16[160,256]{1,0:T(8,128)(2,1)S(1)}, u32[]{:S(2)}, u32[]{:S(2)}) collective-permute-start(bf16[160,256]{1,0:T(8,128)(2,1)S(1)} %get-tuple-element.17), channel_id=1, source_target_pairs={{0,20},{4,16},{8,28},{12,24},{16,4},{20,0},{24,12},{28,8},{1,21},{... | collective-permute-start | bytes 245768 | tf_op jit(solution)/shard_map/ppermute | solution.py:191
  24.8 12.1 %collective-permute-start.7 = (bf16[160,256]{1,0:T(8,128)(2,1)S(1)}, bf16[160,256]{1,0:T(8,128)(2,1)S(1)}, u32[]{:S(2)}, u32[]{:S(2)}) collective-permute-start(bf16[160,256]{1,0:T(8,128)(2,1)S(1)} %get-tuple-element.18), channel_id=1, source_target_pairs={{0,24},{4,28},{8,16},{12,20},{16,8},{20,12},{24,0},{28,4},{1,25},{... | collective-permute-start | bytes 245768 | tf_op jit(solution)/shard_map/ppermute | solution.py:191
  28.4 8.4 %collective-permute-start.8 = (bf16[160,256]{1,0:T(8,128)(2,1)S(1)}, bf16[160,256]{1,0:T(8,128)(2,1)S(1)}, u32[]{:S(2)}, u32[]{:S(2)}) collective-permute-start(bf16[160,256]{1,0:T(8,128)(2,1)S(1)} %get-tuple-element.19), channel_id=1, source_target_pairs={{0,28},{4,24},{8,20},{12,16},{16,12},{20,8},{24,4},{28,0},{1,29},{... | collective-permute-start | bytes 245768 | tf_op jit(solution)/shard_map/ppermute | solution.py:191

commit v2 on v1

--- a/solution.py
+++ b/solution.py
@@ -14,7 +14,9 @@
 SIGMA_RESIDUAL = 0.04
 PRECISE = lax.Precision.HIGHEST
 LANES = 128
+GROUP = 4
 VMEM = pl.BlockSpec(memory_space=pltpu.VMEM)
+HBM = pl.BlockSpec(memory_space=pltpu.HBM)
 SMEM = pl.BlockSpec(memory_space=pltpu.SMEM)
 BOTH_LAST = (((1,), (1,)), ((), ()))
 FIRST_LAST = (((1,), (0,)), ((), ()))
@@ -29,17 +31,38 @@
     return lax.broadcasted_iota(jnp.int32, shape, axis)
 
 
-def project_kernel(pub_in, pub_out, priv_in, priv_out, down_t, up, out):
+def project_kernel(pub_in, pub_out, priv_in, priv_out, down_t, up, *rest):
+    out, held, (down_held, up_held, sems) = rest[0], rest[1:5], rest[5:]
     rank = up.shape[0]
     tokens = pub_in.shape[1]
+    copies = [
+        pltpu.make_async_copy(down_t, down_held, sems.at[0]),
+        pltpu.make_async_copy(up, up_held, sems.at[1]),
+    ]
+    pieces = []
+    for inputs, cotangents, inputs_held, cotangents_held in (
+        (pub_in, pub_out, held[0], held[1]),
+        (priv_in, priv_out, held[2], held[3]),
+    ):
+        for e in range(inputs.shape[0]):
+            pieces += [(down_held, inputs_held.at[e]), (up_held, cotangents_held.at[e])]
+            for source, to in ((inputs, inputs_held), (cotangents, cotangents_held)):
+                copies.append(
+                    pltpu.make_async_copy(source.at[e], to.at[e], sems.at[len(copies)])
+                )
+    for copy in copies:
+        copy.start()
     out[...] = jnp.zeros_like(out)
-    slot = 0
-    for inputs, cotangents in ((pub_in, pub_out), (priv_in, priv_out)):
-        for e in range(inputs.shape[0]):
-            at = slice(slot * LANES, slot * LANES + tokens)
-            out[0:rank, at] = dot(down_t[...], inputs[e], BOTH_LAST)
-            out[rank : 2 * rank, at] = dot(up[...], cotangents[e], BOTH_LAST)
-            slot += 1
+    for copy in copies[:2]:
+        copy.wait()
+    for i, (weights, piece) in enumerate(pieces):
+        if i % GROUP == 0:
+            for copy in copies[2 + i : 2 + i + GROUP]:
+                copy.wait()
+        slot, half = i // 2, i % 2
+        out[half * rank : (half + 1) * rank, slot * LANES : slot * LANES + tokens] = dot(
+            weights[...], piece[...], BOTH_LAST
+        )
 
 
 def gradient_kernel(dp, pub_len, priv_len, own, other, pub_in, pub_out, priv_in, priv_out, *rest):
@@ -83,17 +106,18 @@
             slot += 1
 
 
-def gram_kernel(dp, n_pub, n_priv, *refs):
+def gram_kernel(order, n_pub, n_priv, *refs):
+    dp = len(order)
     blocks, group, out = refs[:dp], refs[dp], refs[dp + 1]
     me = lax.axis_index("dp")
     rows = blocks[0].shape[0] // (n_pub + n_priv)
     pub_rows, priv_rows = n_pub * rows, n_priv * rows
-    for k in range(dp):
+    for k, block in zip(order, blocks):
         source = me ^ k
-        group[pl.ds(pl.multiple_of(source * pub_rows, pub_rows), pub_rows), :] = blocks[k][:pub_rows]
+        group[pl.ds(pl.multiple_of(source * pub_rows, pub_rows), pub_rows), :] = block[:pub_rows]
         group[
             pl.ds(pl.multiple_of(dp * pub_rows + source * priv_rows, priv_rows), priv_rows), :
-        ] = blocks[k][pub_rows:]
+        ] = block[pub_rows:]
     publics = dp * n_pub
     span = publics * rows
     lanes = group.shape[1]
@@ -202,14 +226,25 @@
     lanes = width // dp
     f32, bf16 = jnp.float32, jnp.bfloat16
 
-    own = pl.pallas_call(
+    own, *held = pl.pallas_call(
         project_kernel,
-        out_shape=jax.ShapeDtypeStruct((2 * rank, examples * LANES), f32),
-        in_specs=[VMEM] * 6,
-        out_specs=VMEM,
+        out_shape=[jax.ShapeDtypeStruct((2 * rank, examples * LANES), f32)]
+        + [jax.ShapeDtypeStruct(x.shape, bf16) for x in (pub_in, pub_out, priv_in, priv_out)],
+        in_specs=[HBM] * 6,
+        out_specs=[VMEM] * 5,
+        scratch_shapes=[
+            pltpu.VMEM(up.shape, bf16),
+            pltpu.VMEM(up.shape, bf16),
+            pltpu.SemaphoreType.DMA((2 + 2 * examples,)),
+        ],
         compiler_params=PARAMS,
         name="project",
-    )(pub_in, pub_out, priv_in, priv_out, down.T, up)
+    )(
+        *(
+            pltpu.with_memory_space_constraint(x, pltpu.HBM)
+            for x in (pub_in, pub_out, priv_in, priv_out, down.T, up)
+        )
+    )
     step = 1
     while step < mp:
         other = exchange(own, "mp", step)
@@ -229,11 +264,12 @@
         ],
         compiler_params=PARAMS,
         name="gradients",
-    )(pub_len, priv_len, own, other, pub_in, pub_out, priv_in, priv_out)
-    blocks = [blocks[0]] + [exchange(blocks[k], "dp", k) for k in range(1, dp)]
+    )(pub_len, priv_len, own, other, *held)
+    order = sorted(range(1, dp), key=lambda k: (-k.bit_length(), k & 1, k)) + [0]
+    blocks = [exchange(blocks[k], "dp", k) if k else blocks[k] for k in order]
 
     group, shares = pl.pallas_call(
-        functools.partial(gram_kernel, dp, n_pub, n_priv),
+        functools.partial(gram_kernel, order, n_pub, n_priv),
         out_shape=[
             jax.ShapeDtypeStruct((dp * examples * 2 * rank, lanes), bf16),
             jax.ShapeDtypeStruct((dp * mp, dp * n_pub, LANES), f32),

time: 54.2 us -> 49.2 us (0.908)
  local copies, waits for them, and re-layouts: 6.73 us -> 0.02 us
  Pallas kernels: 6.57 us -> 8.51 us
    unnamed x20 -> x8, local copies, waits for them, and re-layouts: 6.73 us -> 0.02 us
    pallas_call x2, Pallas kernels: 2.68 us -> 4.58 us  [the longest x1 3.18 us: small_group(): pl.pallas_call(project_kernel, out_shape=[jax.ShapeDtypeStruct((2 * rank,...]
  transfers between devices with their start and end apart: 9 -> 9, of which waited for: 3 -> 6; matrix products, arithmetic and copies ran while one was open for 0% -> 0% of each run, Pallas kernels for 0% -> 0%
where the time goes in v2:
time: 49.2 us; the launch traced here: 49 us
  starting transfers between devices  14.7 us (30%)
  blocking collectives  13.2 us (27%)
  waiting for transfers between devices  11.2 us (23%)
  Pallas kernels  8.51 us (17%)
  between operations  1.34 us (3%)
    ppermute x9, starting transfers between devices, exchange(): lax.ppermute(x, axis, [(s, s ^ step) for s in range(lax.axis_size(axis))])  14.7 us
    all_to_all x1, blocking collectives, small_group(): shares = lax.all_to_all(shares, ('dp', 'mp'), 0, 0, tiled=True)  13.2 us
    ppermute x9, waiting for transfers between devices, exchange(): lax.ppermute(x, axis, [(s, s ^ step) for s in range(lax.axis_size(axis))])  11.2 us
    pallas_call x1, Pallas kernels, small_group(): pl.pallas_call(project_kernel, out_shape=[jax.ShapeDtypeStruct((2 * rank,...  3.18 us
    pallas_call x1, Pallas kernels, small_group(): pl.pallas_call(functools.partial(update_kernel, gain), out_shape=[jax.Sha...  2.52 us
    pallas_call x1, Pallas kernels, small_group(): pl.pallas_call(functools.partial(gradient_kernel, dp), out_shape=[block]...  1.42 us
    pallas_call x1, Pallas kernels, small_group(): pl.pallas_call(functools.partial(gram_kernel, order, n_pub, n_priv), out_...  1.4 us
  transfers between devices with their start and end apart: 9, of which 6 were waited for; matrix products, arithmetic and copies ran while one was open for 0% of the time, Pallas kernels for 0%

profile of v2, /device:TPU:0, one launch (start us, length us, event | category | flops | bytes accessed | tf_op | source)
XLA Modules:
  0.0 49.0 jit_solution(12156131470925998937)
XLA Ops:
  0.6 0.0 copy-start.3
  0.6 3.2 %project.1 = (f32[32,640]{1,0:T(8,128)S(1)}, bf16[1,112,2048]{2,1,0:T(8,128)(2,1)S(1)}, bf16[1,112,2048]{2,1,0:T(8,128)(2,1)S(1)}, bf16[4,112,2048]{2,1,0:T(8,128)(2,1)S(1)}, bf16[4,112,2048]{2,1,0:T(8,128)(2,1)S(1)}) custom-call(bf16[1,112,2048]{2,1,0:T(8,128)(2,1)} %pub_in.1, bf16[1,112,2048]{2,1,0:T(8,128)(2,1)} %pub_out.1, ...), custom_call_target="tpu_custom_call" | custom-call | tf_op jit(solution)/shard_map/project/pallas_call | solution.py:229
  3.8 0.5 %collective-permute-start = (f32[32,640]{1,0:T(8,128)S(1)}, f32[32,640]{1,0:T(8,128)S(1)}, u32[]{:S(2)}, u32[]{:S(2)}) collective-permute-start(f32[32,640]{1,0:T(8,128)S(1)} %get-tuple-element.17), channel_id=1, source_target_pairs={{0,1},{1,0},{2,3},{3,2},{4,5},{5,4},{6,7},{7,6},{8,9},{9,8},{10,11... | collective-permute-start | bytes 245768 | tf_op jit(solution)/shard_map/ppermute | solution.py:215
  4.3 0.9 %collective-permute-done = f32[32,640]{1,0:T(8,128)S(1)} collective-permute-done((f32[32,640]{1,0:T(8,128)S(1)}, f32[32,640]{1,0:T(8,128)S(1)}, u32[]{:S(2)}, u32[]{:S(2)}) %collective-permute-start) | collective-permute-done | bytes 81952 | tf_op jit(solution)/shard_map/ppermute | solution.py:215
  5.3 2.9 %collective-permute-start.1 = (f32[32,640]{1,0:T(8,128)S(1)}, f32[32,640]{1,0:T(8,128)S(1)}, u32[]{:S(2)}, u32[]{:S(2)}) collective-permute-start(f32[32,640]{1,0:T(8,128)S(1)} %add.3.own), channel_id=1, source_target_pairs={{0,2},{1,3},{2,0},{3,1},{4,6},{5,7},{6,4},{7,5},{8,10},{9,11},{10,... | collective-permute-start | bytes 245768 | tf_op jit(solution)/shard_map/ppermute | solution.py:215
  8.8 2.1 %collective-permute-done.1.other = f32[32,640]{1,0:T(8,128)S(1)} collective-permute-done((f32[32,640]{1,0:T(8,128)S(1)}, f32[32,640]{1,0:T(8,128)S(1)}, u32[]{:S(2)}, u32[]{:S(2)}) %collective-permute-start.1) | collective-permute-done | bytes 81952 | tf_op jit(solution)/shard_map/ppermute | solution.py:215
  11.0 0.0 copy-done.3
  11.0 0.0 copy-start
  11.0 0.0 copy-start.1
  11.0 0.0 copy-start.2
  11.0 1.4 %gradients.1 = (bf16[160,256]{1,0:T(8,128)(2,1)S(1)}, bf16[160,256]{1,0:T(8,128)(2,1)S(1)}, bf16[160,256]{1,0:T(8,128)(2,1)S(1)}, bf16[160,256]{1,0:T(8,128)(2,1...) custom-call(s32[1]{0:T(128)S(6)} %copy.13.pub_len, ...), custom_call_target="tpu_custom_call" | custom-call | tf_op jit(solution)/shard_map/gradients/pallas_call | solution.py:256
  12.4 2.9 %collective-permute-start.2 = (bf16[160,256]{1,0:T(8,128)(2,1)S(1)}, bf16[160,256]{1,0:T(8,128)(2,1)S(1)}, u32[]{:S(2)}, u32[]{:S(2)}) collective-permute-start(bf16[160,256]{1,0:T(8,128)(2,1)S(1)} %get-tuple-element.22), channel_id=1, source_target_pairs={{0,16},{4,20},{8,24},{12,28},{16,0},{20,4},{24,8},{28,12},{1,17},{... | collective-permute-start | bytes 245768 | tf_op jit(solution)/shard_map/ppermute | solution.py:215
  15.3 1.3 %collective-permute-start.3 = (bf16[160,256]{1,0:T(8,128)(2,1)S(1)}, bf16[160,256]{1,0:T(8,128)(2,1)S(1)}, u32[]{:S(2)}, u32[]{:S(2)}) collective-permute-start(bf16[160,256]{1,0:T(8,128)(2,1)S(1)} %get-tuple-element.23), channel_id=1, source_target_pairs={{0,24},{4,28},{8,16},{12,20},{16,8},{20,12},{24,0},{28,4},{1,25},{... | collective-permute-start | bytes 245768 | tf_op jit(solution)/shard_map/ppermute | solution.py:215
  16.6 2.7 %collective-permute-start.4 = (bf16[160,256]{1,0:T(8,128)(2,1)S(1)}, bf16[160,256]{1,0:T(8,128)(2,1)S(1)}, u32[]{:S(2)}, u32[]{:S(2)}) collective-permute-start(bf16[160,256]{1,0:T(8,128)(2,1)S(1)} %get-tuple-element.24), channel_id=1, source_target_pairs={{0,20},{4,16},{8,28},{12,24},{16,4},{20,0},{24,12},{28,8},{1,21},{... | collective-permute-start | bytes 245768 | tf_op jit(solution)/shard_map/ppermute | solution.py:215
  19.3 0.8 %collective-permute-start.5 = (bf16[160,256]{1,0:T(8,128)(2,1)S(1)}, bf16[160,256]{1,0:T(8,128)(2,1)S(1)}, u32[]{:S(2)}, u32[]{:S(2)}) collective-permute-start(bf16[160,256]{1,0:T(8,128)(2,1)S(1)} %get-tuple-element.25), channel_id=1, source_target_pairs={{0,28},{4,24},{8,20},{12,16},{16,12},{20,8},{24,4},{28,0},{1,29},{... | collective-permute-start | bytes 245768 | tf_op jit(solution)/shard_map/ppermute | solution.py:215
  20.2 0.9 %collective-permute-start.6 = (bf16[160,256]{1,0:T(8,128)(2,1)S(1)}, bf16[160,256]{1,0:T(8,128)(2,1)S(1)}, u32[]{:S(2)}, u32[]{:S(2)}) collective-permute-start(bf16[160,256]{1,0:T(8,128)(2,1)S(1)} %get-tuple-element.26), channel_id=1, source_target_pairs={{0,8},{4,12},{8,0},{12,4},{16,24},{20,28},{24,16},{28,20},{1,9},{5... | collective-permute-start | bytes 245768 | tf_op jit(solution)/shard_map/ppermute | solution.py:215
  21.0 2.8 %collective-permute-done.2.refs_0_ = bf16[160,256]{1,0:T(8,128)(2,1)S(1)} collective-permute-done((bf16[160,256]{1,0:T(8,128)(2,1)S(1)}, bf16[160,256]{1,0:T(8,128)(2,1)S(1)}, u32[]{:S(2)}, u32[]{:S(2)}) %collective-permute-start.2) | collective-permute-done | bytes 81952 | tf_op jit(solution)/shard_map/ppermute | solution.py:215
  23.9 2.3 %collective-permute-start.7 = (bf16[160,256]{1,0:T(8,128)(2,1)S(1)}, bf16[160,256]{1,0:T(8,128)(2,1)S(1)}, u32[]{:S(2)}, u32[]{:S(2)}) collective-permute-start(bf16[160,256]{1,0:T(8,128)(2,1)S(1)} %get-tuple-element.27), channel_id=1, source_target_pairs={{0,12},{4,8},{8,4},{12,0},{16,28},{20,24},{24,20},{28,16},{1,13},{... | collective-permute-start | bytes 245768 | tf_op jit(solution)/shard_map/ppermute | solution.py:215
  26.2 0.0 collective-permute-done.3.refs_1_
  26.2 0.4 collective-permute-start.8
  26.5 2.8 %collective-permute-done.4.refs_2_ = bf16[160,256]{1,0:T(8,128)(2,1)S(1)} collective-permute-done((bf16[160,256]{1,0:T(8,128)(2,1)S(1)}, bf16[160,256]{1,0:T(8,128)(2,1)S(1)}, u32[]{:S(2)}, u32[]{:S(2)}) %collective-permute-start.4) | collective-permute-done | bytes 81952 | tf_op jit(solution)/shard_map/ppermute | solution.py:215
  29.4 0.0 collective-permute-done.5.refs_3_
  29.4 0.0 collective-permute-done.6.refs_4_
  29.4 0.8 %collective-permute-done.7.refs_5_ = bf16[160,256]{1,0:T(8,128)(2,1)S(1)} collective-permute-done((bf16[160,256]{1,0:T(8,128)(2,1)S(1)}, bf16[160,256]{1,0:T(8,128)(2,1)S(1)}, u32[]{:S(2)}, u32[]{:S(2)}) %collective-permute-start.7) | collective-permute-done | bytes 81952 | tf_op jit(solution)/shard_map/ppermute | solution.py:215
  30.2 1.7 %collective-permute-done.8.refs_6_ = bf16[160,256]{1,0:T(8,128)(2,1)S(1)} collective-permute-done((bf16[160,256]{1,0:T(8,128)(2,1)S(1)}, bf16[160,256]{1,0:T(8,128)(2,1)S(1)}, u32[]{:S(2)}, u32[]{:S(2)}) %collective-permute-start.8) | collective-permute-done | bytes 81952 | tf_op jit(solution)/shard_map/ppermute | solution.py:215
  31.8 1.4 %inner_products.1 = (bf16[1280,256]{1,0:T(8,128)(2,1)S(1)}, f32[32,8,128]{2,1,0:T(8,128)S(1)}) custom-call(bf16[160,256]{1,0:T(8,128)(2,1)S(1)} %collective-permute-done.2.refs_0_, bf16[160,256]{1,0:T(8,128)(2,1)S(1)} %collective-permute-done.3.refs_1_, bf16[160,256]{1,0:T(8,128)(2,1)S(1)} %collective-permute-done.4.refs_2_, ...), custom_call_target="tpu_custom_call" | custom-call | tf_op jit(solution)/shard_map/inner_products/pallas_call | solution.py:271
  33.2 13.2 %all_to_all.5.shares = f32[32,8,128]{2,1,0:T(8,128)S(1)} all-to-all(f32[32,8,128]{2,1,0:T(8,128)S(1)} %get-tuple-element.30), channel_id=1, replica_groups=mesh['dp'=8,'mp'=4] {'dp','mp'}, dimensions={0} | all-to-all | bytes 262144 | tf_op jit(solution)/shard_map/all_to_all | solution.py:282
  46.5 0.0 copy-done
  46.5 0.0 copy-done.1
  46.5 0.0 copy-done.2
  46.5 2.5 %update.1 = (f32[1,4096]{1,0:T(1,128)}, f32[1,4096]{1,0:T(1,128)}) custom-call(f32[32,8,128]{2,1,0:T(8,128)S(1)} %all_to_all.5.shares, bf16[1280,256]{1,0:T(8,128)(2,1)S(1)} %get-tuple-element.31.group, f32[8]{0:T(128)S(1)} %copy-done.2, f32[1,4096]{1,0:T(1,128)S(1)} %copy-done, f32[1,4096]{1,0:T(1,128)S(1)} %copy-done.1), custom_call_target="tpu_custom_call" | custom-call | tf_op jit(solution)/shard_map/update/pallas_call | solution.py:285
  (1 shorter events, 0.0 us)
Async XLA Ops:
  0.6 10.3 %copy-start.3 = (s32[4]{0:T(128)S(1)}, s32[4]{0:T(128)}, u32[]{:S(2)}) copy-start(s32[4]{0:T(128)} %priv_len.1) | copy-start | bytes 52
  3.8 1.4 %collective-permute-start = (f32[32,640]{1,0:T(8,128)S(1)}, f32[32,640]{1,0:T(8,128)S(1)}, u32[]{:S(2)}, u32[]{:S(2)}) collective-permute-start(f32[32,640]{1,0:T(8,128)S(1)} %get-tuple-element.17), channel_id=1, source_target_pairs={{0,1},{1,0},{2,3},{3,2},{4,5},{5,4},{6,7},{7,6},{8,9},{9,8},{10,11... | collective-permute-start | bytes 245768 | tf_op jit(solution)/shard_map/ppermute | solution.py:215
  5.3 5.7 %collective-permute-start.1 = (f32[32,640]{1,0:T(8,128)S(1)}, f32[32,640]{1,0:T(8,128)S(1)}, u32[]{:S(2)}, u32[]{:S(2)}) collective-permute-start(f32[32,640]{1,0:T(8,128)S(1)} %add.3.own), channel_id=1, source_target_pairs={{0,2},{1,3},{2,0},{3,1},{4,6},{5,7},{6,4},{7,5},{8,10},{9,11},{10,... | collective-permute-start | bytes 245768 | tf_op jit(solution)/shard_map/ppermute | solution.py:215
  11.0 35.5 %copy-start = (f32[1,4096]{1,0:T(1,128)S(1)}, f32[1,4096]{1,0:T(1,128)}, u32[]{:S(2)}) copy-start(f32[1,4096]{1,0:T(1,128)} %down_noise.1) | copy-start | bytes 49156
  11.0 35.5 %copy-start.1 = (f32[1,4096]{1,0:T(1,128)S(1)}, f32[1,4096]{1,0:T(1,128)}, u32[]{:S(2)}) copy-start(f32[1,4096]{1,0:T(1,128)} %up_noise.1) | copy-start | bytes 49156
  11.0 35.5 %copy-start.2 = (f32[8]{0:T(128)S(1)}, f32[8]{0:T(128)}, u32[]{:S(2)}) copy-start(f32[8]{0:T(128)} %noise.1) | copy-start | bytes 100
  12.4 11.5 %collective-permute-start.2 = (bf16[160,256]{1,0:T(8,128)(2,1)S(1)}, bf16[160,256]{1,0:T(8,128)(2,1)S(1)}, u32[]{:S(2)}, u32[]{:S(2)}) collective-permute-start(bf16[160,256]{1,0:T(8,128)(2,1)S(1)} %get-tuple-element.22), channel_id=1, source_target_pairs={{0,16},{4,20},{8,24},{12,28},{16,0},{20,4},{24,8},{28,12},{1,17},{... | collective-permute-start | bytes 245768 | tf_op jit(solution)/shard_map/ppermute | solution.py:215
  15.3 10.9 %collective-permute-start.3 = (bf16[160,256]{1,0:T(8,128)(2,1)S(1)}, bf16[160,256]{1,0:T(8,128)(2,1)S(1)}, u32[]{:S(2)}, u32[]{:S(2)}) collective-permute-start(bf16[160,256]{1,0:T(8,128)(2,1)S(1)} %get-tuple-element.23), channel_id=1, source_target_pairs={{0,24},{4,28},{8,16},{12,20},{16,8},{20,12},{24,0},{28,4},{1,25},{... | collective-permute-start | bytes 245768 | tf_op jit(solution)/shard_map/ppermute | solution.py:215
  16.6 12.7 %collective-permute-start.4 = (bf16[160,256]{1,0:T(8,128)(2,1)S(1)}, bf16[160,256]{1,0:T(8,128)(2,1)S(1)}, u32[]{:S(2)}, u32[]{:S(2)}) collective-permute-start(bf16[160,256]{1,0:T(8,128)(2,1)S(1)} %get-tuple-element.24), channel_id=1, source_target_pairs={{0,20},{4,16},{8,28},{12,24},{16,4},{20,0},{24,12},{28,8},{1,21},{... | collective-permute-start | bytes 245768 | tf_op jit(solution)/shard_map/ppermute | solution.py:215
  19.3 10.1 %collective-permute-start.5 = (bf16[160,256]{1,0:T(8,128)(2,1)S(1)}, bf16[160,256]{1,0:T(8,128)(2,1)S(1)}, u32[]{:S(2)}, u32[]{:S(2)}) collective-permute-start(bf16[160,256]{1,0:T(8,128)(2,1)S(1)} %get-tuple-element.25), channel_id=1, source_target_pairs={{0,28},{4,24},{8,20},{12,16},{16,12},{20,8},{24,4},{28,0},{1,29},{... | collective-permute-start | bytes 245768 | tf_op jit(solution)/shard_map/ppermute | solution.py:215
  20.2 9.2 %collective-permute-start.6 = (bf16[160,256]{1,0:T(8,128)(2,1)S(1)}, bf16[160,256]{1,0:T(8,128)(2,1)S(1)}, u32[]{:S(2)}, u32[]{:S(2)}) collective-permute-start(bf16[160,256]{1,0:T(8,128)(2,1)S(1)} %get-tuple-element.26), channel_id=1, source_target_pairs={{0,8},{4,12},{8,0},{12,4},{16,24},{20,28},{24,16},{28,20},{1,9},{5... | collective-permute-start | bytes 245768 | tf_op jit(solution)/shard_map/ppermute | solution.py:215
  23.9 6.3 %collective-permute-start.7 = (bf16[160,256]{1,0:T(8,128)(2,1)S(1)}, bf16[160,256]{1,0:T(8,128)(2,1)S(1)}, u32[]{:S(2)}, u32[]{:S(2)}) collective-permute-start(bf16[160,256]{1,0:T(8,128)(2,1)S(1)} %get-tuple-element.27), channel_id=1, source_target_pairs={{0,12},{4,8},{8,4},{12,0},{16,28},{20,24},{24,20},{28,16},{1,13},{... | collective-permute-start | bytes 245768 | tf_op jit(solution)/shard_map/ppermute | solution.py:215
  26.2 5.6 %collective-permute-start.8 = (bf16[160,256]{1,0:T(8,128)(2,1)S(1)}, bf16[160,256]{1,0:T(8,128)(2,1)S(1)}, u32[]{:S(2)}, u32[]{:S(2)}) collective-permute-start(bf16[160,256]{1,0:T(8,128)(2,1)S(1)} %get-tuple-element.28), channel_id=1, source_target_pairs={{0,4},{4,0},{8,12},{12,8},{16,20},{20,16},{24,28},{28,24},{1,5},{5... | collective-permute-start | bytes 245768 | tf_op jit(solution)/shard_map/ppermute | solution.py:215

commit v3 on v2

--- a/solution.py
+++ b/solution.py
@@ -265,7 +265,9 @@
         compiler_params=PARAMS,
         name="gradients",
     )(pub_len, priv_len, own, other, *held)
-    order = sorted(range(1, dp), key=lambda k: (-k.bit_length(), k & 1, k)) + [0]
+    ranked = sorted(range(1, dp), key=lambda k: (k & 1, k if k & 1 else -k))
+    far, near = [k for k in ranked if 2 * k >= dp], [k for k in ranked if 2 * k < dp]
+    order = [k for pair in zip(far, near + [0]) for k in pair]
     blocks = [exchange(blocks[k], "dp", k) if k else blocks[k] for k in order]
 
     group, shares = pl.pallas_call(

time: 49.2 us -> 46.4 us (0.943)
  waiting for transfers between devices: 11.2 us -> 8.36 us
  starting transfers between devices: 14.7 us -> 16.5 us
  blocking collectives: 13.2 us -> 11.5 us
    ppermute x9, waiting for transfers between devices: 11.2 us -> 8.36 us  [exchange(): lax.ppermute(x, axis, [(s, s ^ step) for s in range(lax.axis_size(axis))])]
    ppermute x9, starting transfers between devices: 14.7 us -> 16.5 us  [exchange(): lax.ppermute(x, axis, [(s, s ^ step) for s in range(lax.axis_size(axis))])]
    all_to_all x1, blocking collectives: 13.2 us -> 11.5 us  [small_group(): shares = lax.all_to_all(shares, ('dp', 'mp'), 0, 0, tiled=True)]
  transfers between devices with their start and end apart: 9 -> 9, of which waited for: 6 -> 4; matrix products, arithmetic and copies ran while one was open for 0% -> 0% of each run, Pallas kernels for 0% -> 0%
where the time goes in v3:
time: 46.4 us; the launch traced here: 46.3 us
  starting transfers between devices  16.5 us (36%)
  blocking collectives  11.5 us (25%)
  Pallas kernels  8.51 us (18%)
  waiting for transfers between devices  8.36 us (18%)
  between operations  1.34 us (3%)
    ppermute x9, starting transfers between devices, exchange(): lax.ppermute(x, axis, [(s, s ^ step) for s in range(lax.axis_size(axis))])  16.5 us
    all_to_all x1, blocking collectives, small_group(): shares = lax.all_to_all(shares, ('dp', 'mp'), 0, 0, tiled=True)  11.5 us
    ppermute x9, waiting for transfers between devices, exchange(): lax.ppermute(x, axis, [(s, s ^ step) for s in range(lax.axis_size(axis))])  8.36 us
    pallas_call x1, Pallas kernels, small_group(): pl.pallas_call(project_kernel, out_shape=[jax.ShapeDtypeStruct((2 * rank,...  3.18 us
    pallas_call x1, Pallas kernels, small_group(): pl.pallas_call(functools.partial(update_kernel, gain), out_shape=[jax.Sha...  2.52 us
    pallas_call x1, Pallas kernels, small_group(): pl.pallas_call(functools.partial(gradient_kernel, dp), out_shape=[block]...  1.42 us
    pallas_call x1, Pallas kernels, small_group(): pl.pallas_call(functools.partial(gram_kernel, order, n_pub, n_priv), out_...  1.39 us
  transfers between devices with their start and end apart: 9, of which 4 were waited for; matrix products, arithmetic and copies ran while one was open for 0% of the time, Pallas kernels for 0%

profile of v3, /device:TPU:0, one launch (start us, length us, event | category | flops | bytes accessed | tf_op | source)
XLA Modules:
  0.0 46.3 jit_solution(14873512896731561842)
XLA Ops:
  0.6 0.0 copy-start.3
  0.6 3.2 %project.1 = (f32[32,640]{1,0:T(8,128)S(1)}, bf16[1,112,2048]{2,1,0:T(8,128)(2,1)S(1)}, bf16[1,112,2048]{2,1,0:T(8,128)(2,1)S(1)}, bf16[4,112,2048]{2,1,0:T(8,128)(2,1)S(1)}, bf16[4,112,2048]{2,1,0:T(8,128)(2,1)S(1)}) custom-call(bf16[1,112,2048]{2,1,0:T(8,128)(2,1)} %pub_in.1, bf16[1,112,2048]{2,1,0:T(8,128)(2,1)} %pub_out.1, ...), custom_call_target="tpu_custom_call" | custom-call | tf_op jit(solution)/shard_map/project/pallas_call | solution.py:229
  3.8 0.5 %collective-permute-start = (f32[32,640]{1,0:T(8,128)S(1)}, f32[32,640]{1,0:T(8,128)S(1)}, u32[]{:S(2)}, u32[]{:S(2)}) collective-permute-start(f32[32,640]{1,0:T(8,128)S(1)} %get-tuple-element.17), channel_id=1, source_target_pairs={{0,1},{1,0},{2,3},{3,2},{4,5},{5,4},{6,7},{7,6},{8,9},{9,8},{10,11... | collective-permute-start | bytes 245768 | tf_op jit(solution)/shard_map/ppermute | solution.py:215
  4.3 0.9 %collective-permute-done = f32[32,640]{1,0:T(8,128)S(1)} collective-permute-done((f32[32,640]{1,0:T(8,128)S(1)}, f32[32,640]{1,0:T(8,128)S(1)}, u32[]{:S(2)}, u32[]{:S(2)}) %collective-permute-start) | collective-permute-done | bytes 81952 | tf_op jit(solution)/shard_map/ppermute | solution.py:215
  5.3 2.9 %collective-permute-start.1 = (f32[32,640]{1,0:T(8,128)S(1)}, f32[32,640]{1,0:T(8,128)S(1)}, u32[]{:S(2)}, u32[]{:S(2)}) collective-permute-start(f32[32,640]{1,0:T(8,128)S(1)} %add.3.own), channel_id=1, source_target_pairs={{0,2},{1,3},{2,0},{3,1},{4,6},{5,7},{6,4},{7,5},{8,10},{9,11},{10,... | collective-permute-start | bytes 245768 | tf_op jit(solution)/shard_map/ppermute | solution.py:215
  8.8 2.1 %collective-permute-done.1.other = f32[32,640]{1,0:T(8,128)S(1)} collective-permute-done((f32[32,640]{1,0:T(8,128)S(1)}, f32[32,640]{1,0:T(8,128)S(1)}, u32[]{:S(2)}, u32[]{:S(2)}) %collective-permute-start.1) | collective-permute-done | bytes 81952 | tf_op jit(solution)/shard_map/ppermute | solution.py:215
  11.0 0.0 copy-done.3
  11.0 0.0 copy-start
  11.0 0.0 copy-start.1
  11.0 0.0 copy-start.2
  11.0 1.4 %gradients.1 = (bf16[160,256]{1,0:T(8,128)(2,1)S(1)}, bf16[160,256]{1,0:T(8,128)(2,1)S(1)}, bf16[160,256]{1,0:T(8,128)(2,1)S(1)}, bf16[160,256]{1,0:T(8,128)(2,1...) custom-call(s32[1]{0:T(128)S(6)} %copy.13.pub_len, ...), custom_call_target="tpu_custom_call" | custom-call | tf_op jit(solution)/shard_map/gradients/pallas_call | solution.py:256
  12.4 3.9 %collective-permute-start.2 = (bf16[160,256]{1,0:T(8,128)(2,1)S(1)}, bf16[160,256]{1,0:T(8,128)(2,1)S(1)}, u32[]{:S(2)}, u32[]{:S(2)}) collective-permute-start(bf16[160,256]{1,0:T(8,128)(2,1)S(1)} %get-tuple-element.22), channel_id=1, source_target_pairs={{0,24},{4,28},{8,16},{12,20},{16,8},{20,12},{24,0},{28,4},{1,25},{... | collective-permute-start | bytes 245768 | tf_op jit(solution)/shard_map/ppermute | solution.py:215
  16.3 0.0 collective-permute-start.3
  16.3 0.6 %collective-permute-start.4 = (bf16[160,256]{1,0:T(8,128)(2,1)S(1)}, bf16[160,256]{1,0:T(8,128)(2,1)S(1)}, u32[]{:S(2)}, u32[]{:S(2)}) collective-permute-start(bf16[160,256]{1,0:T(8,128)(2,1)S(1)} %get-tuple-element.24), channel_id=1, source_target_pairs={{0,16},{4,20},{8,24},{12,28},{16,0},{20,4},{24,8},{28,12},{1,17},{... | collective-permute-start | bytes 245768 | tf_op jit(solution)/shard_map/ppermute | solution.py:215
  17.0 1.6 %collective-permute-start.5 = (bf16[160,256]{1,0:T(8,128)(2,1)S(1)}, bf16[160,256]{1,0:T(8,128)(2,1)S(1)}, u32[]{:S(2)}, u32[]{:S(2)}) collective-permute-start(bf16[160,256]{1,0:T(8,128)(2,1)S(1)} %get-tuple-element.25), channel_id=1, source_target_pairs={{0,4},{4,0},{8,12},{12,8},{16,20},{20,16},{24,28},{28,24},{1,5},{5... | collective-permute-start | bytes 245768 | tf_op jit(solution)/shard_map/ppermute | solution.py:215
  18.6 2.1 %collective-permute-start.6 = (bf16[160,256]{1,0:T(8,128)(2,1)S(1)}, bf16[160,256]{1,0:T(8,128)(2,1)S(1)}, u32[]{:S(2)}, u32[]{:S(2)}) collective-permute-start(bf16[160,256]{1,0:T(8,128)(2,1)S(1)} %get-tuple-element.26), channel_id=1, source_target_pairs={{0,20},{4,16},{8,28},{12,24},{16,4},{20,0},{24,12},{28,8},{1,21},{... | collective-permute-start | bytes 245768 | tf_op jit(solution)/shard_map/ppermute | solution.py:215
  20.7 0.0 collective-permute-done.2.refs_0_
  20.7 3.0 %collective-permute-start.7 = (bf16[160,256]{1,0:T(8,128)(2,1)S(1)}, bf16[160,256]{1,0:T(8,128)(2,1)S(1)}, u32[]{:S(2)}, u32[]{:S(2)}) collective-permute-start(bf16[160,256]{1,0:T(8,128)(2,1)S(1)} %get-tuple-element.27), channel_id=1, source_target_pairs={{0,12},{4,8},{8,4},{12,0},{16,28},{20,24},{24,20},{28,16},{1,13},{... | collective-permute-start | bytes 245768 | tf_op jit(solution)/shard_map/ppermute | solution.py:215
  23.7 0.0 collective-permute-done.3.refs_1_
  23.7 1.8 %collective-permute-start.8 = (bf16[160,256]{1,0:T(8,128)(2,1)S(1)}, bf16[160,256]{1,0:T(8,128)(2,1)S(1)}, u32[]{:S(2)}, u32[]{:S(2)}) collective-permute-start(bf16[160,256]{1,0:T(8,128)(2,1)S(1)} %get-tuple-element.28), channel_id=1, source_target_pairs={{0,28},{4,24},{8,20},{12,16},{16,12},{20,8},{24,4},{28,0},{1,29},{... | collective-permute-start | bytes 245768 | tf_op jit(solution)/shard_map/ppermute | solution.py:215
  25.5 0.0 collective-permute-done.4.refs_2_
  25.5 0.0 collective-permute-done.5.refs_3_
  25.5 3.4 %collective-permute-done.6.refs_4_ = bf16[160,256]{1,0:T(8,128)(2,1)S(1)} collective-permute-done((bf16[160,256]{1,0:T(8,128)(2,1)S(1)}, bf16[160,256]{1,0:T(8,128)(2,1)S(1)}, u32[]{:S(2)}, u32[]{:S(2)}) %collective-permute-start.6) | collective-permute-done | bytes 81952 | tf_op jit(solution)/shard_map/ppermute | solution.py:215
  28.9 0.0 collective-permute-done.7.refs_5_
  28.9 1.9 %collective-permute-done.8.refs_6_ = bf16[160,256]{1,0:T(8,128)(2,1)S(1)} collective-permute-done((bf16[160,256]{1,0:T(8,128)(2,1)S(1)}, bf16[160,256]{1,0:T(8,128)(2,1)S(1)}, u32[]{:S(2)}, u32[]{:S(2)}) %collective-permute-start.8) | collective-permute-done | bytes 81952 | tf_op jit(solution)/shard_map/ppermute | solution.py:215
  30.8 1.4 %inner_products.1 = (bf16[1280,256]{1,0:T(8,128)(2,1)S(1)}, f32[32,8,128]{2,1,0:T(8,128)S(1)}) custom-call(bf16[160,256]{1,0:T(8,128)(2,1)S(1)} %collective-permute-done.2.refs_0_, bf16[160,256]{1,0:T(8,128)(2,1)S(1)} %collective-permute-done.3.refs_1_, bf16[160,256]{1,0:T(8,128)(2,1)S(1)} %collective-permute-done.4.refs_2_, ...), custom_call_target="tpu_custom_call" | custom-call | tf_op jit(solution)/shard_map/inner_products/pallas_call | solution.py:273
  32.2 11.5 %all_to_all.5.shares = f32[32,8,128]{2,1,0:T(8,128)S(1)} all-to-all(f32[32,8,128]{2,1,0:T(8,128)S(1)} %get-tuple-element.30), channel_id=1, replica_groups=mesh['dp'=8,'mp'=4] {'dp','mp'}, dimensions={0} | all-to-all | bytes 262144 | tf_op jit(solution)/shard_map/all_to_all | solution.py:284
  43.7 0.0 copy-done
  43.7 0.0 copy-done.1
  43.7 0.0 copy-done.2
  43.7 2.5 %update.1 = (f32[1,4096]{1,0:T(1,128)}, f32[1,4096]{1,0:T(1,128)}) custom-call(f32[32,8,128]{2,1,0:T(8,128)S(1)} %all_to_all.5.shares, bf16[1280,256]{1,0:T(8,128)(2,1)S(1)} %get-tuple-element.31.group, f32[8]{0:T(128)S(1)} %copy-done.2, f32[1,4096]{1,0:T(1,128)S(1)} %copy-done, f32[1,4096]{1,0:T(1,128)S(1)} %copy-done.1), custom_call_target="tpu_custom_call" | custom-call | tf_op jit(solution)/shard_map/update/pallas_call | solution.py:287
  (1 shorter events, 0.0 us)
Async XLA Ops:
  0.6 10.3 %copy-start.3 = (s32[4]{0:T(128)S(1)}, s32[4]{0:T(128)}, u32[]{:S(2)}) copy-start(s32[4]{0:T(128)} %priv_len.1) | copy-start | bytes 52
  3.8 1.4 %collective-permute-start = (f32[32,640]{1,0:T(8,128)S(1)}, f32[32,640]{1,0:T(8,128)S(1)}, u32[]{:S(2)}, u32[]{:S(2)}) collective-permute-start(f32[32,640]{1,0:T(8,128)S(1)} %get-tuple-element.17), channel_id=1, source_target_pairs={{0,1},{1,0},{2,3},{3,2},{4,5},{5,4},{6,7},{7,6},{8,9},{9,8},{10,11... | collective-permute-start | bytes 245768 | tf_op jit(solution)/shard_map/ppermute | solution.py:215
  5.3 5.7 %collective-permute-start.1 = (f32[32,640]{1,0:T(8,128)S(1)}, f32[32,640]{1,0:T(8,128)S(1)}, u32[]{:S(2)}, u32[]{:S(2)}) collective-permute-start(f32[32,640]{1,0:T(8,128)S(1)} %add.3.own), channel_id=1, source_target_pairs={{0,2},{1,3},{2,0},{3,1},{4,6},{5,7},{6,4},{7,5},{8,10},{9,11},{10,... | collective-permute-start | bytes 245768 | tf_op jit(solution)/shard_map/ppermute | solution.py:215
  11.0 32.8 %copy-start = (f32[1,4096]{1,0:T(1,128)S(1)}, f32[1,4096]{1,0:T(1,128)}, u32[]{:S(2)}) copy-start(f32[1,4096]{1,0:T(1,128)} %down_noise.1) | copy-start | bytes 49156
  11.0 32.8 %copy-start.1 = (f32[1,4096]{1,0:T(1,128)S(1)}, f32[1,4096]{1,0:T(1,128)}, u32[]{:S(2)}) copy-start(f32[1,4096]{1,0:T(1,128)} %up_noise.1) | copy-start | bytes 49156
  11.0 32.8 %copy-start.2 = (f32[8]{0:T(128)S(1)}, f32[8]{0:T(128)}, u32[]{:S(2)}) copy-start(f32[8]{0:T(128)} %noise.1) | copy-start | bytes 100
  12.4 8.3 %collective-permute-start.2 = (bf16[160,256]{1,0:T(8,128)(2,1)S(1)}, bf16[160,256]{1,0:T(8,128)(2,1)S(1)}, u32[]{:S(2)}, u32[]{:S(2)}) collective-permute-start(bf16[160,256]{1,0:T(8,128)(2,1)S(1)} %get-tuple-element.22), channel_id=1, source_target_pairs={{0,24},{4,28},{8,16},{12,20},{16,8},{20,12},{24,0},{28,4},{1,25},{... | collective-permute-start | bytes 245768 | tf_op jit(solution)/shard_map/ppermute | solution.py:215
  16.3 7.4 %collective-permute-start.3 = (bf16[160,256]{1,0:T(8,128)(2,1)S(1)}, bf16[160,256]{1,0:T(8,128)(2,1)S(1)}, u32[]{:S(2)}, u32[]{:S(2)}) collective-permute-start(bf16[160,256]{1,0:T(8,128)(2,1)S(1)} %get-tuple-element.23), channel_id=1, source_target_pairs={{0,8},{4,12},{8,0},{12,4},{16,24},{20,28},{24,16},{28,20},{1,9},{5... | collective-permute-start | bytes 245768 | tf_op jit(solution)/shard_map/ppermute | solution.py:215
  16.3 9.2 %collective-permute-start.4 = (bf16[160,256]{1,0:T(8,128)(2,1)S(1)}, bf16[160,256]{1,0:T(8,128)(2,1)S(1)}, u32[]{:S(2)}, u32[]{:S(2)}) collective-permute-start(bf16[160,256]{1,0:T(8,128)(2,1)S(1)} %get-tuple-element.24), channel_id=1, source_target_pairs={{0,16},{4,20},{8,24},{12,28},{16,0},{20,4},{24,8},{28,12},{1,17},{... | collective-permute-start | bytes 245768 | tf_op jit(solution)/shard_map/ppermute | solution.py:215
  17.0 8.6 %collective-permute-start.5 = (bf16[160,256]{1,0:T(8,128)(2,1)S(1)}, bf16[160,256]{1,0:T(8,128)(2,1)S(1)}, u32[]{:S(2)}, u32[]{:S(2)}) collective-permute-start(bf16[160,256]{1,0:T(8,128)(2,1)S(1)} %get-tuple-element.25), channel_id=1, source_target_pairs={{0,4},{4,0},{8,12},{12,8},{16,20},{20,16},{24,28},{28,24},{1,5},{5... | collective-permute-start | bytes 245768 | tf_op jit(solution)/shard_map/ppermute | solution.py:215
  18.6 10.3 %collective-permute-start.6 = (bf16[160,256]{1,0:T(8,128)(2,1)S(1)}, bf16[160,256]{1,0:T(8,128)(2,1)S(1)}, u32[]{:S(2)}, u32[]{:S(2)}) collective-permute-start(bf16[160,256]{1,0:T(8,128)(2,1)S(1)} %get-tuple-element.26), channel_id=1, source_target_pairs={{0,20},{4,16},{8,28},{12,24},{16,4},{20,0},{24,12},{28,8},{1,21},{... | collective-permute-start | bytes 245768 | tf_op jit(solution)/shard_map/ppermute | solution.py:215
  20.7 8.2 %collective-permute-start.7 = (bf16[160,256]{1,0:T(8,128)(2,1)S(1)}, bf16[160,256]{1,0:T(8,128)(2,1)S(1)}, u32[]{:S(2)}, u32[]{:S(2)}) collective-permute-start(bf16[160,256]{1,0:T(8,128)(2,1)S(1)} %get-tuple-element.27), channel_id=1, source_target_pairs={{0,12},{4,8},{8,4},{12,0},{16,28},{20,24},{24,20},{28,16},{1,13},{... | collective-permute-start | bytes 245768 | tf_op jit(solution)/shard_map/ppermute | solution.py:215
  23.7 7.1 %collective-permute-start.8 = (bf16[160,256]{1,0:T(8,128)(2,1)S(1)}, bf16[160,256]{1,0:T(8,128)(2,1)S(1)}, u32[]{:S(2)}, u32[]{:S(2)}) collective-permute-start(bf16[160,256]{1,0:T(8,128)(2,1)S(1)} %get-tuple-element.28), channel_id=1, source_target_pairs={{0,28},{4,24},{8,20},{12,16},{16,12},{20,8},{24,4},{28,0},{1,29},{... | collective-permute-start | bytes 245768 | tf_op jit(solution)/shard_map/ppermute | solution.py:215

commit v4 on v3

--- a/solution.py
+++ b/solution.py
@@ -29,6 +29,13 @@
 
 def iota(shape, axis):
     return lax.broadcasted_iota(jnp.int32, shape, axis)
+
+
+def exact_parts(x):
+    high = x.astype(jnp.bfloat16)
+    rest = x - high.astype(jnp.float32)
+    middle = rest.astype(jnp.bfloat16)
+    return [high, middle, (rest - middle.astype(jnp.float32)).astype(jnp.bfloat16)]
 
 
 def project_kernel(pub_in, pub_out, priv_in, priv_out, down_t, up, *rest):
@@ -118,59 +125,78 @@
         group[
             pl.ds(pl.multiple_of(dp * pub_rows + source * priv_rows, priv_rows), priv_rows), :
         ] = block[pub_rows:]
-    publics = dp * n_pub
+    publics, privates = dp * n_pub, dp * n_priv
     span = publics * rows
     lanes = group.shape[1]
     public = group[:span, :]
-    total = jnp.zeros((publics, LANES), jnp.float32)
     same = iota((span, span), 0) % rows == iota((span, span), 1) % rows
-    squares = []
+    parts, squares = [], []
     for c in range(group.shape[0] // span):
         part = group[c * span : (c + 1) * span, :]
         products = jnp.where(same, dot(public, part, BOTH_LAST), 0.0)
-        products = jnp.sum(products.reshape(publics, rows, span), axis=1)
-        pick = (iota((span, LANES), 0) // rows + c * publics == iota((span, LANES), 1)).astype(
-            jnp.float32
-        )
-        total += dot(products, pick, FIRST_LAST, PRECISE)
+        products = jnp.sum(products.reshape(publics, rows // 8, 8, span), axis=1)
+        parts += exact_parts(products.reshape(publics * 8, span))
         if c > 0:
             wide = part.astype(jnp.float32)
             squares.append(jnp.sum((wide * wide).reshape(publics, rows, lanes), axis=1))
+    pick = (iota((span, LANES), 0) // rows == iota((span, LANES), 1)).astype(jnp.bfloat16)
+    sums = dot(jnp.concatenate(parts, axis=0), pick, FIRST_LAST).reshape(-1, 3, publics * 8, LANES)
+    total = jnp.zeros((publics * 8, LANES), jnp.float32)
+    for c in range(sums.shape[0]):
+        total += pltpu.roll(sums[c, 0] + sums[c, 1] + sums[c, 2], c * publics, 1)
+    total = jnp.sum(total.reshape(publics, 8, LANES), axis=1)
+    half, each = LANES // 2, privates // 2
+    squares = jnp.concatenate(squares, axis=0)
+    used = publics + privates
+    gap = jnp.zeros((used, lanes), jnp.float32)
+    rest = jnp.zeros((half - used - each, lanes), jnp.float32)
+    stacked = jnp.concatenate([gap, squares[:each], rest, gap, squares[each:], rest], axis=0)
+    total_squares = dot(jnp.ones((8, lanes), jnp.float32), stacked, BOTH_LAST, PRECISE)
+    short = publics // 2
+    lane = iota((short, LANES), 1)
+    packed = jnp.where(lane < half, total[:short], pltpu.roll(total[short:], half, 1))
+    beside = jnp.logical_and(lane % half >= used, iota((short, LANES), 0) == 0)
+    packed = jnp.where(beside, total_squares[:short], packed)
+    for d in range(out.shape[0]):
+        out[d] = packed
+
+
+def update_kernel(gain, shares, group, noise, down_noise, up_noise, down, up):
+    packed = shares[0]
+    for d in range(1, shares.shape[0]):
+        packed = packed + shares[d]
+    publics = 2 * packed.shape[0]
+    half = LANES // 2
+    rows = 2 * up.shape[1] // group.shape[1]
     examples = group.shape[0] // rows
-    before = LANES // 2 + publics
-    after = LANES // 2 - examples
-    stacked = jnp.concatenate(
-        [jnp.zeros((before, lanes), jnp.float32)]
-        + squares
-        + ([jnp.zeros((after, lanes), jnp.float32)] if after else []),
-        axis=0,
-    )
-    total_squares = dot(jnp.ones((publics, lanes), jnp.float32), stacked, BOTH_LAST, PRECISE)
-    total += jnp.where(iota(total.shape, 0) == 0, total_squares, 0.0)
-    for d in range(out.shape[0]):
-        out[d] = total
-
-
-def update_kernel(gain, shares, group, noise, down_noise, up_noise, down, up):
-    total = shares[0]
-    for d in range(1, shares.shape[0]):
-        total = total + shares[d]
-    publics = total.shape[0]
-    shape = total.shape
-    row, lane = iota(shape, 0), iota(shape, 1)
-    half = LANES // 2
-    squares = pltpu.roll(total, half, 1)[0:1]
+    each = (examples - publics) // 2
+    total = jnp.concatenate([packed, pltpu.roll(packed, half, 1)], axis=0)
+    row, lane = iota(total.shape, 0), iota(total.shape, 1)
+    squares = jnp.where(
+        lane[0:1] < publics + each,
+        pltpu.roll(packed[0:1], LANES - (examples - publics), 1),
+        pltpu.roll(packed[0:1], LANES - (half + each), 1),
+    )
     gram_diagonal = jnp.sum(jnp.where(row == lane, total, 0.0), axis=1, keepdims=True)
     norm_scale = jnp.mean(jnp.sqrt(gram_diagonal), axis=0, keepdims=True)
     coefficient_limit = CLIP_COEF * norm_scale
     residual_limit = CLIP_RESIDUAL * norm_scale
     work = jnp.where(lane < half, total, jnp.where(lane == row + half, 1.0, 0.0))
-    for j in range(publics):
-        inverse = lax.rsqrt(work[j : j + 1, j : j + 1])
-        pivot = work[j : j + 1, :] * inverse
-        column = work[:, j : j + 1] * inverse
-        work = jnp.where(row > j, work - column * pivot, jnp.where(row == j, pivot, work))
-    examples = group.shape[0] * publics // (publics * (2 * up.shape[1] // group.shape[1]))
+    for j in range(0, publics, 2):
+        first = jnp.broadcast_to(work[:, j : j + 1], work.shape)
+        second = jnp.broadcast_to(work[:, j + 1 : j + 2], work.shape)
+        inverse = lax.rsqrt(first[j : j + 1])
+        pivot = work[j : j + 1] * inverse
+        below = first[j + 1 : j + 2] * inverse
+        next_inverse = lax.rsqrt(second[j + 1 : j + 2] - below * below)
+        next_pivot = (work[j + 1 : j + 2] - below * pivot) * next_inverse
+        first = first * inverse
+        second = (second - first * below) * next_inverse
+        work = jnp.where(
+            row > j + 1,
+            work - first * pivot - second * next_pivot,
+            jnp.where(row == j, pivot, jnp.where(row == j + 1, next_pivot, work)),
+        )
     private = jnp.logical_and(lane >= publics, lane < examples)
     coeffs = jnp.where(private, work, 0.0)
     coefficient_squares = jnp.sum(coeffs * coeffs, axis=0, keepdims=True)
@@ -191,7 +217,6 @@
     weights = jnp.where(lane[0:1] < publics, anchor, keep_residual)
 
     lanes = group.shape[1]
-    rows = group.shape[0] // examples
     rank = rows // 2
     acc = jnp.zeros((rows, lanes), jnp.float32)
     for i in range(examples):
@@ -201,8 +226,9 @@
     flat = lanes * rank // LANES
     wide = jnp.concatenate([acc[:rank]] * per, axis=0)
     wide = jnp.where(iota((LANES, lanes), 0) // rank == iota((LANES, lanes), 1) % per, wide, 0.0)
-    pick = (iota((flat, lanes), 0) == iota((flat, lanes), 1) // per).astype(jnp.float32)
-    turned = dot(pick, wide, BOTH_LAST, PRECISE)
+    pick = (iota((flat, lanes), 0) == iota((flat, lanes), 1) // per).astype(jnp.bfloat16)
+    parts = dot(pick, jnp.concatenate(exact_parts(wide), axis=0), BOTH_LAST)
+    turned = parts[:, :LANES] + parts[:, LANES : 2 * LANES] + parts[:, 2 * LANES :]
     for a in range(flat):
         at = slice(a * LANES, (a + 1) * LANES)
         down[0:1, at] = (turned[a : a + 1] + scale * down_noise[0:1, at]) * gain
@@ -274,7 +300,7 @@
         functools.partial(gram_kernel, order, n_pub, n_priv),
         out_shape=[
             jax.ShapeDtypeStruct((dp * examples * 2 * rank, lanes), bf16),
-            jax.ShapeDtypeStruct((dp * mp, dp * n_pub, LANES), f32),
+            jax.ShapeDtypeStruct((dp * mp, dp * n_pub // 2, LANES), f32),
         ],
         in_specs=[VMEM] * dp,
         out_specs=[VMEM] * 2,
@@ -307,7 +333,7 @@
         and width % (dp * LANES) == 0
         and publics == 8
         and priv_in.shape[0] % 8 == 0
-        and publics + priv_in.shape[0] <= LANES // 2
+        and publics + priv_in.shape[0] + priv_in.shape[0] // 2 <= LANES // 2
         and pub_in.shape[1] <= LANES
     )
 

time: 46.4 us -> 44.9 us (0.968)
  blocking collectives: 11.5 us -> 10.7 us
  Pallas kernels: 8.51 us -> 7.79 us
    all_to_all x1, blocking collectives: 11.5 us -> 10.7 us  [small_group(): shares = lax.all_to_all(shares, ('dp', 'mp'), 0, 0, tiled=True)]
where the time goes in v4:
time: 44.9 us; the launch traced here: 44.7 us
  starting transfers between devices  16.5 us (37%)
  blocking collectives  10.7 us (24%)
  waiting for transfers between devices  8.36 us (19%)
  Pallas kernels  7.79 us (17%)
  between operations  1.34 us (3%)
    ppermute x9, starting transfers between devices, exchange(): lax.ppermute(x, axis, [(s, s ^ step) for s in range(lax.axis_size(axis))])  16.5 us
    all_to_all x1, blocking collectives, small_group(): shares = lax.all_to_all(shares, ('dp', 'mp'), 0, 0, tiled=True)  10.7 us
    ppermute x9, waiting for transfers between devices, exchange(): lax.ppermute(x, axis, [(s, s ^ step) for s in range(lax.axis_size(axis))])  8.36 us
    pallas_call x1, Pallas kernels, small_group(): pl.pallas_call(project_kernel, out_shape=[jax.ShapeDtypeStruct((2 * rank,...  3.18 us
    pallas_call x1, Pallas kernels, small_group(): pl.pallas_call(functools.partial(update_kernel, gain), out_shape=[jax.Sha...  2.26 us
    pallas_call x1, Pallas kernels, small_group(): pl.pallas_call(functools.partial(gradient_kernel, dp), out_shape=[block]...  1.42 us
    pallas_call x1, Pallas kernels, small_group(): pl.pallas_call(functools.partial(gram_kernel, order, n_pub, n_priv), out_...  0.93 us
  transfers between devices with their start and end apart: 9, of which 4 were waited for; matrix products, arithmetic and copies ran while one was open for 0% of the time, Pallas kernels for 0%

profile of v4, /device:TPU:0, one launch (start us, length us, event | category | flops | bytes accessed | tf_op | source)
XLA Modules:
  0.0 44.7 jit_solution(14048182305895002438)
XLA Ops:
  0.6 0.0 copy-start.3
  0.6 3.2 %project.1 = (f32[32,640]{1,0:T(8,128)S(1)}, bf16[1,112,2048]{2,1,0:T(8,128)(2,1)S(1)}, bf16[1,112,2048]{2,1,0:T(8,128)(2,1)S(1)}, bf16[4,112,2048]{2,1,0:T(8,128)(2,1)S(1)}, bf16[4,112,2048]{2,1,0:T(8,128)(2,1)S(1)}) custom-call(bf16[1,112,2048]{2,1,0:T(8,128)(2,1)} %pub_in.1, bf16[1,112,2048]{2,1,0:T(8,128)(2,1)} %pub_out.1, ...), custom_call_target="tpu_custom_call" | custom-call | tf_op jit(solution)/shard_map/project/pallas_call | solution.py:255
  3.8 0.5 %collective-permute-start = (f32[32,640]{1,0:T(8,128)S(1)}, f32[32,640]{1,0:T(8,128)S(1)}, u32[]{:S(2)}, u32[]{:S(2)}) collective-permute-start(f32[32,640]{1,0:T(8,128)S(1)} %get-tuple-element.17), channel_id=1, source_target_pairs={{0,1},{1,0},{2,3},{3,2},{4,5},{5,4},{6,7},{7,6},{8,9},{9,8},{10,11... | collective-permute-start | bytes 245768 | tf_op jit(solution)/shard_map/ppermute | solution.py:241
  4.3 0.9 %collective-permute-done = f32[32,640]{1,0:T(8,128)S(1)} collective-permute-done((f32[32,640]{1,0:T(8,128)S(1)}, f32[32,640]{1,0:T(8,128)S(1)}, u32[]{:S(2)}, u32[]{:S(2)}) %collective-permute-start) | collective-permute-done | bytes 81952 | tf_op jit(solution)/shard_map/ppermute | solution.py:241
  5.3 2.9 %collective-permute-start.1 = (f32[32,640]{1,0:T(8,128)S(1)}, f32[32,640]{1,0:T(8,128)S(1)}, u32[]{:S(2)}, u32[]{:S(2)}) collective-permute-start(f32[32,640]{1,0:T(8,128)S(1)} %add.3.own), channel_id=1, source_target_pairs={{0,2},{1,3},{2,0},{3,1},{4,6},{5,7},{6,4},{7,5},{8,10},{9,11},{10,... | collective-permute-start | bytes 245768 | tf_op jit(solution)/shard_map/ppermute | solution.py:241
  8.8 2.1 %collective-permute-done.1.other = f32[32,640]{1,0:T(8,128)S(1)} collective-permute-done((f32[32,640]{1,0:T(8,128)S(1)}, f32[32,640]{1,0:T(8,128)S(1)}, u32[]{:S(2)}, u32[]{:S(2)}) %collective-permute-start.1) | collective-permute-done | bytes 81952 | tf_op jit(solution)/shard_map/ppermute | solution.py:241
  11.0 0.0 copy-done.3
  11.0 0.0 copy-start
  11.0 0.0 copy-start.1
  11.0 0.0 copy-start.2
  11.0 1.4 %gradients.1 = (bf16[160,256]{1,0:T(8,128)(2,1)S(1)}, bf16[160,256]{1,0:T(8,128)(2,1)S(1)}, bf16[160,256]{1,0:T(8,128)(2,1)S(1)}, bf16[160,256]{1,0:T(8,128)(2,1...) custom-call(s32[1]{0:T(128)S(6)} %copy.13.pub_len, ...), custom_call_target="tpu_custom_call" | custom-call | tf_op jit(solution)/shard_map/gradients/pallas_call | solution.py:282
  12.4 3.9 %collective-permute-start.2 = (bf16[160,256]{1,0:T(8,128)(2,1)S(1)}, bf16[160,256]{1,0:T(8,128)(2,1)S(1)}, u32[]{:S(2)}, u32[]{:S(2)}) collective-permute-start(bf16[160,256]{1,0:T(8,128)(2,1)S(1)} %get-tuple-element.22), channel_id=1, source_target_pairs={{0,24},{4,28},{8,16},{12,20},{16,8},{20,12},{24,0},{28,4},{1,25},{... | collective-permute-start | bytes 245768 | tf_op jit(solution)/shard_map/ppermute | solution.py:241
  16.3 0.0 collective-permute-start.3
  16.3 0.6 %collective-permute-start.4 = (bf16[160,256]{1,0:T(8,128)(2,1)S(1)}, bf16[160,256]{1,0:T(8,128)(2,1)S(1)}, u32[]{:S(2)}, u32[]{:S(2)}) collective-permute-start(bf16[160,256]{1,0:T(8,128)(2,1)S(1)} %get-tuple-element.24), channel_id=1, source_target_pairs={{0,16},{4,20},{8,24},{12,28},{16,0},{20,4},{24,8},{28,12},{1,17},{... | collective-permute-start | bytes 245768 | tf_op jit(solution)/shard_map/ppermute | solution.py:241
  17.0 1.6 %collective-permute-start.5 = (bf16[160,256]{1,0:T(8,128)(2,1)S(1)}, bf16[160,256]{1,0:T(8,128)(2,1)S(1)}, u32[]{:S(2)}, u32[]{:S(2)}) collective-permute-start(bf16[160,256]{1,0:T(8,128)(2,1)S(1)} %get-tuple-element.25), channel_id=1, source_target_pairs={{0,4},{4,0},{8,12},{12,8},{16,20},{20,16},{24,28},{28,24},{1,5},{5... | collective-permute-start | bytes 245768 | tf_op jit(solution)/shard_map/ppermute | solution.py:241
  18.6 2.1 %collective-permute-start.6 = (bf16[160,256]{1,0:T(8,128)(2,1)S(1)}, bf16[160,256]{1,0:T(8,128)(2,1)S(1)}, u32[]{:S(2)}, u32[]{:S(2)}) collective-permute-start(bf16[160,256]{1,0:T(8,128)(2,1)S(1)} %get-tuple-element.26), channel_id=1, source_target_pairs={{0,20},{4,16},{8,28},{12,24},{16,4},{20,0},{24,12},{28,8},{1,21},{... | collective-permute-start | bytes 245768 | tf_op jit(solution)/shard_map/ppermute | solution.py:241
  20.7 0.0 collective-permute-done.2.refs_0_
  20.7 3.0 %collective-permute-start.7 = (bf16[160,256]{1,0:T(8,128)(2,1)S(1)}, bf16[160,256]{1,0:T(8,128)(2,1)S(1)}, u32[]{:S(2)}, u32[]{:S(2)}) collective-permute-start(bf16[160,256]{1,0:T(8,128)(2,1)S(1)} %get-tuple-element.27), channel_id=1, source_target_pairs={{0,12},{4,8},{8,4},{12,0},{16,28},{20,24},{24,20},{28,16},{1,13},{... | collective-permute-start | bytes 245768 | tf_op jit(solution)/shard_map/ppermute | solution.py:241
  23.7 0.0 collective-permute-done.3.refs_1_
  23.7 1.8 %collective-permute-start.8 = (bf16[160,256]{1,0:T(8,128)(2,1)S(1)}, bf16[160,256]{1,0:T(8,128)(2,1)S(1)}, u32[]{:S(2)}, u32[]{:S(2)}) collective-permute-start(bf16[160,256]{1,0:T(8,128)(2,1)S(1)} %get-tuple-element.28), channel_id=1, source_target_pairs={{0,28},{4,24},{8,20},{12,16},{16,12},{20,8},{24,4},{28,0},{1,29},{... | collective-permute-start | bytes 245768 | tf_op jit(solution)/shard_map/ppermute | solution.py:241
  25.5 0.0 collective-permute-done.4.refs_2_
  25.5 0.0 collective-permute-done.5.refs_3_
  25.5 3.4 %collective-permute-done.6.refs_4_ = bf16[160,256]{1,0:T(8,128)(2,1)S(1)} collective-permute-done((bf16[160,256]{1,0:T(8,128)(2,1)S(1)}, bf16[160,256]{1,0:T(8,128)(2,1)S(1)}, u32[]{:S(2)}, u32[]{:S(2)}) %collective-permute-start.6) | collective-permute-done | bytes 81952 | tf_op jit(solution)/shard_map/ppermute | solution.py:241
  28.9 0.0 collective-permute-done.7.refs_5_
  28.9 1.9 %collective-permute-done.8.refs_6_ = bf16[160,256]{1,0:T(8,128)(2,1)S(1)} collective-permute-done((bf16[160,256]{1,0:T(8,128)(2,1)S(1)}, bf16[160,256]{1,0:T(8,128)(2,1)S(1)}, u32[]{:S(2)}, u32[]{:S(2)}) %collective-permute-start.8) | collective-permute-done | bytes 81952 | tf_op jit(solution)/shard_map/ppermute | solution.py:241
  30.8 0.9 %inner_products.1 = (bf16[1280,256]{1,0:T(8,128)(2,1)S(1)}, f32[32,4,128]{2,1,0:T(4,128)S(1)}) custom-call(bf16[160,256]{1,0:T(8,128)(2,1)S(1)} %collective-permute-done.2.refs_0_, bf16[160,256]{1,0:T(8,128)(2,1)S(1)} %collective-permute-done.3.refs_1_, bf16[160,256]{1,0:T(8,128)(2,1)S(1)} %collective-permute-done.4.refs_2_, ...), custom_call_target="tpu_custom_call" | custom-call | tf_op jit(solution)/shard_map/inner_products/pallas_call | solution.py:299
  31.8 10.7 %all_to_all.5.shares = f32[32,4,128]{2,1,0:T(4,128)S(1)} all-to-all(f32[32,4,128]{2,1,0:T(4,128)S(1)} %get-tuple-element.30), channel_id=1, replica_groups=mesh['dp'=8,'mp'=4] {'dp','mp'}, dimensions={0} | all-to-all | bytes 131072 | tf_op jit(solution)/shard_map/all_to_all | solution.py:310
  42.5 0.0 copy-done
  42.5 0.0 copy-done.1
  42.5 0.0 copy-done.2
  42.5 2.3 %update.1 = (f32[1,4096]{1,0:T(1,128)}, f32[1,4096]{1,0:T(1,128)}) custom-call(f32[32,4,128]{2,1,0:T(4,128)S(1)} %all_to_all.5.shares, bf16[1280,256]{1,0:T(8,128)(2,1)S(1)} %get-tuple-element.31.group, f32[8]{0:T(128)S(1)} %copy-done.2, f32[1,4096]{1,0:T(1,128)S(1)} %copy-done, f32[1,4096]{1,0:T(1,128)S(1)} %copy-done.1), custom_call_target="tpu_custom_call" | custom-call | tf_op jit(solution)/shard_map/update/pallas_call | solution.py:313
  (1 shorter events, 0.0 us)
Async XLA Ops:
  0.6 10.3 %copy-start.3 = (s32[4]{0:T(128)S(1)}, s32[4]{0:T(128)}, u32[]{:S(2)}) copy-start(s32[4]{0:T(128)} %priv_len.1) | copy-start | bytes 52
  3.8 1.4 %collective-permute-start = (f32[32,640]{1,0:T(8,128)S(1)}, f32[32,640]{1,0:T(8,128)S(1)}, u32[]{:S(2)}, u32[]{:S(2)}) collective-permute-start(f32[32,640]{1,0:T(8,128)S(1)} %get-tuple-element.17), channel_id=1, source_target_pairs={{0,1},{1,0},{2,3},{3,2},{4,5},{5,4},{6,7},{7,6},{8,9},{9,8},{10,11... | collective-permute-start | bytes 245768 | tf_op jit(solution)/shard_map/ppermute | solution.py:241
  5.3 5.7 %collective-permute-start.1 = (f32[32,640]{1,0:T(8,128)S(1)}, f32[32,640]{1,0:T(8,128)S(1)}, u32[]{:S(2)}, u32[]{:S(2)}) collective-permute-start(f32[32,640]{1,0:T(8,128)S(1)} %add.3.own), channel_id=1, source_target_pairs={{0,2},{1,3},{2,0},{3,1},{4,6},{5,7},{6,4},{7,5},{8,10},{9,11},{10,... | collective-permute-start | bytes 245768 | tf_op jit(solution)/shard_map/ppermute | solution.py:241
  11.0 31.5 %copy-start = (f32[1,4096]{1,0:T(1,128)S(1)}, f32[1,4096]{1,0:T(1,128)}, u32[]{:S(2)}) copy-start(f32[1,4096]{1,0:T(1,128)} %down_noise.1) | copy-start | bytes 49156
  11.0 31.5 %copy-start.1 = (f32[1,4096]{1,0:T(1,128)S(1)}, f32[1,4096]{1,0:T(1,128)}, u32[]{:S(2)}) copy-start(f32[1,4096]{1,0:T(1,128)} %up_noise.1) | copy-start | bytes 49156
  11.0 31.5 %copy-start.2 = (f32[8]{0:T(128)S(1)}, f32[8]{0:T(128)}, u32[]{:S(2)}) copy-start(f32[8]{0:T(128)} %noise.1) | copy-start | bytes 100
  12.4 8.3 %collective-permute-start.2 = (bf16[160,256]{1,0:T(8,128)(2,1)S(1)}, bf16[160,256]{1,0:T(8,128)(2,1)S(1)}, u32[]{:S(2)}, u32[]{:S(2)}) collective-permute-start(bf16[160,256]{1,0:T(8,128)(2,1)S(1)} %get-tuple-element.22), channel_id=1, source_target_pairs={{0,24},{4,28},{8,16},{12,20},{16,8},{20,12},{24,0},{28,4},{1,25},{... | collective-permute-start | bytes 245768 | tf_op jit(solution)/shard_map/ppermute | solution.py:241
  16.3 7.4 %collective-permute-start.3 = (bf16[160,256]{1,0:T(8,128)(2,1)S(1)}, bf16[160,256]{1,0:T(8,128)(2,1)S(1)}, u32[]{:S(2)}, u32[]{:S(2)}) collective-permute-start(bf16[160,256]{1,0:T(8,128)(2,1)S(1)} %get-tuple-element.23), channel_id=1, source_target_pairs={{0,8},{4,12},{8,0},{12,4},{16,24},{20,28},{24,16},{28,20},{1,9},{5... | collective-permute-start | bytes 245768 | tf_op jit(solution)/shard_map/ppermute | solution.py:241
  16.3 9.2 %collective-permute-start.4 = (bf16[160,256]{1,0:T(8,128)(2,1)S(1)}, bf16[160,256]{1,0:T(8,128)(2,1)S(1)}, u32[]{:S(2)}, u32[]{:S(2)}) collective-permute-start(bf16[160,256]{1,0:T(8,128)(2,1)S(1)} %get-tuple-element.24), channel_id=1, source_target_pairs={{0,16},{4,20},{8,24},{12,28},{16,0},{20,4},{24,8},{28,12},{1,17},{... | collective-permute-start | bytes 245768 | tf_op jit(solution)/shard_map/ppermute | solution.py:241
  17.0 8.6 %collective-permute-start.5 = (bf16[160,256]{1,0:T(8,128)(2,1)S(1)}, bf16[160,256]{1,0:T(8,128)(2,1)S(1)}, u32[]{:S(2)}, u32[]{:S(2)}) collective-permute-start(bf16[160,256]{1,0:T(8,128)(2,1)S(1)} %get-tuple-element.25), channel_id=1, source_target_pairs={{0,4},{4,0},{8,12},{12,8},{16,20},{20,16},{24,28},{28,24},{1,5},{5... | collective-permute-start | bytes 245768 | tf_op jit(solution)/shard_map/ppermute | solution.py:241
  18.6 10.3 %collective-permute-start.6 = (bf16[160,256]{1,0:T(8,128)(2,1)S(1)}, bf16[160,256]{1,0:T(8,128)(2,1)S(1)}, u32[]{:S(2)}, u32[]{:S(2)}) collective-permute-start(bf16[160,256]{1,0:T(8,128)(2,1)S(1)} %get-tuple-element.26), channel_id=1, source_target_pairs={{0,20},{4,16},{8,28},{12,24},{16,4},{20,0},{24,12},{28,8},{1,21},{... | collective-permute-start | bytes 245768 | tf_op jit(solution)/shard_map/ppermute | solution.py:241
  20.7 8.2 %collective-permute-start.7 = (bf16[160,256]{1,0:T(8,128)(2,1)S(1)}, bf16[160,256]{1,0:T(8,128)(2,1)S(1)}, u32[]{:S(2)}, u32[]{:S(2)}) collective-permute-start(bf16[160,256]{1,0:T(8,128)(2,1)S(1)} %get-tuple-element.27), channel_id=1, source_target_pairs={{0,12},{4,8},{8,4},{12,0},{16,28},{20,24},{24,20},{28,16},{1,13},{... | collective-permute-start | bytes 245768 | tf_op jit(solution)/shard_map/ppermute | solution.py:241
  23.7 7.1 %collective-permute-start.8 = (bf16[160,256]{1,0:T(8,128)(2,1)S(1)}, bf16[160,256]{1,0:T(8,128)(2,1)S(1)}, u32[]{:S(2)}, u32[]{:S(2)}) collective-permute-start(bf16[160,256]{1,0:T(8,128)(2,1)S(1)} %get-tuple-element.28), channel_id=1, source_target_pairs={{0,28},{4,24},{8,20},{12,16},{16,12},{20,8},{24,4},{28,0},{1,29},{... | collective-permute-start | bytes 245768 | tf_op jit(solution)/shard_map/ppermute | solution.py:241

commit v5 on v4

--- a/solution.py
+++ b/solution.py
@@ -89,27 +89,30 @@
             both = own[:, at] + other[:, at]
             live = iota(both.shape, 1) < lengths[e]
             both = jnp.where(live, both, 0.0).astype(jnp.bfloat16)
+            down_whole = dot(both[rank:], inputs[e], FIRST_LAST)
+            up_whole = dot(both[:rank], cotangents[e], FIRST_LAST)
             for c in range(dp):
                 features = slice(c * lanes, (c + 1) * lanes)
                 at = slice(c * rank, (c + 1) * rank)
-                down_part = dot(both[rank:], inputs[e, :, features], FIRST_LAST)
-                up_part = dot(both[:rank], cotangents[e, :, features], FIRST_LAST)
+                down_part = down_whole[:, features]
+                up_part = up_whole[:, features]
                 down_rows[at, :] = down_part.astype(jnp.bfloat16)
                 for h in range(lanes // LANES):
                     up_rows[h, at, :] = up_part[:, h * LANES : (h + 1) * LANES]
             for k in range(dp):
                 to = me ^ k
-                row = slot * 2 * rank
-                blocks[k][row : row + rank, :] = down_rows[
+                rows = slice(slot * rank, (slot + 1) * rank)
+                blocks[k][rows, :lanes] = down_rows[
                     pl.ds(pl.multiple_of(to * rank, rank), rank), :
                 ]
                 for h in range(lanes // LANES):
                     pieces = [
                         up_rows[h, pl.ds(to * per + r, dp, stride=rank), :] for r in range(per)
                     ]
-                    blocks[k][row + rank : row + 2 * rank, h * LANES : (h + 1) * LANES] = (
-                        jnp.concatenate(pieces, axis=0).astype(jnp.bfloat16)
-                    )
+                    start = lanes + h * LANES
+                    blocks[k][rows, start : start + LANES] = jnp.concatenate(
+                        pieces, axis=0
+                    ).astype(jnp.bfloat16)
             slot += 1
 
 
@@ -216,15 +219,14 @@
     anchor = pltpu.roll(jnp.sum(inverse_factor * target, axis=0, keepdims=True), half, 1)
     weights = jnp.where(lane[0:1] < publics, anchor, keep_residual)
 
-    lanes = group.shape[1]
-    rank = rows // 2
-    acc = jnp.zeros((rows, lanes), jnp.float32)
+    rank, lanes = rows, group.shape[1] // 2
+    acc = jnp.zeros((rows, 2 * lanes), jnp.float32)
     for i in range(examples):
         acc = acc + weights[:, i : i + 1] * group[i * rows : (i + 1) * rows, :].astype(jnp.float32)
     scale = SIGMA_RESIDUAL * residual_limit
     per = LANES // rank
     flat = lanes * rank // LANES
-    wide = jnp.concatenate([acc[:rank]] * per, axis=0)
+    wide = jnp.concatenate([acc[:, :lanes]] * per, axis=0)
     wide = jnp.where(iota((LANES, lanes), 0) // rank == iota((LANES, lanes), 1) % per, wide, 0.0)
     pick = (iota((flat, lanes), 0) == iota((flat, lanes), 1) // per).astype(jnp.bfloat16)
     parts = dot(pick, jnp.concatenate(exact_parts(wide), axis=0), BOTH_LAST)
@@ -234,7 +236,7 @@
         down[0:1, at] = (turned[a : a + 1] + scale * down_noise[0:1, at]) * gain
     for a in range(rank):
         at = slice(a * lanes, (a + 1) * lanes)
-        up[0:1, at] = (acc[rank + a : rank + a + 1] + scale * up_noise[0:1, at]) * gain
+        up[0:1, at] = (acc[a : a + 1, lanes:] + scale * up_noise[0:1, at]) * gain
 
 
 def exchange(x, axis, step):
@@ -278,7 +280,7 @@
         if step < mp:
             own = own + other
 
-    block = jax.ShapeDtypeStruct((examples * 2 * rank, lanes), bf16)
+    block = jax.ShapeDtypeStruct((examples * rank, 2 * lanes), bf16)
     blocks = pl.pallas_call(
         functools.partial(gradient_kernel, dp),
         out_shape=[block] * dp,
@@ -299,7 +301,7 @@
     group, shares = pl.pallas_call(
         functools.partial(gram_kernel, order, n_pub, n_priv),
         out_shape=[
-            jax.ShapeDtypeStruct((dp * examples * 2 * rank, lanes), bf16),
+            jax.ShapeDtypeStruct((dp * examples * rank, 2 * lanes), bf16),
             jax.ShapeDtypeStruct((dp * mp, dp * n_pub // 2, LANES), f32),
         ],
         in_specs=[VMEM] * dp,

time: 44.9 us -> 44.7 us (level)
  no operation moved by 1% of the time
where the time goes in v5:
time: 44.7 us; the launch traced here: 44.6 us
  starting transfers between devices  16.5 us (37%)
  blocking collectives  10.7 us (24%)
  waiting for transfers between devices  8.35 us (19%)
  Pallas kernels  7.64 us (17%)
  between operations  1.34 us (3%)
    ppermute x9, starting transfers between devices, exchange(): lax.ppermute(x, axis, [(s, s ^ step) for s in range(lax.axis_size(axis))])  16.5 us
    all_to_all x1, blocking collectives, small_group(): shares = lax.all_to_all(shares, ('dp', 'mp'), 0, 0, tiled=True)  10.7 us
    ppermute x9, waiting for transfers between devices, exchange(): lax.ppermute(x, axis, [(s, s ^ step) for s in range(lax.axis_size(axis))])  8.35 us
    pallas_call x1, Pallas kernels, small_group(): pl.pallas_call(project_kernel, out_shape=[jax.ShapeDtypeStruct((2 * rank,...  3.18 us
    pallas_call x1, Pallas kernels, small_group(): pl.pallas_call(functools.partial(update_kernel, gain), out_shape=[jax.Sha...  2.26 us
    pallas_call x1, Pallas kernels, small_group(): pl.pallas_call(functools.partial(gradient_kernel, dp), out_shape=[block]...  1.34 us
  transfers between devices with their start and end apart: 9, of which 4 were waited for; matrix products, arithmetic and copies ran while one was open for 0% of the time, Pallas kernels for 0%

profile of v5, /device:TPU:0, one launch (start us, length us, event | category | flops | bytes accessed | tf_op | source)
XLA Modules:
  0.0 44.6 jit_solution(6360924127530465889)
XLA Ops:
  0.6 0.0 copy-start.3
  0.6 3.2 %project.1 = (f32[32,640]{1,0:T(8,128)S(1)}, bf16[1,112,2048]{2,1,0:T(8,128)(2,1)S(1)}, bf16[1,112,2048]{2,1,0:T(8,128)(2,1)S(1)}, bf16[4,112,2048]{2,1,0:T(8,128)(2,1)S(1)}, bf16[4,112,2048]{2,1,0:T(8,128)(2,1)S(1)}) custom-call(bf16[1,112,2048]{2,1,0:T(8,128)(2,1)} %pub_in.1, bf16[1,112,2048]{2,1,0:T(8,128)(2,1)} %pub_out.1, ...), custom_call_target="tpu_custom_call" | custom-call | tf_op jit(solution)/shard_map/project/pallas_call | solution.py:257
  3.8 0.5 %collective-permute-start = (f32[32,640]{1,0:T(8,128)S(1)}, f32[32,640]{1,0:T(8,128)S(1)}, u32[]{:S(2)}, u32[]{:S(2)}) collective-permute-start(f32[32,640]{1,0:T(8,128)S(1)} %get-tuple-element.17), channel_id=1, source_target_pairs={{0,1},{1,0},{2,3},{3,2},{4,5},{5,4},{6,7},{7,6},{8,9},{9,8},{10,11... | collective-permute-start | bytes 245768 | tf_op jit(solution)/shard_map/ppermute | solution.py:243
  4.3 0.9 %collective-permute-done = f32[32,640]{1,0:T(8,128)S(1)} collective-permute-done((f32[32,640]{1,0:T(8,128)S(1)}, f32[32,640]{1,0:T(8,128)S(1)}, u32[]{:S(2)}, u32[]{:S(2)}) %collective-permute-start) | collective-permute-done | bytes 81952 | tf_op jit(solution)/shard_map/ppermute | solution.py:243
  5.3 2.9 %collective-permute-start.1 = (f32[32,640]{1,0:T(8,128)S(1)}, f32[32,640]{1,0:T(8,128)S(1)}, u32[]{:S(2)}, u32[]{:S(2)}) collective-permute-start(f32[32,640]{1,0:T(8,128)S(1)} %add.3.own), channel_id=1, source_target_pairs={{0,2},{1,3},{2,0},{3,1},{4,6},{5,7},{6,4},{7,5},{8,10},{9,11},{10,... | collective-permute-start | bytes 245768 | tf_op jit(solution)/shard_map/ppermute | solution.py:243
  8.8 2.1 %collective-permute-done.1.other = f32[32,640]{1,0:T(8,128)S(1)} collective-permute-done((f32[32,640]{1,0:T(8,128)S(1)}, f32[32,640]{1,0:T(8,128)S(1)}, u32[]{:S(2)}, u32[]{:S(2)}) %collective-permute-start.1) | collective-permute-done | bytes 81952 | tf_op jit(solution)/shard_map/ppermute | solution.py:243
  11.0 0.0 copy-done.3
  11.0 0.0 copy-start
  11.0 0.0 copy-start.1
  11.0 0.0 copy-start.2
  11.0 1.3 %gradients.1 = (bf16[80,512]{1,0:T(8,128)(2,1)S(1)}, bf16[80,512]{1,0:T(8,128)(2,1)S(1)}, bf16[80,512]{1,0:T(8,128)(2,1)S(1)}, bf16[80,512]{1,0:T(8,128)(2,1)S(1...) custom-call(s32[1]{0:T(128)S(6)} %copy.13.pub_len, ...), custom_call_target="tpu_custom_call" | custom-call | tf_op jit(solution)/shard_map/gradients/pallas_call | solution.py:284
  12.3 3.9 %collective-permute-start.2 = (bf16[80,512]{1,0:T(8,128)(2,1)S(1)}, bf16[80,512]{1,0:T(8,128)(2,1)S(1)}, u32[]{:S(2)}, u32[]{:S(2)}) collective-permute-start(bf16[80,512]{1,0:T(8,128)(2,1)S(1)} %get-tuple-element.22), channel_id=1, source_target_pairs={{0,24},{4,28},{8,16},{12,20},{16,8},{20,12},{24,0},{28,4},{1,25},{... | collective-permute-start | bytes 245768 | tf_op jit(solution)/shard_map/ppermute | solution.py:243
  16.2 0.0 collective-permute-start.3
  16.2 0.6 %collective-permute-start.4 = (bf16[80,512]{1,0:T(8,128)(2,1)S(1)}, bf16[80,512]{1,0:T(8,128)(2,1)S(1)}, u32[]{:S(2)}, u32[]{:S(2)}) collective-permute-start(bf16[80,512]{1,0:T(8,128)(2,1)S(1)} %get-tuple-element.24), channel_id=1, source_target_pairs={{0,16},{4,20},{8,24},{12,28},{16,0},{20,4},{24,8},{28,12},{1,17},{... | collective-permute-start | bytes 245768 | tf_op jit(solution)/shard_map/ppermute | solution.py:243
  16.9 1.7 %collective-permute-start.5 = (bf16[80,512]{1,0:T(8,128)(2,1)S(1)}, bf16[80,512]{1,0:T(8,128)(2,1)S(1)}, u32[]{:S(2)}, u32[]{:S(2)}) collective-permute-start(bf16[80,512]{1,0:T(8,128)(2,1)S(1)} %get-tuple-element.25), channel_id=1, source_target_pairs={{0,4},{4,0},{8,12},{12,8},{16,20},{20,16},{24,28},{28,24},{1,5},{5... | collective-permute-start | bytes 245768 | tf_op jit(solution)/shard_map/ppermute | solution.py:243
  18.5 2.1 %collective-permute-start.6 = (bf16[80,512]{1,0:T(8,128)(2,1)S(1)}, bf16[80,512]{1,0:T(8,128)(2,1)S(1)}, u32[]{:S(2)}, u32[]{:S(2)}) collective-permute-start(bf16[80,512]{1,0:T(8,128)(2,1)S(1)} %get-tuple-element.26), channel_id=1, source_target_pairs={{0,20},{4,16},{8,28},{12,24},{16,4},{20,0},{24,12},{28,8},{1,21},{... | collective-permute-start | bytes 245768 | tf_op jit(solution)/shard_map/ppermute | solution.py:243
  20.6 0.0 collective-permute-done.2.refs_0_
  20.6 3.0 %collective-permute-start.7 = (bf16[80,512]{1,0:T(8,128)(2,1)S(1)}, bf16[80,512]{1,0:T(8,128)(2,1)S(1)}, u32[]{:S(2)}, u32[]{:S(2)}) collective-permute-start(bf16[80,512]{1,0:T(8,128)(2,1)S(1)} %get-tuple-element.27), channel_id=1, source_target_pairs={{0,12},{4,8},{8,4},{12,0},{16,28},{20,24},{24,20},{28,16},{1,13},{... | collective-permute-start | bytes 245768 | tf_op jit(solution)/shard_map/ppermute | solution.py:243
  23.6 0.0 collective-permute-done.3.refs_1_
  23.6 1.8 %collective-permute-start.8 = (bf16[80,512]{1,0:T(8,128)(2,1)S(1)}, bf16[80,512]{1,0:T(8,128)(2,1)S(1)}, u32[]{:S(2)}, u32[]{:S(2)}) collective-permute-start(bf16[80,512]{1,0:T(8,128)(2,1)S(1)} %get-tuple-element.28), channel_id=1, source_target_pairs={{0,28},{4,24},{8,20},{12,16},{16,12},{20,8},{24,4},{28,0},{1,29},{... | collective-permute-start | bytes 245768 | tf_op jit(solution)/shard_map/ppermute | solution.py:243
  25.4 0.0 collective-permute-done.4.refs_2_
  25.4 0.0 collective-permute-done.5.refs_3_
  25.4 3.4 %collective-permute-done.6.refs_4_ = bf16[80,512]{1,0:T(8,128)(2,1)S(1)} collective-permute-done((bf16[80,512]{1,0:T(8,128)(2,1)S(1)}, bf16[80,512]{1,0:T(8,128)(2,1)S(1)}, u32[]{:S(2)}, u32[]{:S(2)}) %collective-permute-start.6) | collective-permute-done | bytes 81952 | tf_op jit(solution)/shard_map/ppermute | solution.py:243
  28.8 0.0 collective-permute-done.7.refs_5_
  28.8 1.9 %collective-permute-done.8.refs_6_ = bf16[80,512]{1,0:T(8,128)(2,1)S(1)} collective-permute-done((bf16[80,512]{1,0:T(8,128)(2,1)S(1)}, bf16[80,512]{1,0:T(8,128)(2,1)S(1)}, u32[]{:S(2)}, u32[]{:S(2)}) %collective-permute-start.8) | collective-permute-done | bytes 81952 | tf_op jit(solution)/shard_map/ppermute | solution.py:243
  30.8 0.9 %inner_products.1 = (bf16[640,512]{1,0:T(8,128)(2,1)S(1)}, f32[32,4,128]{2,1,0:T(4,128)S(1)}) custom-call(bf16[80,512]{1,0:T(8,128)(2,1)S(1)} %collective-permute-done.2.refs_0_, bf16[80,512]{1,0:T(8,128)(2,1)S(1)} %collective-permute-done.3.refs_1_, bf16[80,512]{1,0:T(8,128)(2,1)S(1)} %collective-permute-done.4.refs_2_, ...), custom_call_target="tpu_custom_call" | custom-call | tf_op jit(solution)/shard_map/inner_products/pallas_call | solution.py:301
  31.6 10.7 %all_to_all.5.shares = f32[32,4,128]{2,1,0:T(4,128)S(1)} all-to-all(f32[32,4,128]{2,1,0:T(4,128)S(1)} %get-tuple-element.30), channel_id=1, replica_groups=mesh['dp'=8,'mp'=4] {'dp','mp'}, dimensions={0} | all-to-all | bytes 131072 | tf_op jit(solution)/shard_map/all_to_all | solution.py:312
  42.3 0.0 copy-done
  42.3 0.0 copy-done.1
  42.3 0.0 copy-done.2
  42.3 2.3 %update.1 = (f32[1,4096]{1,0:T(1,128)}, f32[1,4096]{1,0:T(1,128)}) custom-call(f32[32,4,128]{2,1,0:T(4,128)S(1)} %all_to_all.5.shares, bf16[640,512]{1,0:T(8,128)(2,1)S(1)} %get-tuple-element.31.group, f32[8]{0:T(128)S(1)} %copy-done.2, f32[1,4096]{1,0:T(1,128)S(1)} %copy-done, f32[1,4096]{1,0:T(1,128)S(1)} %copy-done.1), custom_call_target="tpu_custom_call" | custom-call | tf_op jit(solution)/shard_map/update/pallas_call | solution.py:315
  (1 shorter events, 0.0 us)
Async XLA Ops:
  0.6 10.3 %copy-start.3 = (s32[4]{0:T(128)S(1)}, s32[4]{0:T(128)}, u32[]{:S(2)}) copy-start(s32[4]{0:T(128)} %priv_len.1) | copy-start | bytes 52
  3.8 1.4 %collective-permute-start = (f32[32,640]{1,0:T(8,128)S(1)}, f32[32,640]{1,0:T(8,128)S(1)}, u32[]{:S(2)}, u32[]{:S(2)}) collective-permute-start(f32[32,640]{1,0:T(8,128)S(1)} %get-tuple-element.17), channel_id=1, source_target_pairs={{0,1},{1,0},{2,3},{3,2},{4,5},{5,4},{6,7},{7,6},{8,9},{9,8},{10,11... | collective-permute-start | bytes 245768 | tf_op jit(solution)/shard_map/ppermute | solution.py:243
  5.3 5.7 %collective-permute-start.1 = (f32[32,640]{1,0:T(8,128)S(1)}, f32[32,640]{1,0:T(8,128)S(1)}, u32[]{:S(2)}, u32[]{:S(2)}) collective-permute-start(f32[32,640]{1,0:T(8,128)S(1)} %add.3.own), channel_id=1, source_target_pairs={{0,2},{1,3},{2,0},{3,1},{4,6},{5,7},{6,4},{7,5},{8,10},{9,11},{10,... | collective-permute-start | bytes 245768 | tf_op jit(solution)/shard_map/ppermute | solution.py:243
  11.0 31.3 %copy-start = (f32[1,4096]{1,0:T(1,128)S(1)}, f32[1,4096]{1,0:T(1,128)}, u32[]{:S(2)}) copy-start(f32[1,4096]{1,0:T(1,128)} %down_noise.1) | copy-start | bytes 49156
  11.0 31.3 %copy-start.1 = (f32[1,4096]{1,0:T(1,128)S(1)}, f32[1,4096]{1,0:T(1,128)}, u32[]{:S(2)}) copy-start(f32[1,4096]{1,0:T(1,128)} %up_noise.1) | copy-start | bytes 49156
  11.0 31.3 %copy-start.2 = (f32[8]{0:T(128)S(1)}, f32[8]{0:T(128)}, u32[]{:S(2)}) copy-start(f32[8]{0:T(128)} %noise.1) | copy-start | bytes 100
  12.3 8.3 %collective-permute-start.2 = (bf16[80,512]{1,0:T(8,128)(2,1)S(1)}, bf16[80,512]{1,0:T(8,128)(2,1)S(1)}, u32[]{:S(2)}, u32[]{:S(2)}) collective-permute-start(bf16[80,512]{1,0:T(8,128)(2,1)S(1)} %get-tuple-element.22), channel_id=1, source_target_pairs={{0,24},{4,28},{8,16},{12,20},{16,8},{20,12},{24,0},{28,4},{1,25},{... | collective-permute-start | bytes 245768 | tf_op jit(solution)/shard_map/ppermute | solution.py:243
  16.2 7.4 %collective-permute-start.3 = (bf16[80,512]{1,0:T(8,128)(2,1)S(1)}, bf16[80,512]{1,0:T(8,128)(2,1)S(1)}, u32[]{:S(2)}, u32[]{:S(2)}) collective-permute-start(bf16[80,512]{1,0:T(8,128)(2,1)S(1)} %get-tuple-element.23), channel_id=1, source_target_pairs={{0,8},{4,12},{8,0},{12,4},{16,24},{20,28},{24,16},{28,20},{1,9},{5... | collective-permute-start | bytes 245768 | tf_op jit(solution)/shard_map/ppermute | solution.py:243
  16.2 9.2 %collective-permute-start.4 = (bf16[80,512]{1,0:T(8,128)(2,1)S(1)}, bf16[80,512]{1,0:T(8,128)(2,1)S(1)}, u32[]{:S(2)}, u32[]{:S(2)}) collective-permute-start(bf16[80,512]{1,0:T(8,128)(2,1)S(1)} %get-tuple-element.24), channel_id=1, source_target_pairs={{0,16},{4,20},{8,24},{12,28},{16,0},{20,4},{24,8},{28,12},{1,17},{... | collective-permute-start | bytes 245768 | tf_op jit(solution)/shard_map/ppermute | solution.py:243
  16.9 8.6 %collective-permute-start.5 = (bf16[80,512]{1,0:T(8,128)(2,1)S(1)}, bf16[80,512]{1,0:T(8,128)(2,1)S(1)}, u32[]{:S(2)}, u32[]{:S(2)}) collective-permute-start(bf16[80,512]{1,0:T(8,128)(2,1)S(1)} %get-tuple-element.25), channel_id=1, source_target_pairs={{0,4},{4,0},{8,12},{12,8},{16,20},{20,16},{24,28},{28,24},{1,5},{5... | collective-permute-start | bytes 245768 | tf_op jit(solution)/shard_map/ppermute | solution.py:243
  18.5 10.3 %collective-permute-start.6 = (bf16[80,512]{1,0:T(8,128)(2,1)S(1)}, bf16[80,512]{1,0:T(8,128)(2,1)S(1)}, u32[]{:S(2)}, u32[]{:S(2)}) collective-permute-start(bf16[80,512]{1,0:T(8,128)(2,1)S(1)} %get-tuple-element.26), channel_id=1, source_target_pairs={{0,20},{4,16},{8,28},{12,24},{16,4},{20,0},{24,12},{28,8},{1,21},{... | collective-permute-start | bytes 245768 | tf_op jit(solution)/shard_map/ppermute | solution.py:243
  20.6 8.2 %collective-permute-start.7 = (bf16[80,512]{1,0:T(8,128)(2,1)S(1)}, bf16[80,512]{1,0:T(8,128)(2,1)S(1)}, u32[]{:S(2)}, u32[]{:S(2)}) collective-permute-start(bf16[80,512]{1,0:T(8,128)(2,1)S(1)} %get-tuple-element.27), channel_id=1, source_target_pairs={{0,12},{4,8},{8,4},{12,0},{16,28},{20,24},{24,20},{28,16},{1,13},{... | collective-permute-start | bytes 245768 | tf_op jit(solution)/shard_map/ppermute | solution.py:243
  23.6 7.1 %collective-permute-start.8 = (bf16[80,512]{1,0:T(8,128)(2,1)S(1)}, bf16[80,512]{1,0:T(8,128)(2,1)S(1)}, u32[]{:S(2)}, u32[]{:S(2)}) collective-permute-start(bf16[80,512]{1,0:T(8,128)(2,1)S(1)} %get-tuple-element.28), channel_id=1, source_target_pairs={{0,28},{4,24},{8,20},{12,16},{16,12},{20,8},{24,4},{28,0},{1,29},{... | collective-permute-start | bytes 245768 | tf_op jit(solution)/shard_map/ppermute | solution.py:243

commit v6 on v5

--- a/solution.py
+++ b/solution.py
@@ -32,7 +32,8 @@
 
 
 def exact_parts(x):
-    high = x.astype(jnp.bfloat16)
+    limit = float(jnp.finfo(jnp.bfloat16).max)
+    high = jnp.clip(x, -limit, limit).astype(jnp.bfloat16)
     rest = x - high.astype(jnp.float32)
     middle = rest.astype(jnp.bfloat16)
     return [high, middle, (rest - middle.astype(jnp.float32)).astype(jnp.bfloat16)]
@@ -86,7 +87,7 @@
     ):
         for e in range(inputs.shape[0]):
             at = slice(slot * LANES, slot * LANES + tokens)
-            both = own[:, at] + other[:, at]
+            both = own[:, at] + other[:, at].astype(jnp.float32)
             live = iota(both.shape, 1) < lengths[e]
             both = jnp.where(live, both, 0.0).astype(jnp.bfloat16)
             down_whole = dot(both[rank:], inputs[e], FIRST_LAST)
@@ -275,7 +276,7 @@
     )
     step = 1
     while step < mp:
-        other = exchange(own, "mp", step)
+        other = exchange(own if 2 * step < mp else own.astype(bf16), "mp", step)
         step *= 2
         if step < mp:
             own = own + other
@@ -293,8 +294,8 @@
         compiler_params=PARAMS,
         name="gradients",
     )(pub_len, priv_len, own, other, *held)
-    ranked = sorted(range(1, dp), key=lambda k: (k & 1, k if k & 1 else -k))
-    far, near = [k for k in ranked if 2 * k >= dp], [k for k in ranked if 2 * k < dp]
+    far = sorted(range(dp // 2, dp), key=lambda k: (k & 1, k if k & 1 else -k))
+    near = sorted(range(1, dp // 2), key=lambda k: (-k.bit_length(), k))
     order = [k for pair in zip(far, near + [0]) for k in pair]
     blocks = [exchange(blocks[k], "dp", k) if k else blocks[k] for k in order]
 

time: 44.7 us -> 44.2 us (0.989)
  transfers between devices with their start and end apart: 9 -> 9, of which waited for: 4 -> 5; matrix products, arithmetic and copies ran while one was open for 0% -> 0% of each run, Pallas kernels for 0% -> 0%
where the time goes in v6:
time: 44.2 us; the launch traced here: 44 us
  starting transfers between devices  16.3 us (37%)
  blocking collectives  10.6 us (24%)
  waiting for transfers between devices  8.08 us (18%)
  Pallas kernels  7.64 us (17%)
  between operations  1.34 us (3%)
    ppermute x9, starting transfers between devices, exchange(): lax.ppermute(x, axis, [(s, s ^ step) for s in range(lax.axis_size(axis))])  16.3 us
    all_to_all x1, blocking collectives, small_group(): shares = lax.all_to_all(shares, ('dp', 'mp'), 0, 0, tiled=True)  10.6 us
    ppermute x9, waiting for transfers between devices, exchange(): lax.ppermute(x, axis, [(s, s ^ step) for s in range(lax.axis_size(axis))])  8.08 us
    pallas_call x1, Pallas kernels, small_group(): pl.pallas_call(project_kernel, out_shape=[jax.ShapeDtypeStruct((2 * rank,...  3.18 us
    pallas_call x1, Pallas kernels, small_group(): pl.pallas_call(functools.partial(update_kernel, gain), out_shape=[jax.Sha...  2.27 us
    pallas_call x1, Pallas kernels, small_group(): pl.pallas_call(functools.partial(gradient_kernel, dp), out_shape=[block]...  1.34 us
  transfers between devices with their start and end apart: 9, of which 5 were waited for; matrix products, arithmetic and copies ran while one was open for 0% of the time, Pallas kernels for 0%

profile of v6, /device:TPU:0, one launch (start us, length us, event | category | flops | bytes accessed | tf_op | source)
XLA Modules:
  0.0 44.0 jit_solution(2866451087008739849)
XLA Ops:
  0.6 0.0 copy-start.2
  0.6 3.2 %project.1 = (f32[32,640]{1,0:T(8,128)S(1)}, bf16[1,112,2048]{2,1,0:T(8,128)(2,1)S(1)}, bf16[1,112,2048]{2,1,0:T(8,128)(2,1)S(1)}, bf16[4,112,2048]{2,1,0:T(8,128)(2,1)S(1)}, bf16[4,112,2048]{2,1,0:T(8,128)(2,1)S(1)}) custom-call(bf16[1,112,2048]{2,1,0:T(8,128)(2,1)} %pub_in.1, bf16[1,112,2048]{2,1,0:T(8,128)(2,1)} %pub_out.1, ...), custom_call_target="tpu_custom_call" | custom-call | tf_op jit(solution)/shard_map/project/pallas_call | solution.py:258
  3.8 0.5 %collective-permute-start = (f32[32,640]{1,0:T(8,128)S(1)}, f32[32,640]{1,0:T(8,128)S(1)}, u32[]{:S(2)}, u32[]{:S(2)}) collective-permute-start(f32[32,640]{1,0:T(8,128)S(1)} %get-tuple-element.17), channel_id=1, source_target_pairs={{0,1},{1,0},{2,3},{3,2},{4,5},{5,4},{6,7},{7,6},{8,9},{9,8},{10,11... | collective-permute-start | bytes 245768 | tf_op jit(solution)/shard_map/ppermute | solution.py:244
  4.4 0.9 %collective-permute-done = f32[32,640]{1,0:T(8,128)S(1)} collective-permute-done((f32[32,640]{1,0:T(8,128)S(1)}, f32[32,640]{1,0:T(8,128)S(1)}, u32[]{:S(2)}, u32[]{:S(2)}) %collective-permute-start) | collective-permute-done | bytes 81952 | tf_op jit(solution)/shard_map/ppermute | solution.py:244
  5.3 2.9 %collective-permute-start.1 = (bf16[32,640]{1,0:T(8,128)(2,1)S(1)}, bf16[32,640]{1,0:T(8,128)(2,1)S(1)}, u32[]{:S(2)}, u32[]{:S(2)}) collective-permute-start(bf16[32,640]{1,0:T(8,128)(2,1)S(1)} %get-tuple-element.32), channel_id=1, source_target_pairs={{0,2},{1,3},{2,0},{3,1},{4,6},{5,7},{6,4},{7,5},{8,10},{9,11},{10,... | collective-permute-start | bytes 122888 | tf_op jit(solution)/shard_map/ppermute | solution.py:244
  8.8 1.3 %collective-permute-done.1.other = bf16[32,640]{1,0:T(8,128)(2,1)S(1)} collective-permute-done((bf16[32,640]{1,0:T(8,128)(2,1)S(1)}, bf16[32,640]{1,0:T(8,128)(2,1)S(1)}, u32[]{:S(2)}, u32[]{:S(2)}) %collective-permute-start.1) | collective-permute-done | bytes 40992 | tf_op jit(solution)/shard_map/ppermute | solution.py:244
  10.2 0.0 copy-done.2
  10.2 0.0 copy-start
  10.2 0.0 copy-start.1
  10.2 0.0 copy-start.3
  10.2 1.3 %gradients.1 = (bf16[80,512]{1,0:T(8,128)(2,1)S(1)}, bf16[80,512]{1,0:T(8,128)(2,1)S(1)}, bf16[80,512]{1,0:T(8,128)(2,1)S(1)}, bf16[80,512]{1,0:T(8,128)(2,1)S(1...) custom-call(s32[1]{0:T(128)S(6)} %copy.13.pub_len, ...), custom_call_target="tpu_custom_call" | custom-call | tf_op jit(solution)/shard_map/gradients/pallas_call | solution.py:285
  11.5 4.2 %collective-permute-start.2 = (bf16[80,512]{1,0:T(8,128)(2,1)S(1)}, bf16[80,512]{1,0:T(8,128)(2,1)S(1)}, u32[]{:S(2)}, u32[]{:S(2)}) collective-permute-start(bf16[80,512]{1,0:T(8,128)(2,1)S(1)} %get-tuple-element.22), channel_id=1, source_target_pairs={{0,24},{4,28},{8,16},{12,20},{16,8},{20,12},{24,0},{28,4},{1,25},{... | collective-permute-start | bytes 245768 | tf_op jit(solution)/shard_map/ppermute | solution.py:244
  15.7 0.0 collective-permute-start.3
  15.7 0.6 %collective-permute-start.4 = (bf16[80,512]{1,0:T(8,128)(2,1)S(1)}, bf16[80,512]{1,0:T(8,128)(2,1)S(1)}, u32[]{:S(2)}, u32[]{:S(2)}) collective-permute-start(bf16[80,512]{1,0:T(8,128)(2,1)S(1)} %get-tuple-element.24), channel_id=1, source_target_pairs={{0,16},{4,20},{8,24},{12,28},{16,0},{20,4},{24,8},{28,12},{1,17},{... | collective-permute-start | bytes 245768 | tf_op jit(solution)/shard_map/ppermute | solution.py:244
  16.4 2.3 %collective-permute-start.5 = (bf16[80,512]{1,0:T(8,128)(2,1)S(1)}, bf16[80,512]{1,0:T(8,128)(2,1)S(1)}, u32[]{:S(2)}, u32[]{:S(2)}) collective-permute-start(bf16[80,512]{1,0:T(8,128)(2,1)S(1)} %get-tuple-element.25), channel_id=1, source_target_pairs={{0,12},{4,8},{8,4},{12,0},{16,28},{20,24},{24,20},{28,16},{1,13},{... | collective-permute-start | bytes 245768 | tf_op jit(solution)/shard_map/ppermute | solution.py:244
  18.7 2.9 %collective-permute-start.6 = (bf16[80,512]{1,0:T(8,128)(2,1)S(1)}, bf16[80,512]{1,0:T(8,128)(2,1)S(1)}, u32[]{:S(2)}, u32[]{:S(2)}) collective-permute-start(bf16[80,512]{1,0:T(8,128)(2,1)S(1)} %get-tuple-element.26), channel_id=1, source_target_pairs={{0,20},{4,16},{8,28},{12,24},{16,4},{20,0},{24,12},{28,8},{1,21},{... | collective-permute-start | bytes 245768 | tf_op jit(solution)/shard_map/ppermute | solution.py:244
  21.6 0.0 collective-permute-done.2.refs_0_
  21.6 1.5 %collective-permute-start.7 = (bf16[80,512]{1,0:T(8,128)(2,1)S(1)}, bf16[80,512]{1,0:T(8,128)(2,1)S(1)}, u32[]{:S(2)}, u32[]{:S(2)}) collective-permute-start(bf16[80,512]{1,0:T(8,128)(2,1)S(1)} %get-tuple-element.27), channel_id=1, source_target_pairs={{0,4},{4,0},{8,12},{12,8},{16,20},{20,16},{24,28},{28,24},{1,5},{5... | collective-permute-start | bytes 245768 | tf_op jit(solution)/shard_map/ppermute | solution.py:244
  23.1 0.0 collective-permute-done.3.refs_1_
  23.1 1.3 %collective-permute-start.8 = (bf16[80,512]{1,0:T(8,128)(2,1)S(1)}, bf16[80,512]{1,0:T(8,128)(2,1)S(1)}, u32[]{:S(2)}, u32[]{:S(2)}) collective-permute-start(bf16[80,512]{1,0:T(8,128)(2,1)S(1)} %get-tuple-element.28), channel_id=1, source_target_pairs={{0,28},{4,24},{8,20},{12,16},{16,12},{20,8},{24,4},{28,0},{1,29},{... | collective-permute-start | bytes 245768 | tf_op jit(solution)/shard_map/ppermute | solution.py:244
  24.4 0.0 collective-permute-done.4.refs_2_
  24.4 0.7 %collective-permute-done.5.refs_3_ = bf16[80,512]{1,0:T(8,128)(2,1)S(1)} collective-permute-done((bf16[80,512]{1,0:T(8,128)(2,1)S(1)}, bf16[80,512]{1,0:T(8,128)(2,1)S(1)}, u32[]{:S(2)}, u32[]{:S(2)}) %collective-permute-start.5) | collective-permute-done | bytes 81952 | tf_op jit(solution)/shard_map/ppermute | solution.py:244
  25.1 3.0 %collective-permute-done.6.refs_4_ = bf16[80,512]{1,0:T(8,128)(2,1)S(1)} collective-permute-done((bf16[80,512]{1,0:T(8,128)(2,1)S(1)}, bf16[80,512]{1,0:T(8,128)(2,1)S(1)}, u32[]{:S(2)}, u32[]{:S(2)}) %collective-permute-start.6) | collective-permute-done | bytes 81952 | tf_op jit(solution)/shard_map/ppermute | solution.py:244
  28.1 0.0 collective-permute-done.7.refs_5_
  28.1 2.2 %collective-permute-done.8.refs_6_ = bf16[80,512]{1,0:T(8,128)(2,1)S(1)} collective-permute-done((bf16[80,512]{1,0:T(8,128)(2,1)S(1)}, bf16[80,512]{1,0:T(8,128)(2,1)S(1)}, u32[]{:S(2)}, u32[]{:S(2)}) %collective-permute-start.8) | collective-permute-done | bytes 81952 | tf_op jit(solution)/shard_map/ppermute | solution.py:244
  30.3 0.8 %inner_products.1 = (bf16[640,512]{1,0:T(8,128)(2,1)S(1)}, f32[32,4,128]{2,1,0:T(4,128)S(1)}) custom-call(bf16[80,512]{1,0:T(8,128)(2,1)S(1)} %collective-permute-done.2.refs_0_, bf16[80,512]{1,0:T(8,128)(2,1)S(1)} %collective-permute-done.3.refs_1_, bf16[80,512]{1,0:T(8,128)(2,1)S(1)} %collective-permute-done.4.refs_2_, ...), custom_call_target="tpu_custom_call" | custom-call | tf_op jit(solution)/shard_map/inner_products/pallas_call | solution.py:302
  31.1 10.6 %all_to_all.5.shares = f32[32,4,128]{2,1,0:T(4,128)S(1)} all-to-all(f32[32,4,128]{2,1,0:T(4,128)S(1)} %get-tuple-element.30), channel_id=1, replica_groups=mesh['dp'=8,'mp'=4] {'dp','mp'}, dimensions={0} | all-to-all | bytes 131072 | tf_op jit(solution)/shard_map/all_to_all | solution.py:313
  41.7 0.0 copy-done
  41.7 0.0 copy-done.1
  41.7 0.0 copy-done.3
  41.7 2.3 %update.1 = (f32[1,4096]{1,0:T(1,128)}, f32[1,4096]{1,0:T(1,128)}) custom-call(f32[32,4,128]{2,1,0:T(4,128)S(1)} %all_to_all.5.shares, bf16[640,512]{1,0:T(8,128)(2,1)S(1)} %get-tuple-element.31.group, f32[8]{0:T(128)S(1)} %copy-done.3, f32[1,4096]{1,0:T(1,128)S(1)} %copy-done, f32[1,4096]{1,0:T(1,128)S(1)} %copy-done.1), custom_call_target="tpu_custom_call" | custom-call | tf_op jit(solution)/shard_map/update/pallas_call | solution.py:316
  (1 shorter events, 0.0 us)
Async XLA Ops:
  0.6 9.5 %copy-start.2 = (s32[4]{0:T(128)S(1)}, s32[4]{0:T(128)}, u32[]{:S(2)}) copy-start(s32[4]{0:T(128)} %priv_len.1) | copy-start | bytes 52
  3.8 1.4 %collective-permute-start = (f32[32,640]{1,0:T(8,128)S(1)}, f32[32,640]{1,0:T(8,128)S(1)}, u32[]{:S(2)}, u32[]{:S(2)}) collective-permute-start(f32[32,640]{1,0:T(8,128)S(1)} %get-tuple-element.17), channel_id=1, source_target_pairs={{0,1},{1,0},{2,3},{3,2},{4,5},{5,4},{6,7},{7,6},{8,9},{9,8},{10,11... | collective-permute-start | bytes 245768 | tf_op jit(solution)/shard_map/ppermute | solution.py:244
  5.3 4.9 %collective-permute-start.1 = (bf16[32,640]{1,0:T(8,128)(2,1)S(1)}, bf16[32,640]{1,0:T(8,128)(2,1)S(1)}, u32[]{:S(2)}, u32[]{:S(2)}) collective-permute-start(bf16[32,640]{1,0:T(8,128)(2,1)S(1)} %get-tuple-element.32), channel_id=1, source_target_pairs={{0,2},{1,3},{2,0},{3,1},{4,6},{5,7},{6,4},{7,5},{8,10},{9,11},{10,... | collective-permute-start | bytes 122888 | tf_op jit(solution)/shard_map/ppermute | solution.py:244
  10.2 31.6 %copy-start = (f32[1,4096]{1,0:T(1,128)S(1)}, f32[1,4096]{1,0:T(1,128)}, u32[]{:S(2)}) copy-start(f32[1,4096]{1,0:T(1,128)} %down_noise.1) | copy-start | bytes 49156
  10.2 31.6 %copy-start.1 = (f32[1,4096]{1,0:T(1,128)S(1)}, f32[1,4096]{1,0:T(1,128)}, u32[]{:S(2)}) copy-start(f32[1,4096]{1,0:T(1,128)} %up_noise.1) | copy-start | bytes 49156
  10.2 31.6 %copy-start.3 = (f32[8]{0:T(128)S(1)}, f32[8]{0:T(128)}, u32[]{:S(2)}) copy-start(f32[8]{0:T(128)} %noise.1) | copy-start | bytes 100
  11.5 10.1 %collective-permute-start.2 = (bf16[80,512]{1,0:T(8,128)(2,1)S(1)}, bf16[80,512]{1,0:T(8,128)(2,1)S(1)}, u32[]{:S(2)}, u32[]{:S(2)}) collective-permute-start(bf16[80,512]{1,0:T(8,128)(2,1)S(1)} %get-tuple-element.22), channel_id=1, source_target_pairs={{0,24},{4,28},{8,16},{12,20},{16,8},{20,12},{24,0},{28,4},{1,25},{... | collective-permute-start | bytes 245768 | tf_op jit(solution)/shard_map/ppermute | solution.py:244
  15.7 7.4 %collective-permute-start.3 = (bf16[80,512]{1,0:T(8,128)(2,1)S(1)}, bf16[80,512]{1,0:T(8,128)(2,1)S(1)}, u32[]{:S(2)}, u32[]{:S(2)}) collective-permute-start(bf16[80,512]{1,0:T(8,128)(2,1)S(1)} %get-tuple-element.23), channel_id=1, source_target_pairs={{0,8},{4,12},{8,0},{12,4},{16,24},{20,28},{24,16},{28,20},{1,9},{5... | collective-permute-start | bytes 245768 | tf_op jit(solution)/shard_map/ppermute | solution.py:244
  15.7 8.7 %collective-permute-start.4 = (bf16[80,512]{1,0:T(8,128)(2,1)S(1)}, bf16[80,512]{1,0:T(8,128)(2,1)S(1)}, u32[]{:S(2)}, u32[]{:S(2)}) collective-permute-start(bf16[80,512]{1,0:T(8,128)(2,1)S(1)} %get-tuple-element.24), channel_id=1, source_target_pairs={{0,16},{4,20},{8,24},{12,28},{16,0},{20,4},{24,8},{28,12},{1,17},{... | collective-permute-start | bytes 245768 | tf_op jit(solution)/shard_map/ppermute | solution.py:244
  16.4 8.7 %collective-permute-start.5 = (bf16[80,512]{1,0:T(8,128)(2,1)S(1)}, bf16[80,512]{1,0:T(8,128)(2,1)S(1)}, u32[]{:S(2)}, u32[]{:S(2)}) collective-permute-start(bf16[80,512]{1,0:T(8,128)(2,1)S(1)} %get-tuple-element.25), channel_id=1, source_target_pairs={{0,12},{4,8},{8,4},{12,0},{16,28},{20,24},{24,20},{28,16},{1,13},{... | collective-permute-start | bytes 245768 | tf_op jit(solution)/shard_map/ppermute | solution.py:244
  18.7 9.4 %collective-permute-start.6 = (bf16[80,512]{1,0:T(8,128)(2,1)S(1)}, bf16[80,512]{1,0:T(8,128)(2,1)S(1)}, u32[]{:S(2)}, u32[]{:S(2)}) collective-permute-start(bf16[80,512]{1,0:T(8,128)(2,1)S(1)} %get-tuple-element.26), channel_id=1, source_target_pairs={{0,20},{4,16},{8,28},{12,24},{16,4},{20,0},{24,12},{28,8},{1,21},{... | collective-permute-start | bytes 245768 | tf_op jit(solution)/shard_map/ppermute | solution.py:244
  21.6 6.5 %collective-permute-start.7 = (bf16[80,512]{1,0:T(8,128)(2,1)S(1)}, bf16[80,512]{1,0:T(8,128)(2,1)S(1)}, u32[]{:S(2)}, u32[]{:S(2)}) collective-permute-start(bf16[80,512]{1,0:T(8,128)(2,1)S(1)} %get-tuple-element.27), channel_id=1, source_target_pairs={{0,4},{4,0},{8,12},{12,8},{16,20},{20,16},{24,28},{28,24},{1,5},{5... | collective-permute-start | bytes 245768 | tf_op jit(solution)/shard_map/ppermute | solution.py:244
  23.1 7.1 %collective-permute-start.8 = (bf16[80,512]{1,0:T(8,128)(2,1)S(1)}, bf16[80,512]{1,0:T(8,128)(2,1)S(1)}, u32[]{:S(2)}, u32[]{:S(2)}) collective-permute-start(bf16[80,512]{1,0:T(8,128)(2,1)S(1)} %get-tuple-element.28), channel_id=1, source_target_pairs={{0,28},{4,24},{8,20},{12,16},{16,12},{20,8},{24,4},{28,0},{1,29},{... | collective-permute-start | bytes 245768 | tf_op jit(solution)/shard_map/ppermute | solution.py:244

commit v7 on v6

--- a/solution.py
+++ b/solution.py
@@ -40,8 +40,7 @@
 
 
 def project_kernel(pub_in, pub_out, priv_in, priv_out, down_t, up, *rest):
-    out, held, (down_held, up_held, sems) = rest[0], rest[1:5], rest[5:]
-    rank = up.shape[0]
+    outs, held, (down_held, up_held, sems) = rest[:2], rest[2:6], rest[6:]
     tokens = pub_in.shape[1]
     copies = [
         pltpu.make_async_copy(down_t, down_held, sems.at[0]),
@@ -60,7 +59,8 @@
                 )
     for copy in copies:
         copy.start()
-    out[...] = jnp.zeros_like(out)
+    for out in outs:
+        out[...] = jnp.zeros_like(out)
     for copy in copies[:2]:
         copy.wait()
     for i, (weights, piece) in enumerate(pieces):
@@ -68,15 +68,16 @@
             for copy in copies[2 + i : 2 + i + GROUP]:
                 copy.wait()
         slot, half = i // 2, i % 2
-        out[half * rank : (half + 1) * rank, slot * LANES : slot * LANES + tokens] = dot(
+        outs[half][:, slot * LANES : slot * LANES + tokens] = dot(
             weights[...], piece[...], BOTH_LAST
         )
 
 
-def gradient_kernel(dp, pub_len, priv_len, own, other, pub_in, pub_out, priv_in, priv_out, *rest):
-    blocks, down_rows, up_rows = rest[:dp], rest[dp], rest[dp + 1]
+def gradient_kernel(dp, pub_len, priv_len, *rest):
+    projected, returned, (pub_in, pub_out, priv_in, priv_out) = rest[:2], rest[2:4], rest[4:8]
+    blocks, (down_rows, up_rows) = rest[8 : 8 + dp], rest[8 + dp :]
     me = lax.axis_index("dp")
-    rank = own.shape[0] // 2
+    rank = projected[0].shape[0]
     tokens, width = pub_in.shape[1:]
     lanes = width // dp
     per = rank // dp
@@ -87,11 +88,13 @@
     ):
         for e in range(inputs.shape[0]):
             at = slice(slot * LANES, slot * LANES + tokens)
-            both = own[:, at] + other[:, at].astype(jnp.float32)
-            live = iota(both.shape, 1) < lengths[e]
-            both = jnp.where(live, both, 0.0).astype(jnp.bfloat16)
-            down_whole = dot(both[rank:], inputs[e], FIRST_LAST)
-            up_whole = dot(both[:rank], cotangents[e], FIRST_LAST)
+            live = iota((rank, tokens), 1) < lengths[e]
+            down_live, up_live = (
+                jnp.where(live, own[:, at] + other[:, at], 0.0).astype(jnp.bfloat16)
+                for own, other in (returned, projected)
+            )
+            down_whole = dot(down_live, inputs[e], FIRST_LAST)
+            up_whole = dot(up_live, cotangents[e], FIRST_LAST)
             for c in range(dp):
                 features = slice(c * lanes, (c + 1) * lanes)
                 at = slice(c * rank, (c + 1) * rank)
@@ -244,6 +247,12 @@
     return lax.ppermute(x, axis, [(s, s ^ step) for s in range(lax.axis_size(axis))])
 
 
+def sum_over(axis, own, steps):
+    for step in steps[:-1]:
+        own = own + exchange(own, axis, step)
+    return own, exchange(own, axis, steps[-1])
+
+
 def small_group(
     pub_in, pub_out, pub_len, priv_in, priv_out, priv_len, down, up, noise, down_noise, up_noise
 ):
@@ -255,12 +264,12 @@
     lanes = width // dp
     f32, bf16 = jnp.float32, jnp.bfloat16
 
-    own, *held = pl.pallas_call(
+    projected, returned, *held = pl.pallas_call(
         project_kernel,
-        out_shape=[jax.ShapeDtypeStruct((2 * rank, examples * LANES), f32)]
+        out_shape=[jax.ShapeDtypeStruct((rank, examples * LANES), f32)] * 2
         + [jax.ShapeDtypeStruct(x.shape, bf16) for x in (pub_in, pub_out, priv_in, priv_out)],
         in_specs=[HBM] * 6,
-        out_specs=[VMEM] * 5,
+        out_specs=[VMEM] * 6,
         scratch_shapes=[
             pltpu.VMEM(up.shape, bf16),
             pltpu.VMEM(up.shape, bf16),
@@ -274,18 +283,15 @@
             for x in (pub_in, pub_out, priv_in, priv_out, down.T, up)
         )
     )
-    step = 1
-    while step < mp:
-        other = exchange(own if 2 * step < mp else own.astype(bf16), "mp", step)
-        step *= 2
-        if step < mp:
-            own = own + other
+    steps = [1 << i for i in range(mp.bit_length() - 1)]
+    projected = sum_over("mp", projected, steps)
+    returned = sum_over("mp", returned, steps[::-1])
 
     block = jax.ShapeDtypeStruct((examples * rank, 2 * lanes), bf16)
     blocks = pl.pallas_call(
         functools.partial(gradient_kernel, dp),
         out_shape=[block] * dp,
-        in_specs=[SMEM] * 2 + [VMEM] * 6,
+        in_specs=[SMEM] * 2 + [VMEM] * 8,
         out_specs=[VMEM] * dp,
         scratch_shapes=[
             pltpu.VMEM((dp * rank, lanes), bf16),
@@ -293,7 +299,7 @@
         ],
         compiler_params=PARAMS,
         name="gradients",
-    )(pub_len, priv_len, own, other, *held)
+    )(pub_len, priv_len, *projected, *returned, *held)
     far = sorted(range(dp // 2, dp), key=lambda k: (k & 1, k if k & 1 else -k))
     near = sorted(range(1, dp // 2), key=lambda k: (-k.bit_length(), k))
     order = [k for pair in zip(far, near + [0]) for k in pair]

time: 44.2 us -> 44.6 us (level)
    ppermute x9 -> x11, waiting for transfers between devices: 8.08 us -> 8.28 us  [exchange(): lax.ppermute(x, axis, [(s, s ^ step) for s in range(lax.axis_size(axis))])]
    ppermute x9 -> x11, starting transfers between devices: 16.3 us -> 16.5 us  [exchange(): lax.ppermute(x, axis, [(s, s ^ step) for s in range(lax.axis_size(axis))])]
  transfers between devices with their start and end apart: 9 -> 11, of which waited for: 5 -> 5; matrix products, arithmetic and copies ran while one was open for 0% -> 0% of each run, Pallas kernels for 0% -> 0%
where the time goes in v7:
time: 44.6 us; the launch traced here: 44.4 us
  starting transfers between devices  16.5 us (37%)
  blocking collectives  10.6 us (24%)
  waiting for transfers between devices  8.28 us (19%)
  Pallas kernels  7.65 us (17%)
  between operations  1.36 us (3%)
    ppermute x11, starting transfers between devices, exchange(): lax.ppermute(x, axis, [(s, s ^ step) for s in range(lax.axis_size(axis))])  16.5 us
    all_to_all x1, blocking collectives, small_group(): shares = lax.all_to_all(shares, ('dp', 'mp'), 0, 0, tiled=True)  10.6 us
    ppermute x11, waiting for transfers between devices, exchange(): lax.ppermute(x, axis, [(s, s ^ step) for s in range(lax.axis_size(axis))])  8.28 us
    pallas_call x1, Pallas kernels, small_group(): pl.pallas_call(project_kernel, out_shape=[jax.ShapeDtypeStruct((rank, exa...  3.18 us
    pallas_call x1, Pallas kernels, small_group(): pl.pallas_call(functools.partial(update_kernel, gain), out_shape=[jax.Sha...  2.27 us
    pallas_call x1, Pallas kernels, small_group(): pl.pallas_call(functools.partial(gradient_kernel, dp), out_shape=[block]...  1.35 us
  transfers between devices with their start and end apart: 11, of which 5 were waited for; matrix products, arithmetic and copies ran while one was open for 0% of the time, Pallas kernels for 0%

profile of v7, /device:TPU:0, one launch (start us, length us, event | category | flops | bytes accessed | tf_op | source)
XLA Modules:
  0.0 44.4 jit_solution(11070092818920865060)
XLA Ops:
  0.6 0.0 copy-start.3
  0.6 3.2 %project.1 = (f32[16,640]{1,0:T(8,128)S(1)}, f32[16,640]{1,0:T(8,128)S(1)}, bf16[1,112,2048]{2,1,0:T(8,128)(2,1)S(1)}, bf16[1,112,2048]{2,1,0:T(8,128)(2,1)S(1)}...) custom-call(bf16[1,112,2048]{2,1,0:T(8,128)(2,1)} %pub_in.1, bf16[1,112,2048]{2,1,0:T(8,128)(2,1)} %pub_out.1, ...), custom_call_target="tpu_custom_call" | custom-call | tf_op jit(solution)/shard_map/project/pallas_call | solution.py:267
  3.8 0.5 %collective-permute-start = (f32[16,640]{1,0:T(8,128)S(1)}, f32[16,640]{1,0:T(8,128)S(1)}, u32[]{:S(2)}, u32[]{:S(2)}) collective-permute-start(f32[16,640]{1,0:T(8,128)S(1)} %get-tuple-element.18), channel_id=1, source_target_pairs={{0,1},{1,0},{2,3},{3,2},{4,5},{5,4},{6,7},{7,6},{8,9},{9,8},{10,11... | collective-permute-start | bytes 122888 | tf_op jit(solution)/shard_map/ppermute | solution.py:247
  4.3 2.6 %collective-permute-start.2 = (f32[16,640]{1,0:T(8,128)S(1)}, f32[16,640]{1,0:T(8,128)S(1)}, u32[]{:S(2)}, u32[]{:S(2)}) collective-permute-start(f32[16,640]{1,0:T(8,128)S(1)} %get-tuple-element.19), channel_id=1, source_target_pairs={{0,2},{1,3},{2,0},{3,1},{4,6},{5,7},{6,4},{7,5},{8,10},{9,11},{10,... | collective-permute-start | bytes 122888 | tf_op jit(solution)/shard_map/ppermute | solution.py:247
  6.9 0.0 collective-permute-done
  6.9 1.1 %collective-permute-start.1 = (f32[16,640]{1,0:T(8,128)S(1)}, f32[16,640]{1,0:T(8,128)S(1)}, u32[]{:S(2)}, u32[]{:S(2)}) collective-permute-start(f32[16,640]{1,0:T(8,128)S(1)} %add.6.rest_0_), channel_id=1, source_target_pairs={{0,2},{1,3},{2,0},{3,1},{4,6},{5,7},{6,4},{7,5},{8,10},{9,11},{10,... | collective-permute-start | bytes 122888 | tf_op jit(solution)/shard_map/ppermute | solution.py:247
  8.1 1.0 %collective-permute-done.2 = f32[16,640]{1,0:T(8,128)S(1)} collective-permute-done((f32[16,640]{1,0:T(8,128)S(1)}, f32[16,640]{1,0:T(8,128)S(1)}, u32[]{:S(2)}, u32[]{:S(2)}) %collective-permute-start.2) | collective-permute-done | bytes 40992 | tf_op jit(solution)/shard_map/ppermute | solution.py:247
  9.1 0.0 collective-permute-start.3
  9.7 1.3 %collective-permute-done.1.rest_1_ = f32[16,640]{1,0:T(8,128)S(1)} collective-permute-done((f32[16,640]{1,0:T(8,128)S(1)}, f32[16,640]{1,0:T(8,128)S(1)}, u32[]{:S(2)}, u32[]{:S(2)}) %collective-permute-start.1) | collective-permute-done | bytes 40992 | tf_op jit(solution)/shard_map/ppermute | solution.py:247
  11.0 0.0 collective-permute-done.3.rest_3_
  11.0 0.0 copy-done.3
  11.0 0.0 copy-start
  11.0 0.0 copy-start.1
  11.0 0.0 copy-start.2
  11.0 1.4 %gradients.1 = (bf16[80,512]{1,0:T(8,128)(2,1)S(1)}, bf16[80,512]{1,0:T(8,128)(2,1)S(1)}, bf16[80,512]{1,0:T(8,128)(2,1)S(1)}, bf16[80,512]{1,0:T(8,128)(2,1)S(1...) custom-call(s32[1]{0:T(128)S(6)} %copy.13.pub_len, ...), custom_call_target="tpu_custom_call" | custom-call | tf_op jit(solution)/shard_map/gradients/pallas_call | solution.py:291
  12.4 3.7 %collective-permute-start.4 = (bf16[80,512]{1,0:T(8,128)(2,1)S(1)}, bf16[80,512]{1,0:T(8,128)(2,1)S(1)}, u32[]{:S(2)}, u32[]{:S(2)}) collective-permute-start(bf16[80,512]{1,0:T(8,128)(2,1)S(1)} %get-tuple-element.24), channel_id=1, source_target_pairs={{0,24},{4,28},{8,16},{12,20},{16,8},{20,12},{24,0},{28,4},{1,25},{... | collective-permute-start | bytes 245768 | tf_op jit(solution)/shard_map/ppermute | solution.py:247
  16.1 0.0 collective-permute-start.5
  16.1 0.8 %collective-permute-start.6 = (bf16[80,512]{1,0:T(8,128)(2,1)S(1)}, bf16[80,512]{1,0:T(8,128)(2,1)S(1)}, u32[]{:S(2)}, u32[]{:S(2)}) collective-permute-start(bf16[80,512]{1,0:T(8,128)(2,1)S(1)} %get-tuple-element.26), channel_id=1, source_target_pairs={{0,16},{4,20},{8,24},{12,28},{16,0},{20,4},{24,8},{28,12},{1,17},{... | collective-permute-start | bytes 245768 | tf_op jit(solution)/shard_map/ppermute | solution.py:247
  16.8 2.2 %collective-permute-start.7 = (bf16[80,512]{1,0:T(8,128)(2,1)S(1)}, bf16[80,512]{1,0:T(8,128)(2,1)S(1)}, u32[]{:S(2)}, u32[]{:S(2)}) collective-permute-start(bf16[80,512]{1,0:T(8,128)(2,1)S(1)} %get-tuple-element.27), channel_id=1, source_target_pairs={{0,12},{4,8},{8,4},{12,0},{16,28},{20,24},{24,20},{28,16},{1,13},{... | collective-permute-start | bytes 245768 | tf_op jit(solution)/shard_map/ppermute | solution.py:247
  19.0 2.9 %collective-permute-start.8 = (bf16[80,512]{1,0:T(8,128)(2,1)S(1)}, bf16[80,512]{1,0:T(8,128)(2,1)S(1)}, u32[]{:S(2)}, u32[]{:S(2)}) collective-permute-start(bf16[80,512]{1,0:T(8,128)(2,1)S(1)} %get-tuple-element.28), channel_id=1, source_target_pairs={{0,20},{4,16},{8,28},{12,24},{16,4},{20,0},{24,12},{28,8},{1,21},{... | collective-permute-start | bytes 245768 | tf_op jit(solution)/shard_map/ppermute | solution.py:247
  21.9 0.0 collective-permute-done.4.refs_0_
  21.9 1.5 %collective-permute-start.9 = (bf16[80,512]{1,0:T(8,128)(2,1)S(1)}, bf16[80,512]{1,0:T(8,128)(2,1)S(1)}, u32[]{:S(2)}, u32[]{:S(2)}) collective-permute-start(bf16[80,512]{1,0:T(8,128)(2,1)S(1)} %get-tuple-element.29), channel_id=1, source_target_pairs={{0,4},{4,0},{8,12},{12,8},{16,20},{20,16},{24,28},{28,24},{1,5},{5... | collective-permute-start | bytes 245768 | tf_op jit(solution)/shard_map/ppermute | solution.py:247
  23.4 0.0 collective-permute-done.5.refs_1_
  23.4 1.2 %collective-permute-start.10 = (bf16[80,512]{1,0:T(8,128)(2,1)S(1)}, bf16[80,512]{1,0:T(8,128)(2,1)S(1)}, u32[]{:S(2)}, u32[]{:S(2)}) collective-permute-start(bf16[80,512]{1,0:T(8,128)(2,1)S(1)} %get-tuple-element.30), channel_id=1, source_target_pairs={{0,28},{4,24},{8,20},{12,16},{16,12},{20,8},{24,4},{28,0},{1,29},{... | collective-permute-start | bytes 245768 | tf_op jit(solution)/shard_map/ppermute | solution.py:247
  24.7 0.0 collective-permute-done.6.refs_2_
  24.7 1.5 %collective-permute-done.7.refs_3_ = bf16[80,512]{1,0:T(8,128)(2,1)S(1)} collective-permute-done((bf16[80,512]{1,0:T(8,128)(2,1)S(1)}, bf16[80,512]{1,0:T(8,128)(2,1)S(1)}, u32[]{:S(2)}, u32[]{:S(2)}) %collective-permute-start.7) | collective-permute-done | bytes 81952 | tf_op jit(solution)/shard_map/ppermute | solution.py:247
  26.2 2.7 %collective-permute-done.8.refs_4_ = bf16[80,512]{1,0:T(8,128)(2,1)S(1)} collective-permute-done((bf16[80,512]{1,0:T(8,128)(2,1)S(1)}, bf16[80,512]{1,0:T(8,128)(2,1)S(1)}, u32[]{:S(2)}, u32[]{:S(2)}) %collective-permute-start.8) | collective-permute-done | bytes 81952 | tf_op jit(solution)/shard_map/ppermute | solution.py:247
  28.8 0.0 collective-permute-done.9.refs_5_
  28.8 1.9 %collective-permute-done.10.refs_6_ = bf16[80,512]{1,0:T(8,128)(2,1)S(1)} collective-permute-done((bf16[80,512]{1,0:T(8,128)(2,1)S(1)}, bf16[80,512]{1,0:T(8,128)(2,1)S(1)}, u32[]{:S(2)}, u32[]{:S(2)}) %collective-permute-start.10) | collective-permute-done | bytes 81952 | tf_op jit(solution)/shard_map/ppermute | solution.py:247
  30.7 0.9 %inner_products.1 = (bf16[640,512]{1,0:T(8,128)(2,1)S(1)}, f32[32,4,128]{2,1,0:T(4,128)S(1)}) custom-call(bf16[80,512]{1,0:T(8,128)(2,1)S(1)} %collective-permute-done.4.refs_0_, bf16[80,512]{1,0:T(8,128)(2,1)S(1)} %collective-permute-done.5.refs_1_, bf16[80,512]{1,0:T(8,128)(2,1)S(1)} %collective-permute-done.6.refs_2_, ...), custom_call_target="tpu_custom_call" | custom-call | tf_op jit(solution)/shard_map/inner_products/pallas_call | solution.py:308
  31.5 10.6 %all_to_all.5.shares = f32[32,4,128]{2,1,0:T(4,128)S(1)} all-to-all(f32[32,4,128]{2,1,0:T(4,128)S(1)} %get-tuple-element.32), channel_id=1, replica_groups=mesh['dp'=8,'mp'=4] {'dp','mp'}, dimensions={0} | all-to-all | bytes 131072 | tf_op jit(solution)/shard_map/all_to_all | solution.py:319
  42.1 0.0 copy-done
  42.1 0.0 copy-done.1
  42.1 0.0 copy-done.2
  42.1 2.3 %update.1 = (f32[1,4096]{1,0:T(1,128)}, f32[1,4096]{1,0:T(1,128)}) custom-call(f32[32,4,128]{2,1,0:T(4,128)S(1)} %all_to_all.5.shares, bf16[640,512]{1,0:T(8,128)(2,1)S(1)} %get-tuple-element.33.group, f32[8]{0:T(128)S(1)} %copy-done.2, f32[1,4096]{1,0:T(1,128)S(1)} %copy-done, f32[1,4096]{1,0:T(1,128)S(1)} %copy-done.1), custom_call_target="tpu_custom_call" | custom-call | tf_op jit(solution)/shard_map/update/pallas_call | solution.py:322
  (2 shorter events, 0.0 us)
Async XLA Ops:
  0.6 10.4 %copy-start.3 = (s32[4]{0:T(128)S(1)}, s32[4]{0:T(128)}, u32[]{:S(2)}) copy-start(s32[4]{0:T(128)} %priv_len.1) | copy-start | bytes 52
  3.8 3.1 %collective-permute-start = (f32[16,640]{1,0:T(8,128)S(1)}, f32[16,640]{1,0:T(8,128)S(1)}, u32[]{:S(2)}, u32[]{:S(2)}) collective-permute-start(f32[16,640]{1,0:T(8,128)S(1)} %get-tuple-element.18), channel_id=1, source_target_pairs={{0,1},{1,0},{2,3},{3,2},{4,5},{5,4},{6,7},{7,6},{8,9},{9,8},{10,11... | collective-permute-start | bytes 122888 | tf_op jit(solution)/shard_map/ppermute | solution.py:247
  4.3 4.7 %collective-permute-start.2 = (f32[16,640]{1,0:T(8,128)S(1)}, f32[16,640]{1,0:T(8,128)S(1)}, u32[]{:S(2)}, u32[]{:S(2)}) collective-permute-start(f32[16,640]{1,0:T(8,128)S(1)} %get-tuple-element.19), channel_id=1, source_target_pairs={{0,2},{1,3},{2,0},{3,1},{4,6},{5,7},{6,4},{7,5},{8,10},{9,11},{10,... | collective-permute-start | bytes 122888 | tf_op jit(solution)/shard_map/ppermute | solution.py:247
  6.9 4.1 %collective-permute-start.1 = (f32[16,640]{1,0:T(8,128)S(1)}, f32[16,640]{1,0:T(8,128)S(1)}, u32[]{:S(2)}, u32[]{:S(2)}) collective-permute-start(f32[16,640]{1,0:T(8,128)S(1)} %add.6.rest_0_), channel_id=1, source_target_pairs={{0,2},{1,3},{2,0},{3,1},{4,6},{5,7},{6,4},{7,5},{8,10},{9,11},{10,... | collective-permute-start | bytes 122888 | tf_op jit(solution)/shard_map/ppermute | solution.py:247
  9.1 1.9 %collective-permute-start.3 = (f32[16,640]{1,0:T(8,128)S(1)}, f32[16,640]{1,0:T(8,128)S(1)}, u32[]{:S(2)}, u32[]{:S(2)}) collective-permute-start(f32[16,640]{1,0:T(8,128)S(1)} %add.7.rest_2_), channel_id=1, source_target_pairs={{0,1},{1,0},{2,3},{3,2},{4,5},{5,4},{6,7},{7,6},{8,9},{9,8},{10,11... | collective-permute-start | bytes 122888 | tf_op jit(solution)/shard_map/ppermute | solution.py:247
  11.0 31.1 %copy-start = (f32[1,4096]{1,0:T(1,128)S(1)}, f32[1,4096]{1,0:T(1,128)}, u32[]{:S(2)}) copy-start(f32[1,4096]{1,0:T(1,128)} %down_noise.1) | copy-start | bytes 49156
  11.0 31.1 %copy-start.1 = (f32[1,4096]{1,0:T(1,128)S(1)}, f32[1,4096]{1,0:T(1,128)}, u32[]{:S(2)}) copy-start(f32[1,4096]{1,0:T(1,128)} %up_noise.1) | copy-start | bytes 49156
  11.0 31.1 %copy-start.2 = (f32[8]{0:T(128)S(1)}, f32[8]{0:T(128)}, u32[]{:S(2)}) copy-start(f32[8]{0:T(128)} %noise.1) | copy-start | bytes 100
  12.4 9.5 %collective-permute-start.4 = (bf16[80,512]{1,0:T(8,128)(2,1)S(1)}, bf16[80,512]{1,0:T(8,128)(2,1)S(1)}, u32[]{:S(2)}, u32[]{:S(2)}) collective-permute-start(bf16[80,512]{1,0:T(8,128)(2,1)S(1)} %get-tuple-element.24), channel_id=1, source_target_pairs={{0,24},{4,28},{8,16},{12,20},{16,8},{20,12},{24,0},{28,4},{1,25},{... | collective-permute-start | bytes 245768 | tf_op jit(solution)/shard_map/ppermute | solution.py:247
  16.1 7.4 %collective-permute-start.5 = (bf16[80,512]{1,0:T(8,128)(2,1)S(1)}, bf16[80,512]{1,0:T(8,128)(2,1)S(1)}, u32[]{:S(2)}, u32[]{:S(2)}) collective-permute-start(bf16[80,512]{1,0:T(8,128)(2,1)S(1)} %get-tuple-element.25), channel_id=1, source_target_pairs={{0,8},{4,12},{8,0},{12,4},{16,24},{20,28},{24,16},{28,20},{1,9},{5... | collective-permute-start | bytes 245768 | tf_op jit(solution)/shard_map/ppermute | solution.py:247
  16.1 8.6 %collective-permute-start.6 = (bf16[80,512]{1,0:T(8,128)(2,1)S(1)}, bf16[80,512]{1,0:T(8,128)(2,1)S(1)}, u32[]{:S(2)}, u32[]{:S(2)}) collective-permute-start(bf16[80,512]{1,0:T(8,128)(2,1)S(1)} %get-tuple-element.26), channel_id=1, source_target_pairs={{0,16},{4,20},{8,24},{12,28},{16,0},{20,4},{24,8},{28,12},{1,17},{... | collective-permute-start | bytes 245768 | tf_op jit(solution)/shard_map/ppermute | solution.py:247
  16.8 9.3 %collective-permute-start.7 = (bf16[80,512]{1,0:T(8,128)(2,1)S(1)}, bf16[80,512]{1,0:T(8,128)(2,1)S(1)}, u32[]{:S(2)}, u32[]{:S(2)}) collective-permute-start(bf16[80,512]{1,0:T(8,128)(2,1)S(1)} %get-tuple-element.27), channel_id=1, source_target_pairs={{0,12},{4,8},{8,4},{12,0},{16,28},{20,24},{24,20},{28,16},{1,13},{... | collective-permute-start | bytes 245768 | tf_op jit(solution)/shard_map/ppermute | solution.py:247
  19.0 9.8 %collective-permute-start.8 = (bf16[80,512]{1,0:T(8,128)(2,1)S(1)}, bf16[80,512]{1,0:T(8,128)(2,1)S(1)}, u32[]{:S(2)}, u32[]{:S(2)}) collective-permute-start(bf16[80,512]{1,0:T(8,128)(2,1)S(1)} %get-tuple-element.28), channel_id=1, source_target_pairs={{0,20},{4,16},{8,28},{12,24},{16,4},{20,0},{24,12},{28,8},{1,21},{... | collective-permute-start | bytes 245768 | tf_op jit(solution)/shard_map/ppermute | solution.py:247
  21.9 6.9 %collective-permute-start.9 = (bf16[80,512]{1,0:T(8,128)(2,1)S(1)}, bf16[80,512]{1,0:T(8,128)(2,1)S(1)}, u32[]{:S(2)}, u32[]{:S(2)}) collective-permute-start(bf16[80,512]{1,0:T(8,128)(2,1)S(1)} %get-tuple-element.29), channel_id=1, source_target_pairs={{0,4},{4,0},{8,12},{12,8},{16,20},{20,16},{24,28},{28,24},{1,5},{5... | collective-permute-start | bytes 245768 | tf_op jit(solution)/shard_map/ppermute | solution.py:247
  23.4 7.2 %collective-permute-start.10 = (bf16[80,512]{1,0:T(8,128)(2,1)S(1)}, bf16[80,512]{1,0:T(8,128)(2,1)S(1)}, u32[]{:S(2)}, u32[]{:S(2)}) collective-permute-start(bf16[80,512]{1,0:T(8,128)(2,1)S(1)} %get-tuple-element.30), channel_id=1, source_target_pairs={{0,28},{4,24},{8,20},{12,16},{16,12},{20,8},{24,4},{28,0},{1,29},{... | collective-permute-start | bytes 245768 | tf_op jit(solution)/shard_map/ppermute | solution.py:247

commit v8 on v7

--- a/solution.py
+++ b/solution.py
@@ -158,7 +158,9 @@
     gap = jnp.zeros((used, lanes), jnp.float32)
     rest = jnp.zeros((half - used - each, lanes), jnp.float32)
     stacked = jnp.concatenate([gap, squares[:each], rest, gap, squares[each:], rest], axis=0)
-    total_squares = dot(jnp.ones((8, lanes), jnp.float32), stacked, BOTH_LAST, PRECISE)
+    ones = jnp.ones((16, lanes), jnp.bfloat16)
+    three = dot(ones, jnp.concatenate(exact_parts(stacked), axis=0), BOTH_LAST)[:8]
+    total_squares = three[:, :LANES] + three[:, LANES : 2 * LANES] + three[:, 2 * LANES :]
     short = publics // 2
     lane = iota((short, LANES), 1)
     packed = jnp.where(lane < half, total[:short], pltpu.roll(total[short:], half, 1))

time: 44.6 us -> 44.4 us (level)
  no operation moved by 1% of the time
where the time goes in v8:
time: 44.4 us; the launch traced here: 44.3 us
  starting transfers between devices  16.5 us (37%)
  blocking collectives  10.6 us (24%)
  waiting for transfers between devices  8.28 us (19%)
  Pallas kernels  7.53 us (17%)
  between operations  1.36 us (3%)
    ppermute x11, starting transfers between devices, exchange(): lax.ppermute(x, axis, [(s, s ^ step) for s in range(lax.axis_size(axis))])  16.5 us
    all_to_all x1, blocking collectives, small_group(): shares = lax.all_to_all(shares, ('dp', 'mp'), 0, 0, tiled=True)  10.6 us
    ppermute x11, waiting for transfers between devices, exchange(): lax.ppermute(x, axis, [(s, s ^ step) for s in range(lax.axis_size(axis))])  8.28 us
    pallas_call x1, Pallas kernels, small_group(): pl.pallas_call(project_kernel, out_shape=[jax.ShapeDtypeStruct((rank, exa...  3.18 us
    pallas_call x1, Pallas kernels, small_group(): pl.pallas_call(functools.partial(update_kernel, gain), out_shape=[jax.Sha...  2.27 us
    pallas_call x1, Pallas kernels, small_group(): pl.pallas_call(functools.partial(gradient_kernel, dp), out_shape=[block]...  1.35 us
  transfers between devices with their start and end apart: 11, of which 5 were waited for; matrix products, arithmetic and copies ran while one was open for 0% of the time, Pallas kernels for 0%

profile of v8, /device:TPU:0, one launch (start us, length us, event | category | flops | bytes accessed | tf_op | source)
XLA Modules:
  0.0 44.3 jit_solution(2184647222670379727)
XLA Ops:
  0.6 0.0 copy-start.3
  0.6 3.2 %project.1 = (f32[16,640]{1,0:T(8,128)S(1)}, f32[16,640]{1,0:T(8,128)S(1)}, bf16[1,112,2048]{2,1,0:T(8,128)(2,1)S(1)}, bf16[1,112,2048]{2,1,0:T(8,128)(2,1)S(1)}...) custom-call(bf16[1,112,2048]{2,1,0:T(8,128)(2,1)} %pub_in.1, bf16[1,112,2048]{2,1,0:T(8,128)(2,1)} %pub_out.1, ...), custom_call_target="tpu_custom_call" | custom-call | tf_op jit(solution)/shard_map/project/pallas_call | solution.py:269
  3.8 0.5 %collective-permute-start = (f32[16,640]{1,0:T(8,128)S(1)}, f32[16,640]{1,0:T(8,128)S(1)}, u32[]{:S(2)}, u32[]{:S(2)}) collective-permute-start(f32[16,640]{1,0:T(8,128)S(1)} %get-tuple-element.18), channel_id=1, source_target_pairs={{0,1},{1,0},{2,3},{3,2},{4,5},{5,4},{6,7},{7,6},{8,9},{9,8},{10,11... | collective-permute-start | bytes 122888 | tf_op jit(solution)/shard_map/ppermute | solution.py:249
  4.3 2.6 %collective-permute-start.2 = (f32[16,640]{1,0:T(8,128)S(1)}, f32[16,640]{1,0:T(8,128)S(1)}, u32[]{:S(2)}, u32[]{:S(2)}) collective-permute-start(f32[16,640]{1,0:T(8,128)S(1)} %get-tuple-element.19), channel_id=1, source_target_pairs={{0,2},{1,3},{2,0},{3,1},{4,6},{5,7},{6,4},{7,5},{8,10},{9,11},{10,... | collective-permute-start | bytes 122888 | tf_op jit(solution)/shard_map/ppermute | solution.py:249
  6.9 0.0 collective-permute-done
  6.9 1.1 %collective-permute-start.1 = (f32[16,640]{1,0:T(8,128)S(1)}, f32[16,640]{1,0:T(8,128)S(1)}, u32[]{:S(2)}, u32[]{:S(2)}) collective-permute-start(f32[16,640]{1,0:T(8,128)S(1)} %add.6.rest_0_), channel_id=1, source_target_pairs={{0,2},{1,3},{2,0},{3,1},{4,6},{5,7},{6,4},{7,5},{8,10},{9,11},{10,... | collective-permute-start | bytes 122888 | tf_op jit(solution)/shard_map/ppermute | solution.py:249
  8.1 1.0 %collective-permute-done.2 = f32[16,640]{1,0:T(8,128)S(1)} collective-permute-done((f32[16,640]{1,0:T(8,128)S(1)}, f32[16,640]{1,0:T(8,128)S(1)}, u32[]{:S(2)}, u32[]{:S(2)}) %collective-permute-start.2) | collective-permute-done | bytes 40992 | tf_op jit(solution)/shard_map/ppermute | solution.py:249
  9.1 0.0 collective-permute-start.3
  9.7 1.3 %collective-permute-done.1.rest_1_ = f32[16,640]{1,0:T(8,128)S(1)} collective-permute-done((f32[16,640]{1,0:T(8,128)S(1)}, f32[16,640]{1,0:T(8,128)S(1)}, u32[]{:S(2)}, u32[]{:S(2)}) %collective-permute-start.1) | collective-permute-done | bytes 40992 | tf_op jit(solution)/shard_map/ppermute | solution.py:249
  11.0 0.0 collective-permute-done.3.rest_3_
  11.0 0.0 copy-done.3
  11.0 0.0 copy-start
  11.0 0.0 copy-start.1
  11.0 0.0 copy-start.2
  11.0 1.4 %gradients.1 = (bf16[80,512]{1,0:T(8,128)(2,1)S(1)}, bf16[80,512]{1,0:T(8,128)(2,1)S(1)}, bf16[80,512]{1,0:T(8,128)(2,1)S(1)}, bf16[80,512]{1,0:T(8,128)(2,1)S(1...) custom-call(s32[1]{0:T(128)S(6)} %copy.13.pub_len, ...), custom_call_target="tpu_custom_call" | custom-call | tf_op jit(solution)/shard_map/gradients/pallas_call | solution.py:293
  12.4 3.7 %collective-permute-start.4 = (bf16[80,512]{1,0:T(8,128)(2,1)S(1)}, bf16[80,512]{1,0:T(8,128)(2,1)S(1)}, u32[]{:S(2)}, u32[]{:S(2)}) collective-permute-start(bf16[80,512]{1,0:T(8,128)(2,1)S(1)} %get-tuple-element.24), channel_id=1, source_target_pairs={{0,24},{4,28},{8,16},{12,20},{16,8},{20,12},{24,0},{28,4},{1,25},{... | collective-permute-start | bytes 245768 | tf_op jit(solution)/shard_map/ppermute | solution.py:249
  16.1 0.0 collective-permute-start.5
  16.1 0.8 %collective-permute-start.6 = (bf16[80,512]{1,0:T(8,128)(2,1)S(1)}, bf16[80,512]{1,0:T(8,128)(2,1)S(1)}, u32[]{:S(2)}, u32[]{:S(2)}) collective-permute-start(bf16[80,512]{1,0:T(8,128)(2,1)S(1)} %get-tuple-element.26), channel_id=1, source_target_pairs={{0,16},{4,20},{8,24},{12,28},{16,0},{20,4},{24,8},{28,12},{1,17},{... | collective-permute-start | bytes 245768 | tf_op jit(solution)/shard_map/ppermute | solution.py:249
  16.8 2.2 %collective-permute-start.7 = (bf16[80,512]{1,0:T(8,128)(2,1)S(1)}, bf16[80,512]{1,0:T(8,128)(2,1)S(1)}, u32[]{:S(2)}, u32[]{:S(2)}) collective-permute-start(bf16[80,512]{1,0:T(8,128)(2,1)S(1)} %get-tuple-element.27), channel_id=1, source_target_pairs={{0,12},{4,8},{8,4},{12,0},{16,28},{20,24},{24,20},{28,16},{1,13},{... | collective-permute-start | bytes 245768 | tf_op jit(solution)/shard_map/ppermute | solution.py:249
  19.0 2.9 %collective-permute-start.8 = (bf16[80,512]{1,0:T(8,128)(2,1)S(1)}, bf16[80,512]{1,0:T(8,128)(2,1)S(1)}, u32[]{:S(2)}, u32[]{:S(2)}) collective-permute-start(bf16[80,512]{1,0:T(8,128)(2,1)S(1)} %get-tuple-element.28), channel_id=1, source_target_pairs={{0,20},{4,16},{8,28},{12,24},{16,4},{20,0},{24,12},{28,8},{1,21},{... | collective-permute-start | bytes 245768 | tf_op jit(solution)/shard_map/ppermute | solution.py:249
  21.9 0.0 collective-permute-done.4.refs_0_
  21.9 1.5 %collective-permute-start.9 = (bf16[80,512]{1,0:T(8,128)(2,1)S(1)}, bf16[80,512]{1,0:T(8,128)(2,1)S(1)}, u32[]{:S(2)}, u32[]{:S(2)}) collective-permute-start(bf16[80,512]{1,0:T(8,128)(2,1)S(1)} %get-tuple-element.29), channel_id=1, source_target_pairs={{0,4},{4,0},{8,12},{12,8},{16,20},{20,16},{24,28},{28,24},{1,5},{5... | collective-permute-start | bytes 245768 | tf_op jit(solution)/shard_map/ppermute | solution.py:249
  23.4 0.0 collective-permute-done.5.refs_1_
  23.4 1.2 %collective-permute-start.10 = (bf16[80,512]{1,0:T(8,128)(2,1)S(1)}, bf16[80,512]{1,0:T(8,128)(2,1)S(1)}, u32[]{:S(2)}, u32[]{:S(2)}) collective-permute-start(bf16[80,512]{1,0:T(8,128)(2,1)S(1)} %get-tuple-element.30), channel_id=1, source_target_pairs={{0,28},{4,24},{8,20},{12,16},{16,12},{20,8},{24,4},{28,0},{1,29},{... | collective-permute-start | bytes 245768 | tf_op jit(solution)/shard_map/ppermute | solution.py:249
  24.7 0.0 collective-permute-done.6.refs_2_
  24.7 1.5 %collective-permute-done.7.refs_3_ = bf16[80,512]{1,0:T(8,128)(2,1)S(1)} collective-permute-done((bf16[80,512]{1,0:T(8,128)(2,1)S(1)}, bf16[80,512]{1,0:T(8,128)(2,1)S(1)}, u32[]{:S(2)}, u32[]{:S(2)}) %collective-permute-start.7) | collective-permute-done | bytes 81952 | tf_op jit(solution)/shard_map/ppermute | solution.py:249
  26.2 2.7 %collective-permute-done.8.refs_4_ = bf16[80,512]{1,0:T(8,128)(2,1)S(1)} collective-permute-done((bf16[80,512]{1,0:T(8,128)(2,1)S(1)}, bf16[80,512]{1,0:T(8,128)(2,1)S(1)}, u32[]{:S(2)}, u32[]{:S(2)}) %collective-permute-start.8) | collective-permute-done | bytes 81952 | tf_op jit(solution)/shard_map/ppermute | solution.py:249
  28.8 0.0 collective-permute-done.9.refs_5_
  28.8 1.9 %collective-permute-done.10.refs_6_ = bf16[80,512]{1,0:T(8,128)(2,1)S(1)} collective-permute-done((bf16[80,512]{1,0:T(8,128)(2,1)S(1)}, bf16[80,512]{1,0:T(8,128)(2,1)S(1)}, u32[]{:S(2)}, u32[]{:S(2)}) %collective-permute-start.10) | collective-permute-done | bytes 81952 | tf_op jit(solution)/shard_map/ppermute | solution.py:249
  30.7 0.7 %inner_products.1 = (bf16[640,512]{1,0:T(8,128)(2,1)S(1)}, f32[32,4,128]{2,1,0:T(4,128)S(1)}) custom-call(bf16[80,512]{1,0:T(8,128)(2,1)S(1)} %collective-permute-done.4.refs_0_, bf16[80,512]{1,0:T(8,128)(2,1)S(1)} %collective-permute-done.5.refs_1_, bf16[80,512]{1,0:T(8,128)(2,1)S(1)} %collective-permute-done.6.refs_2_, ...), custom_call_target="tpu_custom_call" | custom-call | tf_op jit(solution)/shard_map/inner_products/pallas_call | solution.py:310
  31.4 10.6 %all_to_all.5.shares = f32[32,4,128]{2,1,0:T(4,128)S(1)} all-to-all(f32[32,4,128]{2,1,0:T(4,128)S(1)} %get-tuple-element.32), channel_id=1, replica_groups=mesh['dp'=8,'mp'=4] {'dp','mp'}, dimensions={0} | all-to-all | bytes 131072 | tf_op jit(solution)/shard_map/all_to_all | solution.py:321
  42.0 0.0 copy-done
  42.0 0.0 copy-done.1
  42.0 0.0 copy-done.2
  42.0 2.3 %update.1 = (f32[1,4096]{1,0:T(1,128)}, f32[1,4096]{1,0:T(1,128)}) custom-call(f32[32,4,128]{2,1,0:T(4,128)S(1)} %all_to_all.5.shares, bf16[640,512]{1,0:T(8,128)(2,1)S(1)} %get-tuple-element.33.group, f32[8]{0:T(128)S(1)} %copy-done.2, f32[1,4096]{1,0:T(1,128)S(1)} %copy-done, f32[1,4096]{1,0:T(1,128)S(1)} %copy-done.1), custom_call_target="tpu_custom_call" | custom-call | tf_op jit(solution)/shard_map/update/pallas_call | solution.py:324
  (2 shorter events, 0.0 us)
Async XLA Ops:
  0.6 10.4 %copy-start.3 = (s32[4]{0:T(128)S(1)}, s32[4]{0:T(128)}, u32[]{:S(2)}) copy-start(s32[4]{0:T(128)} %priv_len.1) | copy-start | bytes 52
  3.8 3.1 %collective-permute-start = (f32[16,640]{1,0:T(8,128)S(1)}, f32[16,640]{1,0:T(8,128)S(1)}, u32[]{:S(2)}, u32[]{:S(2)}) collective-permute-start(f32[16,640]{1,0:T(8,128)S(1)} %get-tuple-element.18), channel_id=1, source_target_pairs={{0,1},{1,0},{2,3},{3,2},{4,5},{5,4},{6,7},{7,6},{8,9},{9,8},{10,11... | collective-permute-start | bytes 122888 | tf_op jit(solution)/shard_map/ppermute | solution.py:249
  4.3 4.7 %collective-permute-start.2 = (f32[16,640]{1,0:T(8,128)S(1)}, f32[16,640]{1,0:T(8,128)S(1)}, u32[]{:S(2)}, u32[]{:S(2)}) collective-permute-start(f32[16,640]{1,0:T(8,128)S(1)} %get-tuple-element.19), channel_id=1, source_target_pairs={{0,2},{1,3},{2,0},{3,1},{4,6},{5,7},{6,4},{7,5},{8,10},{9,11},{10,... | collective-permute-start | bytes 122888 | tf_op jit(solution)/shard_map/ppermute | solution.py:249
  6.9 4.1 %collective-permute-start.1 = (f32[16,640]{1,0:T(8,128)S(1)}, f32[16,640]{1,0:T(8,128)S(1)}, u32[]{:S(2)}, u32[]{:S(2)}) collective-permute-start(f32[16,640]{1,0:T(8,128)S(1)} %add.6.rest_0_), channel_id=1, source_target_pairs={{0,2},{1,3},{2,0},{3,1},{4,6},{5,7},{6,4},{7,5},{8,10},{9,11},{10,... | collective-permute-start | bytes 122888 | tf_op jit(solution)/shard_map/ppermute | solution.py:249
  9.1 1.9 %collective-permute-start.3 = (f32[16,640]{1,0:T(8,128)S(1)}, f32[16,640]{1,0:T(8,128)S(1)}, u32[]{:S(2)}, u32[]{:S(2)}) collective-permute-start(f32[16,640]{1,0:T(8,128)S(1)} %add.7.rest_2_), channel_id=1, source_target_pairs={{0,1},{1,0},{2,3},{3,2},{4,5},{5,4},{6,7},{7,6},{8,9},{9,8},{10,11... | collective-permute-start | bytes 122888 | tf_op jit(solution)/shard_map/ppermute | solution.py:249
  11.0 31.0 %copy-start = (f32[1,4096]{1,0:T(1,128)S(1)}, f32[1,4096]{1,0:T(1,128)}, u32[]{:S(2)}) copy-start(f32[1,4096]{1,0:T(1,128)} %down_noise.1) | copy-start | bytes 49156
  11.0 31.0 %copy-start.1 = (f32[1,4096]{1,0:T(1,128)S(1)}, f32[1,4096]{1,0:T(1,128)}, u32[]{:S(2)}) copy-start(f32[1,4096]{1,0:T(1,128)} %up_noise.1) | copy-start | bytes 49156
  11.0 31.0 %copy-start.2 = (f32[8]{0:T(128)S(1)}, f32[8]{0:T(128)}, u32[]{:S(2)}) copy-start(f32[8]{0:T(128)} %noise.1) | copy-start | bytes 100
  12.4 9.5 %collective-permute-start.4 = (bf16[80,512]{1,0:T(8,128)(2,1)S(1)}, bf16[80,512]{1,0:T(8,128)(2,1)S(1)}, u32[]{:S(2)}, u32[]{:S(2)}) collective-permute-start(bf16[80,512]{1,0:T(8,128)(2,1)S(1)} %get-tuple-element.24), channel_id=1, source_target_pairs={{0,24},{4,28},{8,16},{12,20},{16,8},{20,12},{24,0},{28,4},{1,25},{... | collective-permute-start | bytes 245768 | tf_op jit(solution)/shard_map/ppermute | solution.py:249
  16.1 7.4 %collective-permute-start.5 = (bf16[80,512]{1,0:T(8,128)(2,1)S(1)}, bf16[80,512]{1,0:T(8,128)(2,1)S(1)}, u32[]{:S(2)}, u32[]{:S(2)}) collective-permute-start(bf16[80,512]{1,0:T(8,128)(2,1)S(1)} %get-tuple-element.25), channel_id=1, source_target_pairs={{0,8},{4,12},{8,0},{12,4},{16,24},{20,28},{24,16},{28,20},{1,9},{5... | collective-permute-start | bytes 245768 | tf_op jit(solution)/shard_map/ppermute | solution.py:249
  16.1 8.6 %collective-permute-start.6 = (bf16[80,512]{1,0:T(8,128)(2,1)S(1)}, bf16[80,512]{1,0:T(8,128)(2,1)S(1)}, u32[]{:S(2)}, u32[]{:S(2)}) collective-permute-start(bf16[80,512]{1,0:T(8,128)(2,1)S(1)} %get-tuple-element.26), channel_id=1, source_target_pairs={{0,16},{4,20},{8,24},{12,28},{16,0},{20,4},{24,8},{28,12},{1,17},{... | collective-permute-start | bytes 245768 | tf_op jit(solution)/shard_map/ppermute | solution.py:249
  16.8 9.3 %collective-permute-start.7 = (bf16[80,512]{1,0:T(8,128)(2,1)S(1)}, bf16[80,512]{1,0:T(8,128)(2,1)S(1)}, u32[]{:S(2)}, u32[]{:S(2)}) collective-permute-start(bf16[80,512]{1,0:T(8,128)(2,1)S(1)} %get-tuple-element.27), channel_id=1, source_target_pairs={{0,12},{4,8},{8,4},{12,0},{16,28},{20,24},{24,20},{28,16},{1,13},{... | collective-permute-start | bytes 245768 | tf_op jit(solution)/shard_map/ppermute | solution.py:249
  19.0 9.8 %collective-permute-start.8 = (bf16[80,512]{1,0:T(8,128)(2,1)S(1)}, bf16[80,512]{1,0:T(8,128)(2,1)S(1)}, u32[]{:S(2)}, u32[]{:S(2)}) collective-permute-start(bf16[80,512]{1,0:T(8,128)(2,1)S(1)} %get-tuple-element.28), channel_id=1, source_target_pairs={{0,20},{4,16},{8,28},{12,24},{16,4},{20,0},{24,12},{28,8},{1,21},{... | collective-permute-start | bytes 245768 | tf_op jit(solution)/shard_map/ppermute | solution.py:249
  21.9 6.9 %collective-permute-start.9 = (bf16[80,512]{1,0:T(8,128)(2,1)S(1)}, bf16[80,512]{1,0:T(8,128)(2,1)S(1)}, u32[]{:S(2)}, u32[]{:S(2)}) collective-permute-start(bf16[80,512]{1,0:T(8,128)(2,1)S(1)} %get-tuple-element.29), channel_id=1, source_target_pairs={{0,4},{4,0},{8,12},{12,8},{16,20},{20,16},{24,28},{28,24},{1,5},{5... | collective-permute-start | bytes 245768 | tf_op jit(solution)/shard_map/ppermute | solution.py:249
  23.4 7.2 %collective-permute-start.10 = (bf16[80,512]{1,0:T(8,128)(2,1)S(1)}, bf16[80,512]{1,0:T(8,128)(2,1)S(1)}, u32[]{:S(2)}, u32[]{:S(2)}) collective-permute-start(bf16[80,512]{1,0:T(8,128)(2,1)S(1)} %get-tuple-element.30), channel_id=1, source_target_pairs={{0,28},{4,24},{8,20},{12,16},{16,12},{20,8},{24,4},{28,0},{1,29},{... | collective-permute-start | bytes 245768 | tf_op jit(solution)/shard_map/ppermute | solution.py:249

commit v9 on v8

--- a/solution.py
+++ b/solution.py
@@ -93,25 +93,25 @@
                 jnp.where(live, own[:, at] + other[:, at], 0.0).astype(jnp.bfloat16)
                 for own, other in (returned, projected)
             )
+            up_whole = dot(up_live, cotangents[e], FIRST_LAST)
             down_whole = dot(down_live, inputs[e], FIRST_LAST)
-            up_whole = dot(up_live, cotangents[e], FIRST_LAST)
             for c in range(dp):
                 features = slice(c * lanes, (c + 1) * lanes)
                 at = slice(c * rank, (c + 1) * rank)
                 down_part = down_whole[:, features]
                 up_part = up_whole[:, features]
-                down_rows[at, :] = down_part.astype(jnp.bfloat16)
+                down_rows[slot % 2, at, :] = down_part.astype(jnp.bfloat16)
                 for h in range(lanes // LANES):
-                    up_rows[h, at, :] = up_part[:, h * LANES : (h + 1) * LANES]
+                    up_rows[slot % 2, h, at, :] = up_part[:, h * LANES : (h + 1) * LANES]
             for k in range(dp):
                 to = me ^ k
                 rows = slice(slot * rank, (slot + 1) * rank)
                 blocks[k][rows, :lanes] = down_rows[
-                    pl.ds(pl.multiple_of(to * rank, rank), rank), :
+                    slot % 2, pl.ds(pl.multiple_of(to * rank, rank), rank), :
                 ]
                 for h in range(lanes // LANES):
                     pieces = [
-                        up_rows[h, pl.ds(to * per + r, dp, stride=rank), :] for r in range(per)
+                        up_rows[slot % 2, h, pl.ds(to * per + r, dp, stride=rank), :] for r in range(per)
                     ]
                     start = lanes + h * LANES
                     blocks[k][rows, start : start + LANES] = jnp.concatenate(
@@ -296,8 +296,8 @@
         in_specs=[SMEM] * 2 + [VMEM] * 8,
         out_specs=[VMEM] * dp,
         scratch_shapes=[
-            pltpu.VMEM((dp * rank, lanes), bf16),
-            pltpu.VMEM((lanes // LANES, dp * rank, LANES), f32),
+            pltpu.VMEM((2, dp * rank, lanes), bf16),
+            pltpu.VMEM((2, lanes // LANES, dp * rank, LANES), f32),
         ],
         compiler_params=PARAMS,
         name="gradients",

time: 44.4 us -> 44.4 us (level)
  no operation moved by 1% of the time
where the time goes in v9:
time: 44.4 us; the launch traced here: 44.2 us
  starting transfers between devices  16.5 us (37%)
  blocking collectives  10.6 us (24%)
  waiting for transfers between devices  8.29 us (19%)
  Pallas kernels  7.5 us (17%)
  between operations  1.35 us (3%)
    ppermute x11, starting transfers between devices, exchange(): lax.ppermute(x, axis, [(s, s ^ step) for s in range(lax.axis_size(axis))])  16.5 us
    all_to_all x1, blocking collectives, small_group(): shares = lax.all_to_all(shares, ('dp', 'mp'), 0, 0, tiled=True)  10.6 us
    ppermute x11, waiting for transfers between devices, exchange(): lax.ppermute(x, axis, [(s, s ^ step) for s in range(lax.axis_size(axis))])  8.29 us
    pallas_call x1, Pallas kernels, small_group(): pl.pallas_call(project_kernel, out_shape=[jax.ShapeDtypeStruct((rank, exa...  3.18 us
    pallas_call x1, Pallas kernels, small_group(): pl.pallas_call(functools.partial(update_kernel, gain), out_shape=[jax.Sha...  2.27 us
    pallas_call x1, Pallas kernels, small_group(): pl.pallas_call(functools.partial(gradient_kernel, dp), out_shape=[block]...  1.32 us
  transfers between devices with their start and end apart: 11, of which 5 were waited for; matrix products, arithmetic and copies ran while one was open for 0% of the time, Pallas kernels for 0%

profile of v9, /device:TPU:0, one launch (start us, length us, event | category | flops | bytes accessed | tf_op | source)
XLA Modules:
  0.0 44.2 jit_solution(18438178923689006157)
XLA Ops:
  0.6 0.0 copy-start.3
  0.6 3.2 %project.1 = (f32[16,640]{1,0:T(8,128)S(1)}, f32[16,640]{1,0:T(8,128)S(1)}, bf16[1,112,2048]{2,1,0:T(8,128)(2,1)S(1)}, bf16[1,112,2048]{2,1,0:T(8,128)(2,1)S(1)}...) custom-call(bf16[1,112,2048]{2,1,0:T(8,128)(2,1)} %pub_in.1, bf16[1,112,2048]{2,1,0:T(8,128)(2,1)} %pub_out.1, ...), custom_call_target="tpu_custom_call" | custom-call | tf_op jit(solution)/shard_map/project/pallas_call | solution.py:269
  3.8 0.5 %collective-permute-start = (f32[16,640]{1,0:T(8,128)S(1)}, f32[16,640]{1,0:T(8,128)S(1)}, u32[]{:S(2)}, u32[]{:S(2)}) collective-permute-start(f32[16,640]{1,0:T(8,128)S(1)} %get-tuple-element.18), channel_id=1, source_target_pairs={{0,1},{1,0},{2,3},{3,2},{4,5},{5,4},{6,7},{7,6},{8,9},{9,8},{10,11... | collective-permute-start | bytes 122888 | tf_op jit(solution)/shard_map/ppermute | solution.py:249
  4.3 2.6 %collective-permute-start.2 = (f32[16,640]{1,0:T(8,128)S(1)}, f32[16,640]{1,0:T(8,128)S(1)}, u32[]{:S(2)}, u32[]{:S(2)}) collective-permute-start(f32[16,640]{1,0:T(8,128)S(1)} %get-tuple-element.19), channel_id=1, source_target_pairs={{0,2},{1,3},{2,0},{3,1},{4,6},{5,7},{6,4},{7,5},{8,10},{9,11},{10,... | collective-permute-start | bytes 122888 | tf_op jit(solution)/shard_map/ppermute | solution.py:249
  6.9 0.0 collective-permute-done
  6.9 1.1 %collective-permute-start.1 = (f32[16,640]{1,0:T(8,128)S(1)}, f32[16,640]{1,0:T(8,128)S(1)}, u32[]{:S(2)}, u32[]{:S(2)}) collective-permute-start(f32[16,640]{1,0:T(8,128)S(1)} %add.6.rest_0_), channel_id=1, source_target_pairs={{0,2},{1,3},{2,0},{3,1},{4,6},{5,7},{6,4},{7,5},{8,10},{9,11},{10,... | collective-permute-start | bytes 122888 | tf_op jit(solution)/shard_map/ppermute | solution.py:249
  8.1 1.0 %collective-permute-done.2 = f32[16,640]{1,0:T(8,128)S(1)} collective-permute-done((f32[16,640]{1,0:T(8,128)S(1)}, f32[16,640]{1,0:T(8,128)S(1)}, u32[]{:S(2)}, u32[]{:S(2)}) %collective-permute-start.2) | collective-permute-done | bytes 40992 | tf_op jit(solution)/shard_map/ppermute | solution.py:249
  9.1 0.0 collective-permute-start.3
  9.7 1.3 %collective-permute-done.1.rest_1_ = f32[16,640]{1,0:T(8,128)S(1)} collective-permute-done((f32[16,640]{1,0:T(8,128)S(1)}, f32[16,640]{1,0:T(8,128)S(1)}, u32[]{:S(2)}, u32[]{:S(2)}) %collective-permute-start.1) | collective-permute-done | bytes 40992 | tf_op jit(solution)/shard_map/ppermute | solution.py:249
  11.0 0.0 collective-permute-done.3.rest_3_
  11.0 0.0 copy-done.3
  11.0 0.0 copy-start
  11.0 0.0 copy-start.1
  11.0 0.0 copy-start.2
  11.0 1.3 %gradients.1 = (bf16[80,512]{1,0:T(8,128)(2,1)S(1)}, bf16[80,512]{1,0:T(8,128)(2,1)S(1)}, bf16[80,512]{1,0:T(8,128)(2,1)S(1)}, bf16[80,512]{1,0:T(8,128)(2,1)S(1...) custom-call(s32[1]{0:T(128)S(6)} %copy.13.pub_len, ...), custom_call_target="tpu_custom_call" | custom-call | tf_op jit(solution)/shard_map/gradients/pallas_call | solution.py:293
  12.3 3.7 %collective-permute-start.4 = (bf16[80,512]{1,0:T(8,128)(2,1)S(1)}, bf16[80,512]{1,0:T(8,128)(2,1)S(1)}, u32[]{:S(2)}, u32[]{:S(2)}) collective-permute-start(bf16[80,512]{1,0:T(8,128)(2,1)S(1)} %get-tuple-element.24), channel_id=1, source_target_pairs={{0,24},{4,28},{8,16},{12,20},{16,8},{20,12},{24,0},{28,4},{1,25},{... | collective-permute-start | bytes 245768 | tf_op jit(solution)/shard_map/ppermute | solution.py:249
  16.0 0.0 collective-permute-start.5
  16.0 0.8 %collective-permute-start.6 = (bf16[80,512]{1,0:T(8,128)(2,1)S(1)}, bf16[80,512]{1,0:T(8,128)(2,1)S(1)}, u32[]{:S(2)}, u32[]{:S(2)}) collective-permute-start(bf16[80,512]{1,0:T(8,128)(2,1)S(1)} %get-tuple-element.26), channel_id=1, source_target_pairs={{0,16},{4,20},{8,24},{12,28},{16,0},{20,4},{24,8},{28,12},{1,17},{... | collective-permute-start | bytes 245768 | tf_op jit(solution)/shard_map/ppermute | solution.py:249
  16.8 2.2 %collective-permute-start.7 = (bf16[80,512]{1,0:T(8,128)(2,1)S(1)}, bf16[80,512]{1,0:T(8,128)(2,1)S(1)}, u32[]{:S(2)}, u32[]{:S(2)}) collective-permute-start(bf16[80,512]{1,0:T(8,128)(2,1)S(1)} %get-tuple-element.27), channel_id=1, source_target_pairs={{0,12},{4,8},{8,4},{12,0},{16,28},{20,24},{24,20},{28,16},{1,13},{... | collective-permute-start | bytes 245768 | tf_op jit(solution)/shard_map/ppermute | solution.py:249
  19.0 2.9 %collective-permute-start.8 = (bf16[80,512]{1,0:T(8,128)(2,1)S(1)}, bf16[80,512]{1,0:T(8,128)(2,1)S(1)}, u32[]{:S(2)}, u32[]{:S(2)}) collective-permute-start(bf16[80,512]{1,0:T(8,128)(2,1)S(1)} %get-tuple-element.28), channel_id=1, source_target_pairs={{0,20},{4,16},{8,28},{12,24},{16,4},{20,0},{24,12},{28,8},{1,21},{... | collective-permute-start | bytes 245768 | tf_op jit(solution)/shard_map/ppermute | solution.py:249
  21.9 0.0 collective-permute-done.4.refs_0_
  21.9 1.5 %collective-permute-start.9 = (bf16[80,512]{1,0:T(8,128)(2,1)S(1)}, bf16[80,512]{1,0:T(8,128)(2,1)S(1)}, u32[]{:S(2)}, u32[]{:S(2)}) collective-permute-start(bf16[80,512]{1,0:T(8,128)(2,1)S(1)} %get-tuple-element.29), channel_id=1, source_target_pairs={{0,4},{4,0},{8,12},{12,8},{16,20},{20,16},{24,28},{28,24},{1,5},{5... | collective-permute-start | bytes 245768 | tf_op jit(solution)/shard_map/ppermute | solution.py:249
  23.4 0.0 collective-permute-done.5.refs_1_
  23.4 1.2 %collective-permute-start.10 = (bf16[80,512]{1,0:T(8,128)(2,1)S(1)}, bf16[80,512]{1,0:T(8,128)(2,1)S(1)}, u32[]{:S(2)}, u32[]{:S(2)}) collective-permute-start(bf16[80,512]{1,0:T(8,128)(2,1)S(1)} %get-tuple-element.30), channel_id=1, source_target_pairs={{0,28},{4,24},{8,20},{12,16},{16,12},{20,8},{24,4},{28,0},{1,29},{... | collective-permute-start | bytes 245768 | tf_op jit(solution)/shard_map/ppermute | solution.py:249
  24.6 0.0 collective-permute-done.6.refs_2_
  24.6 1.5 %collective-permute-done.7.refs_3_ = bf16[80,512]{1,0:T(8,128)(2,1)S(1)} collective-permute-done((bf16[80,512]{1,0:T(8,128)(2,1)S(1)}, bf16[80,512]{1,0:T(8,128)(2,1)S(1)}, u32[]{:S(2)}, u32[]{:S(2)}) %collective-permute-start.7) | collective-permute-done | bytes 81952 | tf_op jit(solution)/shard_map/ppermute | solution.py:249
  26.1 2.6 %collective-permute-done.8.refs_4_ = bf16[80,512]{1,0:T(8,128)(2,1)S(1)} collective-permute-done((bf16[80,512]{1,0:T(8,128)(2,1)S(1)}, bf16[80,512]{1,0:T(8,128)(2,1)S(1)}, u32[]{:S(2)}, u32[]{:S(2)}) %collective-permute-start.8) | collective-permute-done | bytes 81952 | tf_op jit(solution)/shard_map/ppermute | solution.py:249
  28.8 0.0 collective-permute-done.9.refs_5_
  28.8 1.9 %collective-permute-done.10.refs_6_ = bf16[80,512]{1,0:T(8,128)(2,1)S(1)} collective-permute-done((bf16[80,512]{1,0:T(8,128)(2,1)S(1)}, bf16[80,512]{1,0:T(8,128)(2,1)S(1)}, u32[]{:S(2)}, u32[]{:S(2)}) %collective-permute-start.10) | collective-permute-done | bytes 81952 | tf_op jit(solution)/shard_map/ppermute | solution.py:249
  30.6 0.7 %inner_products.1 = (bf16[640,512]{1,0:T(8,128)(2,1)S(1)}, f32[32,4,128]{2,1,0:T(4,128)S(1)}) custom-call(bf16[80,512]{1,0:T(8,128)(2,1)S(1)} %collective-permute-done.4.refs_0_, bf16[80,512]{1,0:T(8,128)(2,1)S(1)} %collective-permute-done.5.refs_1_, bf16[80,512]{1,0:T(8,128)(2,1)S(1)} %collective-permute-done.6.refs_2_, ...), custom_call_target="tpu_custom_call" | custom-call | tf_op jit(solution)/shard_map/inner_products/pallas_call | solution.py:310
  31.4 10.6 %all_to_all.5.shares = f32[32,4,128]{2,1,0:T(4,128)S(1)} all-to-all(f32[32,4,128]{2,1,0:T(4,128)S(1)} %get-tuple-element.32), channel_id=1, replica_groups=mesh['dp'=8,'mp'=4] {'dp','mp'}, dimensions={0} | all-to-all | bytes 131072 | tf_op jit(solution)/shard_map/all_to_all | solution.py:321
  41.9 0.0 copy-done
  41.9 0.0 copy-done.1
  41.9 0.0 copy-done.2
  41.9 2.3 %update.1 = (f32[1,4096]{1,0:T(1,128)}, f32[1,4096]{1,0:T(1,128)}) custom-call(f32[32,4,128]{2,1,0:T(4,128)S(1)} %all_to_all.5.shares, bf16[640,512]{1,0:T(8,128)(2,1)S(1)} %get-tuple-element.33.group, f32[8]{0:T(128)S(1)} %copy-done.2, f32[1,4096]{1,0:T(1,128)S(1)} %copy-done, f32[1,4096]{1,0:T(1,128)S(1)} %copy-done.1), custom_call_target="tpu_custom_call" | custom-call | tf_op jit(solution)/shard_map/update/pallas_call | solution.py:324
  (2 shorter events, 0.0 us)
Async XLA Ops:
  0.6 10.4 %copy-start.3 = (s32[4]{0:T(128)S(1)}, s32[4]{0:T(128)}, u32[]{:S(2)}) copy-start(s32[4]{0:T(128)} %priv_len.1) | copy-start | bytes 52
  3.8 3.1 %collective-permute-start = (f32[16,640]{1,0:T(8,128)S(1)}, f32[16,640]{1,0:T(8,128)S(1)}, u32[]{:S(2)}, u32[]{:S(2)}) collective-permute-start(f32[16,640]{1,0:T(8,128)S(1)} %get-tuple-element.18), channel_id=1, source_target_pairs={{0,1},{1,0},{2,3},{3,2},{4,5},{5,4},{6,7},{7,6},{8,9},{9,8},{10,11... | collective-permute-start | bytes 122888 | tf_op jit(solution)/shard_map/ppermute | solution.py:249
  4.3 4.7 %collective-permute-start.2 = (f32[16,640]{1,0:T(8,128)S(1)}, f32[16,640]{1,0:T(8,128)S(1)}, u32[]{:S(2)}, u32[]{:S(2)}) collective-permute-start(f32[16,640]{1,0:T(8,128)S(1)} %get-tuple-element.19), channel_id=1, source_target_pairs={{0,2},{1,3},{2,0},{3,1},{4,6},{5,7},{6,4},{7,5},{8,10},{9,11},{10,... | collective-permute-start | bytes 122888 | tf_op jit(solution)/shard_map/ppermute | solution.py:249
  6.9 4.1 %collective-permute-start.1 = (f32[16,640]{1,0:T(8,128)S(1)}, f32[16,640]{1,0:T(8,128)S(1)}, u32[]{:S(2)}, u32[]{:S(2)}) collective-permute-start(f32[16,640]{1,0:T(8,128)S(1)} %add.6.rest_0_), channel_id=1, source_target_pairs={{0,2},{1,3},{2,0},{3,1},{4,6},{5,7},{6,4},{7,5},{8,10},{9,11},{10,... | collective-permute-start | bytes 122888 | tf_op jit(solution)/shard_map/ppermute | solution.py:249
  9.1 1.9 %collective-permute-start.3 = (f32[16,640]{1,0:T(8,128)S(1)}, f32[16,640]{1,0:T(8,128)S(1)}, u32[]{:S(2)}, u32[]{:S(2)}) collective-permute-start(f32[16,640]{1,0:T(8,128)S(1)} %add.7.rest_2_), channel_id=1, source_target_pairs={{0,1},{1,0},{2,3},{3,2},{4,5},{5,4},{6,7},{7,6},{8,9},{9,8},{10,11... | collective-permute-start | bytes 122888 | tf_op jit(solution)/shard_map/ppermute | solution.py:249
  11.0 30.9 %copy-start = (f32[1,4096]{1,0:T(1,128)S(1)}, f32[1,4096]{1,0:T(1,128)}, u32[]{:S(2)}) copy-start(f32[1,4096]{1,0:T(1,128)} %down_noise.1) | copy-start | bytes 49156
  11.0 30.9 %copy-start.1 = (f32[1,4096]{1,0:T(1,128)S(1)}, f32[1,4096]{1,0:T(1,128)}, u32[]{:S(2)}) copy-start(f32[1,4096]{1,0:T(1,128)} %up_noise.1) | copy-start | bytes 49156
  11.0 30.9 %copy-start.2 = (f32[8]{0:T(128)S(1)}, f32[8]{0:T(128)}, u32[]{:S(2)}) copy-start(f32[8]{0:T(128)} %noise.1) | copy-start | bytes 100
  12.3 9.5 %collective-permute-start.4 = (bf16[80,512]{1,0:T(8,128)(2,1)S(1)}, bf16[80,512]{1,0:T(8,128)(2,1)S(1)}, u32[]{:S(2)}, u32[]{:S(2)}) collective-permute-start(bf16[80,512]{1,0:T(8,128)(2,1)S(1)} %get-tuple-element.24), channel_id=1, source_target_pairs={{0,24},{4,28},{8,16},{12,20},{16,8},{20,12},{24,0},{28,4},{1,25},{... | collective-permute-start | bytes 245768 | tf_op jit(solution)/shard_map/ppermute | solution.py:249
  16.0 7.4 %collective-permute-start.5 = (bf16[80,512]{1,0:T(8,128)(2,1)S(1)}, bf16[80,512]{1,0:T(8,128)(2,1)S(1)}, u32[]{:S(2)}, u32[]{:S(2)}) collective-permute-start(bf16[80,512]{1,0:T(8,128)(2,1)S(1)} %get-tuple-element.25), channel_id=1, source_target_pairs={{0,8},{4,12},{8,0},{12,4},{16,24},{20,28},{24,16},{28,20},{1,9},{5... | collective-permute-start | bytes 245768 | tf_op jit(solution)/shard_map/ppermute | solution.py:249
  16.0 8.6 %collective-permute-start.6 = (bf16[80,512]{1,0:T(8,128)(2,1)S(1)}, bf16[80,512]{1,0:T(8,128)(2,1)S(1)}, u32[]{:S(2)}, u32[]{:S(2)}) collective-permute-start(bf16[80,512]{1,0:T(8,128)(2,1)S(1)} %get-tuple-element.26), channel_id=1, source_target_pairs={{0,16},{4,20},{8,24},{12,28},{16,0},{20,4},{24,8},{28,12},{1,17},{... | collective-permute-start | bytes 245768 | tf_op jit(solution)/shard_map/ppermute | solution.py:249
  16.8 9.3 %collective-permute-start.7 = (bf16[80,512]{1,0:T(8,128)(2,1)S(1)}, bf16[80,512]{1,0:T(8,128)(2,1)S(1)}, u32[]{:S(2)}, u32[]{:S(2)}) collective-permute-start(bf16[80,512]{1,0:T(8,128)(2,1)S(1)} %get-tuple-element.27), channel_id=1, source_target_pairs={{0,12},{4,8},{8,4},{12,0},{16,28},{20,24},{24,20},{28,16},{1,13},{... | collective-permute-start | bytes 245768 | tf_op jit(solution)/shard_map/ppermute | solution.py:249
  19.0 9.8 %collective-permute-start.8 = (bf16[80,512]{1,0:T(8,128)(2,1)S(1)}, bf16[80,512]{1,0:T(8,128)(2,1)S(1)}, u32[]{:S(2)}, u32[]{:S(2)}) collective-permute-start(bf16[80,512]{1,0:T(8,128)(2,1)S(1)} %get-tuple-element.28), channel_id=1, source_target_pairs={{0,20},{4,16},{8,28},{12,24},{16,4},{20,0},{24,12},{28,8},{1,21},{... | collective-permute-start | bytes 245768 | tf_op jit(solution)/shard_map/ppermute | solution.py:249
  21.9 6.9 %collective-permute-start.9 = (bf16[80,512]{1,0:T(8,128)(2,1)S(1)}, bf16[80,512]{1,0:T(8,128)(2,1)S(1)}, u32[]{:S(2)}, u32[]{:S(2)}) collective-permute-start(bf16[80,512]{1,0:T(8,128)(2,1)S(1)} %get-tuple-element.29), channel_id=1, source_target_pairs={{0,4},{4,0},{8,12},{12,8},{16,20},{20,16},{24,28},{28,24},{1,5},{5... | collective-permute-start | bytes 245768 | tf_op jit(solution)/shard_map/ppermute | solution.py:249
  23.4 7.2 %collective-permute-start.10 = (bf16[80,512]{1,0:T(8,128)(2,1)S(1)}, bf16[80,512]{1,0:T(8,128)(2,1)S(1)}, u32[]{:S(2)}, u32[]{:S(2)}) collective-permute-start(bf16[80,512]{1,0:T(8,128)(2,1)S(1)} %get-tuple-element.30), channel_id=1, source_target_pairs={{0,28},{4,24},{8,20},{12,16},{16,12},{20,8},{24,4},{28,0},{1,29},{... | collective-permute-start | bytes 245768 | tf_op jit(solution)/shard_map/ppermute | solution.py:249

commit v10 on v9

--- a/solution.py
+++ b/solution.py
@@ -223,13 +223,13 @@
     target = correction + SIGMA_COEF * coefficient_limit * noise_column
     inverse_factor = jnp.where(lane >= half, work, 0.0)
     anchor = pltpu.roll(jnp.sum(inverse_factor * target, axis=0, keepdims=True), half, 1)
-    weights = jnp.where(lane[0:1] < publics, anchor, keep_residual)
+    weights = jnp.where(lane[0:1] < publics, anchor, keep_residual) * gain
 
     rank, lanes = rows, group.shape[1] // 2
     acc = jnp.zeros((rows, 2 * lanes), jnp.float32)
     for i in range(examples):
         acc = acc + weights[:, i : i + 1] * group[i * rows : (i + 1) * rows, :].astype(jnp.float32)
-    scale = SIGMA_RESIDUAL * residual_limit
+    scale = (SIGMA_RESIDUAL * gain) * residual_limit
     per = LANES // rank
     flat = lanes * rank // LANES
     wide = jnp.concatenate([acc[:, :lanes]] * per, axis=0)
@@ -239,10 +239,10 @@
     turned = parts[:, :LANES] + parts[:, LANES : 2 * LANES] + parts[:, 2 * LANES :]
     for a in range(flat):
         at = slice(a * LANES, (a + 1) * LANES)
-        down[0:1, at] = (turned[a : a + 1] + scale * down_noise[0:1, at]) * gain
+        down[0:1, at] = turned[a : a + 1] + scale * down_noise[0:1, at]
     for a in range(rank):
         at = slice(a * lanes, (a + 1) * lanes)
-        up[0:1, at] = (acc[a : a + 1, lanes:] + scale * up_noise[0:1, at]) * gain
+        up[0:1, at] = acc[a : a + 1, lanes:] + scale * up_noise[0:1, at]
 
 
 def exchange(x, axis, step):

time: 44.4 us -> 44.4 us (level)
  no operation moved by 1% of the time
where the time goes in v10:
time: 44.4 us; the launch traced here: 44.2 us
  starting transfers between devices  16.5 us (37%)
  blocking collectives  10.6 us (24%)
  waiting for transfers between devices  8.29 us (19%)
  Pallas kernels  7.49 us (17%)
  between operations  1.35 us (3%)
    ppermute x11, starting transfers between devices, exchange(): lax.ppermute(x, axis, [(s, s ^ step) for s in range(lax.axis_size(axis))])  16.5 us
    all_to_all x1, blocking collectives, small_group(): shares = lax.all_to_all(shares, ('dp', 'mp'), 0, 0, tiled=True)  10.6 us
    ppermute x11, waiting for transfers between devices, exchange(): lax.ppermute(x, axis, [(s, s ^ step) for s in range(lax.axis_size(axis))])  8.29 us
    pallas_call x1, Pallas kernels, small_group(): pl.pallas_call(project_kernel, out_shape=[jax.ShapeDtypeStruct((rank, exa...  3.18 us
    pallas_call x1, Pallas kernels, small_group(): pl.pallas_call(functools.partial(update_kernel, gain), out_shape=[jax.Sha...  2.26 us
    pallas_call x1, Pallas kernels, small_group(): pl.pallas_call(functools.partial(gradient_kernel, dp), out_shape=[block]...  1.32 us
  transfers between devices with their start and end apart: 11, of which 5 were waited for; matrix products, arithmetic and copies ran while one was open for 0% of the time, Pallas kernels for 0%

profile of v10, /device:TPU:0, one launch (start us, length us, event | category | flops | bytes accessed | tf_op | source)
XLA Modules:
  0.0 44.2 jit_solution(11935866795456011593)
XLA Ops:
  0.6 0.0 copy-start.3
  0.6 3.2 %project.1 = (f32[16,640]{1,0:T(8,128)S(1)}, f32[16,640]{1,0:T(8,128)S(1)}, bf16[1,112,2048]{2,1,0:T(8,128)(2,1)S(1)}, bf16[1,112,2048]{2,1,0:T(8,128)(2,1)S(1)}...) custom-call(bf16[1,112,2048]{2,1,0:T(8,128)(2,1)} %pub_in.1, bf16[1,112,2048]{2,1,0:T(8,128)(2,1)} %pub_out.1, ...), custom_call_target="tpu_custom_call" | custom-call | tf_op jit(solution)/shard_map/project/pallas_call | solution.py:269
  3.8 0.5 %collective-permute-start = (f32[16,640]{1,0:T(8,128)S(1)}, f32[16,640]{1,0:T(8,128)S(1)}, u32[]{:S(2)}, u32[]{:S(2)}) collective-permute-start(f32[16,640]{1,0:T(8,128)S(1)} %get-tuple-element.18), channel_id=1, source_target_pairs={{0,1},{1,0},{2,3},{3,2},{4,5},{5,4},{6,7},{7,6},{8,9},{9,8},{10,11... | collective-permute-start | bytes 122888 | tf_op jit(solution)/shard_map/ppermute | solution.py:249
  4.3 2.6 %collective-permute-start.2 = (f32[16,640]{1,0:T(8,128)S(1)}, f32[16,640]{1,0:T(8,128)S(1)}, u32[]{:S(2)}, u32[]{:S(2)}) collective-permute-start(f32[16,640]{1,0:T(8,128)S(1)} %get-tuple-element.19), channel_id=1, source_target_pairs={{0,2},{1,3},{2,0},{3,1},{4,6},{5,7},{6,4},{7,5},{8,10},{9,11},{10,... | collective-permute-start | bytes 122888 | tf_op jit(solution)/shard_map/ppermute | solution.py:249
  6.9 0.0 collective-permute-done
  6.9 1.1 %collective-permute-start.1 = (f32[16,640]{1,0:T(8,128)S(1)}, f32[16,640]{1,0:T(8,128)S(1)}, u32[]{:S(2)}, u32[]{:S(2)}) collective-permute-start(f32[16,640]{1,0:T(8,128)S(1)} %add.6.rest_0_), channel_id=1, source_target_pairs={{0,2},{1,3},{2,0},{3,1},{4,6},{5,7},{6,4},{7,5},{8,10},{9,11},{10,... | collective-permute-start | bytes 122888 | tf_op jit(solution)/shard_map/ppermute | solution.py:249
  8.1 1.0 %collective-permute-done.2 = f32[16,640]{1,0:T(8,128)S(1)} collective-permute-done((f32[16,640]{1,0:T(8,128)S(1)}, f32[16,640]{1,0:T(8,128)S(1)}, u32[]{:S(2)}, u32[]{:S(2)}) %collective-permute-start.2) | collective-permute-done | bytes 40992 | tf_op jit(solution)/shard_map/ppermute | solution.py:249
  9.1 0.0 collective-permute-start.3
  9.7 1.3 %collective-permute-done.1.rest_1_ = f32[16,640]{1,0:T(8,128)S(1)} collective-permute-done((f32[16,640]{1,0:T(8,128)S(1)}, f32[16,640]{1,0:T(8,128)S(1)}, u32[]{:S(2)}, u32[]{:S(2)}) %collective-permute-start.1) | collective-permute-done | bytes 40992 | tf_op jit(solution)/shard_map/ppermute | solution.py:249
  11.0 0.0 collective-permute-done.3.rest_3_
  11.0 0.0 copy-done.3
  11.0 0.0 copy-start
  11.0 0.0 copy-start.1
  11.0 0.0 copy-start.2
  11.0 1.3 %gradients.1 = (bf16[80,512]{1,0:T(8,128)(2,1)S(1)}, bf16[80,512]{1,0:T(8,128)(2,1)S(1)}, bf16[80,512]{1,0:T(8,128)(2,1)S(1)}, bf16[80,512]{1,0:T(8,128)(2,1)S(1...) custom-call(s32[1]{0:T(128)S(6)} %copy.13.pub_len, ...), custom_call_target="tpu_custom_call" | custom-call | tf_op jit(solution)/shard_map/gradients/pallas_call | solution.py:293
  12.3 3.7 %collective-permute-start.4 = (bf16[80,512]{1,0:T(8,128)(2,1)S(1)}, bf16[80,512]{1,0:T(8,128)(2,1)S(1)}, u32[]{:S(2)}, u32[]{:S(2)}) collective-permute-start(bf16[80,512]{1,0:T(8,128)(2,1)S(1)} %get-tuple-element.24), channel_id=1, source_target_pairs={{0,24},{4,28},{8,16},{12,20},{16,8},{20,12},{24,0},{28,4},{1,25},{... | collective-permute-start | bytes 245768 | tf_op jit(solution)/shard_map/ppermute | solution.py:249
  16.0 0.0 collective-permute-start.5
  16.0 0.8 %collective-permute-start.6 = (bf16[80,512]{1,0:T(8,128)(2,1)S(1)}, bf16[80,512]{1,0:T(8,128)(2,1)S(1)}, u32[]{:S(2)}, u32[]{:S(2)}) collective-permute-start(bf16[80,512]{1,0:T(8,128)(2,1)S(1)} %get-tuple-element.26), channel_id=1, source_target_pairs={{0,16},{4,20},{8,24},{12,28},{16,0},{20,4},{24,8},{28,12},{1,17},{... | collective-permute-start | bytes 245768 | tf_op jit(solution)/shard_map/ppermute | solution.py:249
  16.8 2.2 %collective-permute-start.7 = (bf16[80,512]{1,0:T(8,128)(2,1)S(1)}, bf16[80,512]{1,0:T(8,128)(2,1)S(1)}, u32[]{:S(2)}, u32[]{:S(2)}) collective-permute-start(bf16[80,512]{1,0:T(8,128)(2,1)S(1)} %get-tuple-element.27), channel_id=1, source_target_pairs={{0,12},{4,8},{8,4},{12,0},{16,28},{20,24},{24,20},{28,16},{1,13},{... | collective-permute-start | bytes 245768 | tf_op jit(solution)/shard_map/ppermute | solution.py:249
  19.0 2.9 %collective-permute-start.8 = (bf16[80,512]{1,0:T(8,128)(2,1)S(1)}, bf16[80,512]{1,0:T(8,128)(2,1)S(1)}, u32[]{:S(2)}, u32[]{:S(2)}) collective-permute-start(bf16[80,512]{1,0:T(8,128)(2,1)S(1)} %get-tuple-element.28), channel_id=1, source_target_pairs={{0,20},{4,16},{8,28},{12,24},{16,4},{20,0},{24,12},{28,8},{1,21},{... | collective-permute-start | bytes 245768 | tf_op jit(solution)/shard_map/ppermute | solution.py:249
  21.9 0.0 collective-permute-done.4.refs_0_
  21.9 1.5 %collective-permute-start.9 = (bf16[80,512]{1,0:T(8,128)(2,1)S(1)}, bf16[80,512]{1,0:T(8,128)(2,1)S(1)}, u32[]{:S(2)}, u32[]{:S(2)}) collective-permute-start(bf16[80,512]{1,0:T(8,128)(2,1)S(1)} %get-tuple-element.29), channel_id=1, source_target_pairs={{0,4},{4,0},{8,12},{12,8},{16,20},{20,16},{24,28},{28,24},{1,5},{5... | collective-permute-start | bytes 245768 | tf_op jit(solution)/shard_map/ppermute | solution.py:249
  23.4 0.0 collective-permute-done.5.refs_1_
  23.4 1.2 %collective-permute-start.10 = (bf16[80,512]{1,0:T(8,128)(2,1)S(1)}, bf16[80,512]{1,0:T(8,128)(2,1)S(1)}, u32[]{:S(2)}, u32[]{:S(2)}) collective-permute-start(bf16[80,512]{1,0:T(8,128)(2,1)S(1)} %get-tuple-element.30), channel_id=1, source_target_pairs={{0,28},{4,24},{8,20},{12,16},{16,12},{20,8},{24,4},{28,0},{1,29},{... | collective-permute-start | bytes 245768 | tf_op jit(solution)/shard_map/ppermute | solution.py:249
  24.6 0.0 collective-permute-done.6.refs_2_
  24.6 1.5 %collective-permute-done.7.refs_3_ = bf16[80,512]{1,0:T(8,128)(2,1)S(1)} collective-permute-done((bf16[80,512]{1,0:T(8,128)(2,1)S(1)}, bf16[80,512]{1,0:T(8,128)(2,1)S(1)}, u32[]{:S(2)}, u32[]{:S(2)}) %collective-permute-start.7) | collective-permute-done | bytes 81952 | tf_op jit(solution)/shard_map/ppermute | solution.py:249
  26.1 2.6 %collective-permute-done.8.refs_4_ = bf16[80,512]{1,0:T(8,128)(2,1)S(1)} collective-permute-done((bf16[80,512]{1,0:T(8,128)(2,1)S(1)}, bf16[80,512]{1,0:T(8,128)(2,1)S(1)}, u32[]{:S(2)}, u32[]{:S(2)}) %collective-permute-start.8) | collective-permute-done | bytes 81952 | tf_op jit(solution)/shard_map/ppermute | solution.py:249
  28.8 0.0 collective-permute-done.9.refs_5_
  28.8 1.9 %collective-permute-done.10.refs_6_ = bf16[80,512]{1,0:T(8,128)(2,1)S(1)} collective-permute-done((bf16[80,512]{1,0:T(8,128)(2,1)S(1)}, bf16[80,512]{1,0:T(8,128)(2,1)S(1)}, u32[]{:S(2)}, u32[]{:S(2)}) %collective-permute-start.10) | collective-permute-done | bytes 81952 | tf_op jit(solution)/shard_map/ppermute | solution.py:249
  30.6 0.7 %inner_products.1 = (bf16[640,512]{1,0:T(8,128)(2,1)S(1)}, f32[32,4,128]{2,1,0:T(4,128)S(1)}) custom-call(bf16[80,512]{1,0:T(8,128)(2,1)S(1)} %collective-permute-done.4.refs_0_, bf16[80,512]{1,0:T(8,128)(2,1)S(1)} %collective-permute-done.5.refs_1_, bf16[80,512]{1,0:T(8,128)(2,1)S(1)} %collective-permute-done.6.refs_2_, ...), custom_call_target="tpu_custom_call" | custom-call | tf_op jit(solution)/shard_map/inner_products/pallas_call | solution.py:310
  31.4 10.6 %all_to_all.5.shares = f32[32,4,128]{2,1,0:T(4,128)S(1)} all-to-all(f32[32,4,128]{2,1,0:T(4,128)S(1)} %get-tuple-element.32), channel_id=1, replica_groups=mesh['dp'=8,'mp'=4] {'dp','mp'}, dimensions={0} | all-to-all | bytes 131072 | tf_op jit(solution)/shard_map/all_to_all | solution.py:321
  41.9 0.0 copy-done
  41.9 0.0 copy-done.1
  41.9 0.0 copy-done.2
  41.9 2.3 %update.1 = (f32[1,4096]{1,0:T(1,128)}, f32[1,4096]{1,0:T(1,128)}) custom-call(f32[32,4,128]{2,1,0:T(4,128)S(1)} %all_to_all.5.shares, bf16[640,512]{1,0:T(8,128)(2,1)S(1)} %get-tuple-element.33.group, f32[8]{0:T(128)S(1)} %copy-done.2, f32[1,4096]{1,0:T(1,128)S(1)} %copy-done, f32[1,4096]{1,0:T(1,128)S(1)} %copy-done.1), custom_call_target="tpu_custom_call" | custom-call | tf_op jit(solution)/shard_map/update/pallas_call | solution.py:324
  (2 shorter events, 0.0 us)
Async XLA Ops:
  0.6 10.4 %copy-start.3 = (s32[4]{0:T(128)S(1)}, s32[4]{0:T(128)}, u32[]{:S(2)}) copy-start(s32[4]{0:T(128)} %priv_len.1) | copy-start | bytes 52
  3.8 3.1 %collective-permute-start = (f32[16,640]{1,0:T(8,128)S(1)}, f32[16,640]{1,0:T(8,128)S(1)}, u32[]{:S(2)}, u32[]{:S(2)}) collective-permute-start(f32[16,640]{1,0:T(8,128)S(1)} %get-tuple-element.18), channel_id=1, source_target_pairs={{0,1},{1,0},{2,3},{3,2},{4,5},{5,4},{6,7},{7,6},{8,9},{9,8},{10,11... | collective-permute-start | bytes 122888 | tf_op jit(solution)/shard_map/ppermute | solution.py:249
  4.3 4.7 %collective-permute-start.2 = (f32[16,640]{1,0:T(8,128)S(1)}, f32[16,640]{1,0:T(8,128)S(1)}, u32[]{:S(2)}, u32[]{:S(2)}) collective-permute-start(f32[16,640]{1,0:T(8,128)S(1)} %get-tuple-element.19), channel_id=1, source_target_pairs={{0,2},{1,3},{2,0},{3,1},{4,6},{5,7},{6,4},{7,5},{8,10},{9,11},{10,... | collective-permute-start | bytes 122888 | tf_op jit(solution)/shard_map/ppermute | solution.py:249
  6.9 4.1 %collective-permute-start.1 = (f32[16,640]{1,0:T(8,128)S(1)}, f32[16,640]{1,0:T(8,128)S(1)}, u32[]{:S(2)}, u32[]{:S(2)}) collective-permute-start(f32[16,640]{1,0:T(8,128)S(1)} %add.6.rest_0_), channel_id=1, source_target_pairs={{0,2},{1,3},{2,0},{3,1},{4,6},{5,7},{6,4},{7,5},{8,10},{9,11},{10,... | collective-permute-start | bytes 122888 | tf_op jit(solution)/shard_map/ppermute | solution.py:249
  9.1 1.9 %collective-permute-start.3 = (f32[16,640]{1,0:T(8,128)S(1)}, f32[16,640]{1,0:T(8,128)S(1)}, u32[]{:S(2)}, u32[]{:S(2)}) collective-permute-start(f32[16,640]{1,0:T(8,128)S(1)} %add.7.rest_2_), channel_id=1, source_target_pairs={{0,1},{1,0},{2,3},{3,2},{4,5},{5,4},{6,7},{7,6},{8,9},{9,8},{10,11... | collective-permute-start | bytes 122888 | tf_op jit(solution)/shard_map/ppermute | solution.py:249
  11.0 30.9 %copy-start = (f32[1,4096]{1,0:T(1,128)S(1)}, f32[1,4096]{1,0:T(1,128)}, u32[]{:S(2)}) copy-start(f32[1,4096]{1,0:T(1,128)} %down_noise.1) | copy-start | bytes 49156
  11.0 30.9 %copy-start.1 = (f32[1,4096]{1,0:T(1,128)S(1)}, f32[1,4096]{1,0:T(1,128)}, u32[]{:S(2)}) copy-start(f32[1,4096]{1,0:T(1,128)} %up_noise.1) | copy-start | bytes 49156
  11.0 30.9 %copy-start.2 = (f32[8]{0:T(128)S(1)}, f32[8]{0:T(128)}, u32[]{:S(2)}) copy-start(f32[8]{0:T(128)} %noise.1) | copy-start | bytes 100
  12.3 9.5 %collective-permute-start.4 = (bf16[80,512]{1,0:T(8,128)(2,1)S(1)}, bf16[80,512]{1,0:T(8,128)(2,1)S(1)}, u32[]{:S(2)}, u32[]{:S(2)}) collective-permute-start(bf16[80,512]{1,0:T(8,128)(2,1)S(1)} %get-tuple-element.24), channel_id=1, source_target_pairs={{0,24},{4,28},{8,16},{12,20},{16,8},{20,12},{24,0},{28,4},{1,25},{... | collective-permute-start | bytes 245768 | tf_op jit(solution)/shard_map/ppermute | solution.py:249
  16.0 7.4 %collective-permute-start.5 = (bf16[80,512]{1,0:T(8,128)(2,1)S(1)}, bf16[80,512]{1,0:T(8,128)(2,1)S(1)}, u32[]{:S(2)}, u32[]{:S(2)}) collective-permute-start(bf16[80,512]{1,0:T(8,128)(2,1)S(1)} %get-tuple-element.25), channel_id=1, source_target_pairs={{0,8},{4,12},{8,0},{12,4},{16,24},{20,28},{24,16},{28,20},{1,9},{5... | collective-permute-start | bytes 245768 | tf_op jit(solution)/shard_map/ppermute | solution.py:249
  16.0 8.6 %collective-permute-start.6 = (bf16[80,512]{1,0:T(8,128)(2,1)S(1)}, bf16[80,512]{1,0:T(8,128)(2,1)S(1)}, u32[]{:S(2)}, u32[]{:S(2)}) collective-permute-start(bf16[80,512]{1,0:T(8,128)(2,1)S(1)} %get-tuple-element.26), channel_id=1, source_target_pairs={{0,16},{4,20},{8,24},{12,28},{16,0},{20,4},{24,8},{28,12},{1,17},{... | collective-permute-start | bytes 245768 | tf_op jit(solution)/shard_map/ppermute | solution.py:249
  16.8 9.3 %collective-permute-start.7 = (bf16[80,512]{1,0:T(8,128)(2,1)S(1)}, bf16[80,512]{1,0:T(8,128)(2,1)S(1)}, u32[]{:S(2)}, u32[]{:S(2)}) collective-permute-start(bf16[80,512]{1,0:T(8,128)(2,1)S(1)} %get-tuple-element.27), channel_id=1, source_target_pairs={{0,12},{4,8},{8,4},{12,0},{16,28},{20,24},{24,20},{28,16},{1,13},{... | collective-permute-start | bytes 245768 | tf_op jit(solution)/shard_map/ppermute | solution.py:249
  19.0 9.8 %collective-permute-start.8 = (bf16[80,512]{1,0:T(8,128)(2,1)S(1)}, bf16[80,512]{1,0:T(8,128)(2,1)S(1)}, u32[]{:S(2)}, u32[]{:S(2)}) collective-permute-start(bf16[80,512]{1,0:T(8,128)(2,1)S(1)} %get-tuple-element.28), channel_id=1, source_target_pairs={{0,20},{4,16},{8,28},{12,24},{16,4},{20,0},{24,12},{28,8},{1,21},{... | collective-permute-start | bytes 245768 | tf_op jit(solution)/shard_map/ppermute | solution.py:249
  21.9 6.9 %collective-permute-start.9 = (bf16[80,512]{1,0:T(8,128)(2,1)S(1)}, bf16[80,512]{1,0:T(8,128)(2,1)S(1)}, u32[]{:S(2)}, u32[]{:S(2)}) collective-permute-start(bf16[80,512]{1,0:T(8,128)(2,1)S(1)} %get-tuple-element.29), channel_id=1, source_target_pairs={{0,4},{4,0},{8,12},{12,8},{16,20},{20,16},{24,28},{28,24},{1,5},{5... | collective-permute-start | bytes 245768 | tf_op jit(solution)/shard_map/ppermute | solution.py:249
  23.4 7.2 %collective-permute-start.10 = (bf16[80,512]{1,0:T(8,128)(2,1)S(1)}, bf16[80,512]{1,0:T(8,128)(2,1)S(1)}, u32[]{:S(2)}, u32[]{:S(2)}) collective-permute-start(bf16[80,512]{1,0:T(8,128)(2,1)S(1)} %get-tuple-element.30), channel_id=1, source_target_pairs={{0,28},{4,24},{8,20},{12,16},{16,12},{20,8},{24,4},{28,0},{1,29},{... | collective-permute-start | bytes 245768 | tf_op jit(solution)/shard_map/ppermute | solution.py:249
